TPU v7x, 512 devices: a whole 4x4x16 slice. The times are simulated.
512 devices in a mesh: dp: 32 (over y, z_lo, core), inv: 16 (over z_hi, x).
Axes of the slice: x: 4, y: 4, z: 16 (z_hi: 4, z_lo: 4; z = z_hi * 4 + z_lo), core: 2. Of those that a mesh axis runs over, the one named last changes fastest.
Arguments:
- acts: bfloat16 [4096, 6144], P('dp', 'inv'), may hold values from -6 to 6
- grads_out: bfloat16 [4096, 24576], P('inv', 'dp'), may hold values from -0.119628906 to 0.119628906
- scale_exp: int32 [4096], replicated, may hold values from 0 to 3
- shard_tokens: int32 [32], replicated, may hold values from 1 to 128, 3072 in all
Outputs:
- precond: bfloat16 [6144, 24576], P('inv', 'dp')
Inputs may be any that keep to these rules, and one draw needn't show every extreme that they name: `shard_tokens`: largest entry is exactly 128; entries sum to 3072.
All inputs are finite; a program needn't handle non-finite values.
Results may differ from a plain program's by a relative error of at most 0.0015.
Values may be sent and summed in bfloat16 or wider, within the bound.
No kernel may reach another device: no remote copies, remote signals or barrier semaphores. Data moves between devices by JAX's collectives and lax.ppermute only.
A program may use at most 64 MiB of HBM per device.

v0:
```python
import jax
import jax.numpy as jnp
from jax import lax
from jax.sharding import PartitionSpec as P

BLK = 128
ITERS = 8
TOK_DEV = 128


damping = 0.001


def damped(cov):
    order = cov.shape[-1]
    eye = jnp.eye(order, dtype=jnp.float32)
    trace = jnp.trace(cov, axis1=1, axis2=2)
    return cov + damping * (trace / order)[:, None, None] * eye


def newton(matrix):
    order = matrix.shape[-1]
    eye = jnp.eye(order, dtype=jnp.float32)
    trace = jnp.trace(matrix, axis1=1, axis2=2)
    approx = eye[None] / trace[:, None, None]
    for step in range(ITERS):
        inner = jnp.einsum("bij,bjk->bik", matrix, approx, precision=lax.Precision.HIGHEST)
        approx = jnp.einsum(
            "bij,bjk->bik", approx, 2.0 * eye - inner, precision=lax.Precision.HIGHEST
        )
    return approx


def local_cov(rows, order):
    shaped = rows.reshape(rows.shape[0], rows.shape[1] // order, order)
    return jnp.einsum("tbi,tbj->bij", shaped, shaped, preferred_element_type=jnp.float32)


def local(acts, grads_out, scale_exp, shard_tokens):
    dp_count = lax.axis_size("dp")
    inv_index = lax.axis_index("inv")
    tokens = acts.shape[0] * dp_count
    grad_rows = grads_out.shape[0]
    in_units = acts.shape[1]
    out_units = grads_out.shape[1]
    ids = jnp.arange(tokens, dtype=jnp.int32)
    limit = jnp.repeat(shard_tokens, TOK_DEV)
    live = ids % TOK_DEV < limit
    live_half = live.astype(jnp.bfloat16)
    row_weight = jnp.where(live, jnp.exp2(-scale_exp.astype(jnp.float32)), 0.0)
    count = jnp.sum(shard_tokens).astype(jnp.float32)
    mine_weight = lax.dynamic_slice_in_dim(row_weight, inv_index * grad_rows, grad_rows)
    scaled = grads_out * mine_weight.astype(jnp.bfloat16)[:, None]
    scaled_all = lax.all_gather(scaled, "inv", axis=0, tiled=True)
    masked = lax.all_gather(acts, "dp", axis=0, tiled=True) * live_half[:, None]
    grad_sum = lax.dot_general(
        masked, scaled_all, (((0,), (0,)), ((), ())), preferred_element_type=jnp.float32
    )
    grad_sum, a_sum = (grad_sum, local_cov(masked, BLK))
    grad = grad_sum / count
    a_inv = newton(damped(a_sum / count))
    g_total = lax.psum(local_cov(scaled, BLK), "inv")
    g_inv = newton(damped(g_total / count))
    shaped = grad.reshape(in_units // BLK, BLK, out_units // BLK, BLK)
    left = jnp.einsum("bij,bjck->bick", a_inv, shaped, precision=lax.Precision.HIGHEST)
    both = jnp.einsum("bick,ckl->bicl", left, g_inv, precision=lax.Precision.HIGHEST)
    return both.reshape(in_units, out_units).astype(jnp.bfloat16)


def solution(mesh):
    placed = (P("dp", "inv"), P("inv", "dp"), P(), P())
    return jax.shard_map(
        local, mesh=mesh, in_specs=placed, out_specs=P("inv", "dp"), check_vma=False
    )
```

profile of v0, /device:TPU:6, one launch (start us, length us, event | category | flops | bytes accessed | tf_op | source)
XLA Modules:
  0.0 357.3 jit_solution(17129203898789001428)
XLA Ops:
  7.4 1.2 copy.9
  8.6 0.7 fusion.27
  9.3 0.8 fusion.23
  10.1 1.0 fusion.29
  11.2 0.8 copy.11
  12.1 0.5 all-gather.5.cloned.1.call-update
  12.6 0.7 reduce_sum.41
  13.9 302.4 %all-reduce.2.cloned.1.call-done = f32[6,128,128]{2,1,0:T(8,128)} async-done(((f32[6,128,128]{2,1,0:T(8,128)}), f32[6,128,128]{2,1,0:T(8,128)}) %all-reduce.2.cloned.1.call-update) | async-done | bytes 393232 | tf_op jit(solution)/shard_map/psum | solution.py:62
  316.3 1.1 select_reduce_fusion.1
  317.5 1.2 select_reduce_fusion
  318.7 0.6 convolution_subtract_fusion.7
  319.3 0.6 fusion.3
  319.9 0.5 convolution_subtract_fusion.6
  320.4 0.5 fusion.30
  321.0 0.5 convolution_subtract_fusion.5
  321.5 0.5 fusion.31
  322.0 0.5 convolution_subtract_fusion.4
  322.6 0.5 fusion.32
  323.1 0.5 convolution_subtract_fusion.3
  323.6 0.5 fusion.33
  324.2 0.5 convolution_subtract_fusion.2
  324.7 0.5 fusion.34
  325.3 0.5 convolution_subtract_fusion.1
  325.8 0.5 fusion.35
  326.3 0.5 convolution_subtract_fusion
  326.9 1.6 convolution_bitcast_fusion
  328.4 2.1 broadcast_multiply_fusion
  330.5 1.1 select_reduce_fusion.3
  331.8 0.4 convolution_subtract_fusion.15
  332.2 0.4 fusion.10
  332.6 0.4 convolution_subtract_fusion.14
  332.9 0.4 fusion.36
  333.3 0.4 convolution_subtract_fusion.13
  333.7 0.4 fusion.37
  334.0 0.5 convolution_subtract_fusion.12
  334.6 0.4 fusion.38
  334.9 0.4 convolution_subtract_fusion.11
  335.3 0.4 fusion.39
  335.6 0.4 convolution_subtract_fusion.10
  336.3 0.4 convolution_subtract_fusion.9
  336.7 0.4 fusion.41
  337.1 0.4 convolution_subtract_fusion.8
  337.8 6.5 %convolution_divide_fusion = f32[384,768]{1,0:T(8,128)} fusion(bf16[4096,384]{0,1:T(8,128)(2,1)S(1)} %broadcast_multiply_fusion, bf16[4096,768]{0,1:T(8,128)(2,1)} %all-gather.5.cloned.1.call-done, f32[]{:T(128)S(6)} %convert_element_type.44), kind=kOutput, calls=%fused_computation.2 | convolution fusion | flops 2416214016 | bytes 10616836 | tf_op jit(solution)/shard_map/dot_general | solution.py:56
  344.3 1.4 reshape.56
  345.8 1.2 fusion.1
  347.0 1.5 fusion
  348.5 0.4 copy.13
  349.0 0.9 copy.22
  (23 shorter events, 1.1 us)
Async XLA Ops:
  7.4 5.2 %copy-start.3 = (s32[32]{0:T(128)S(1)}, s32[32]{0:T(128)}, u32[]{:S(2)}) copy-start(s32[32]{0:T(128)} %param.7) | copy-start | bytes 388
  7.4 3.9 %copy-start.2 = (bf16[128,384]{1,0:T(8,128)(2,1)S(1)}, bf16[128,384]{1,0:T(8,128)(2,1)}, u32[]{:S(2)}) copy-start(bf16[128,384]{1,0:T(8,128)(2,1)} %param.4) | copy-start | bytes 294916
  7.4 309.0 %all-reduce.2.cloned.1.call-start = ((), (), s32[]{:S(2)}) async-start(), calls=%async_computation | async-start | bytes 786432 | tf_op jit(solution)/shard_map/psum | solution.py:62
  10.1 1.9 copy-start
  11.2 317.3 %all-gather.3.cloned.1.call-start = ((), (), s32[]{:S(2)}) async-start(), calls=%async_computation.1 | async-start | bytes 3244032 | tf_op jit(solution)/shard_map/all_gather | solution.py:55
  12.0 325.8 %all-gather.5.cloned.1.call-start = ((), (), s32[]{:S(2)}) async-start(), calls=%async_computation.2 | async-start | bytes 6684672 | tf_op jit(solution)/shard_map/all_gather | solution.py:54
  344.3 2.7 copy-start.1
Sparse Core Ops, SparseCore 0:
  11.3 305.0 all-reduce.1
Sparse Core Ops, SparseCore 1:
  13.9 77.1 all-gather.2
  94.4 184.0 all-gather.4
where the time goes:
time: 361 us; the launch traced here: 357 us
  waiting for transfers between devices  303 us (84%)
  matrix products  26.8 us (7%)
  between operations  15.8 us (4%)
  other arithmetic  6.89 us (2%)
  local copies, waits for them, and re-layouts  4.73 us (1%)
    psum x1, waiting for transfers between devices, local(): g_total = lax.psum(local_cov(scaled, BLK), 'inv')  302 us
    dot_general x16, matrix products, newton(): jnp.einsum('bij,bjk->bik', approx, 2.0 * eye - inner, precision=lax.Preci...  8.14 us
    dot_general x16, matrix products, newton(): jnp.einsum('bij,bjk->bik', matrix, approx, precision=lax.Precision.HIGHEST)  7.3 us
  transfers between devices with their start and end apart: 3, of which 1 were waited for; matrix products, arithmetic and copies ran while one was open for 6% of the time, Pallas kernels for 0%

commit v1 on v0

v1 whole, which is shorter than its diff:
```python
import functools

import jax
import jax.numpy as jnp
from jax import lax
from jax.experimental import pallas as pl
from jax.experimental.pallas import tpu as pltpu
from jax.sharding import PartitionSpec as P

BLK = 128
TOK_DEV = 128
DAMPING = 0.001
VMEM_LIMIT = 40 * 1024 * 1024


def shift_x(step):
    return [(i, i // 4 * 4 + (i + step) % 4) for i in range(16)]


def shift_z(step):
    return [(i, (i // 4 + step) % 4 * 4 + i % 4) for i in range(16)]


def flip_dp(mask):
    return [(j, j ^ mask) for j in range(32)]


def hop(value, pairs):
    return lax.ppermute(value, "inv", pairs)


def swap(value, mask):
    return lax.ppermute(value, "dp", flip_dp(mask))


def both_ways(value, shift):
    return hop(value, shift(1)), hop(value, shift(-1))


def far_halves(lower, upper, shift):
    half = lower.shape[0] // 2
    return hop(lower[:half], shift(1)), hop(upper[half:], shift(-1))


def eye(order):
    rows = lax.broadcasted_iota(jnp.int32, (order, order), 0)
    cols = lax.broadcasted_iota(jnp.int32, (order, order), 1)
    return rows == cols


def dot32(a, b):
    return jnp.dot(
        a, b, precision=lax.Precision.HIGHEST, preferred_element_type=jnp.float32
    )


def pair_diag(a, b):
    zero = jnp.zeros_like(a)
    return jnp.concatenate(
        [jnp.concatenate([a, zero], 1), jnp.concatenate([zero, b], 1)], 0
    )


def newton(covs):
    unit = eye(BLK)
    ident = unit.astype(jnp.float32)
    errors, approxes = [], []
    for cov in covs:
        trace = jnp.sum(jnp.where(unit, cov, 0.0))
        damped = cov + (DAMPING * (trace / BLK)) * ident
        total = jnp.sum(jnp.where(unit, damped, 0.0))
        error = ident - damped / total
        errors.append(error)
        approxes.append((ident + error) / total)
    if len(covs) % 2:
        errors.append(errors[-1])
        approxes.append(approxes[-1])
    pairs = len(errors) // 2
    err = [jnp.concatenate(errors[2 * p : 2 * p + 2], 1) for p in range(pairs)]
    app = [jnp.concatenate(approxes[2 * p : 2 * p + 2], 1) for p in range(pairs)]

    def spread(wide):
        return pair_diag(wide[:, :BLK], wide[:, BLK:])

    err = [dot32(e, spread(e)) for e in err]
    for step in range(6):
        both = [
            dot32(jnp.concatenate([x, e], 0), spread(e))
            for x, e in zip(app, err, strict=True)
        ]
        app = [x + b[:BLK] for x, b in zip(app, both, strict=True)]
        err = [b[BLK:] for b in both]
    app = [x + dot32(x, spread(e)) for x, e in zip(app, err, strict=True)]
    return [
        app[n // 2][:, n % 2 * BLK : (n % 2 + 1) * BLK] for n in range(len(covs))
    ]


def acts_kernel(where_ref, count_ref, *refs):
    parts, (acts_ref, inv_ref) = refs[:4], refs[4:]
    mine = where_ref[0]
    blocks = acts_ref.shape[2] // BLK
    covs = [jnp.zeros((BLK, BLK), jnp.float32) for _ in range(blocks)]
    for n, part in enumerate(parts):
        for k in range(8):
            zl = (k & 1) ^ (k & 2)
            y = (k >> 2 & 1) ^ (3 if n % 2 else 0)
            mask = y * 8 + zl * 2 + n // 2
            acts_ref[mine ^ mask] = part[k]
        rows = part[...].reshape(8 * TOK_DEV, blocks * BLK)
        flipped = rows.T
        for b in range(blocks):
            cols = slice(b * BLK, (b + 1) * BLK)
            covs[b] += jnp.dot(
                flipped[cols], rows[:, cols], preferred_element_type=jnp.float32
            )
    count = count_ref[0]
    for b, inverse in enumerate(newton([c / count for c in covs])):
        inv_ref[b] = inverse


def add_rows(where_ref, acts_ref, piece, dz, dx, half, sums, first):
    zh, x = where_ref[1], where_ref[2]
    token = ((zh + dz) & 3) * 8 + ((x + dx) & 3) * 2
    if half is None:
        rows = acts_ref[pl.ds(token, 2)].reshape(2 * TOK_DEV, acts_ref.shape[2])
    else:
        rows = acts_ref[token + half]
    wide = rows.shape[1]
    flipped = piece.T
    main = jnp.dot(flipped, rows, preferred_element_type=jnp.float32)
    cov = [
        jnp.dot(
            flipped[f * BLK : (f + 1) * BLK],
            piece[:, f * BLK : (f + 1) * BLK],
            preferred_element_type=jnp.float32,
        )
        for f in range(piece.shape[1] // BLK)
    ]
    cov = jnp.concatenate(cov, 0)
    if first:
        sums[:, :wide] = main
        sums[:, wide:] = cov
    else:
        sums[:, :wide] += main
        sums[:, wide:] += cov


def add_group(where_ref, acts_ref, group, kind, sums, first):
    own, low, high, far_low, far_high = group
    step = 2 * TOK_DEV
    for ref, dx in ((own, 0), (low, -1), (high, 1)):
        if kind == 1:
            for n, dz in ((0, -1), (1, 1)):
                piece = ref[n * step : (n + 1) * step, :]
                add_rows(where_ref, acts_ref, piece, dz, dx, None, sums, first)
                first = False
        else:
            add_rows(where_ref, acts_ref, ref[...], kind, dx, None, sums, first)
            first = False
    for ref, n in ((far_low, 0), (far_high, 1)):
        if kind == 1:
            dz = (-1, 1)[n]
            add_rows(where_ref, acts_ref, ref[...], dz, 2, None, sums, False)
        else:
            add_rows(where_ref, acts_ref, ref[...], kind, 2, n, sums, False)


def first_kernel(kind, where_ref, acts_ref, *refs):
    add_group(where_ref, acts_ref, refs[:5], kind, refs[5], True)


def more_kernel(kind, where_ref, acts_ref, *refs):
    sums = refs[6]
    sums[...] = refs[5][...]
    add_group(where_ref, acts_ref, refs[:5], kind, sums, False)


def last_kernel(kind, where_ref, count_ref, acts_ref, inv_ref, *refs):
    out_ref, sums = refs[6], refs[7]
    sums[...] = refs[5][...]
    add_group(where_ref, acts_ref, refs[:5], kind, sums, False)
    wide = acts_ref.shape[2]
    count = count_ref[0]
    outs = sums.shape[0]
    blocks = outs // BLK
    inverse = newton(
        [sums[f * BLK : (f + 1) * BLK, wide:] / count for f in range(blocks)]
    )
    lefts = []
    for b in range(wide // BLK):
        grad = sums[:, b * BLK : (b + 1) * BLK] / count
        lefts.append(dot32(grad, inv_ref[b].T))
    for f in range(0, blocks, 2):
        right = pair_diag(inverse[f], inverse[f + 1])
        for b in range(wide // BLK):
            left = jnp.concatenate(
                [lefts[b][(f + n) * BLK : (f + n + 1) * BLK].T for n in range(2)], 1
            )
            out_ref[b * BLK : (b + 1) * BLK, f * BLK : (f + 2) * BLK] = dot32(
                left, right
            ).astype(jnp.bfloat16)


def call(kernel, smem, vmem, shapes, scratch=()):
    return pl.pallas_call(
        kernel,
        out_shape=shapes,
        in_specs=[pl.BlockSpec(memory_space=pltpu.SMEM)] * len(smem)
        + [pl.BlockSpec(memory_space=pltpu.VMEM)] * len(vmem),
        out_specs=jax.tree.map(
            lambda _: pl.BlockSpec(memory_space=pltpu.VMEM), shapes
        ),
        scratch_shapes=list(scratch),
        compiler_params=pltpu.CompilerParams(vmem_limit_bytes=VMEM_LIMIT),
    )(*smem, *vmem)


def local(acts, grads_out, scale_exp, shard_tokens):
    dp_index = lax.axis_index("dp")
    inv_index = lax.axis_index("inv")
    rows = grads_out.shape[0]
    wide = acts.shape[1]
    outs = grads_out.shape[1]
    where = jnp.stack([dp_index, inv_index // 4, inv_index % 4]).astype(jnp.int32)
    count = jnp.sum(shard_tokens).astype(jnp.float32)[None]

    exps = lax.dynamic_slice_in_dim(scale_exp, inv_index * rows, rows)
    limit = lax.dynamic_slice_in_dim(shard_tokens, inv_index * 2, 2)
    live = jnp.arange(rows, dtype=jnp.int32) % TOK_DEV < jnp.repeat(limit, TOK_DEV)
    weight = jnp.where(live, jnp.exp2(-exps.astype(jnp.float32)), 0.0)
    scaled = grads_out * weight.astype(jnp.bfloat16)[:, None]
    mine = lax.dynamic_slice_in_dim(shard_tokens, dp_index, 1)
    masked = acts * (jnp.arange(TOK_DEV, dtype=jnp.int32) < mine).astype(
        jnp.bfloat16
    )[:, None]

    z_low, z_high = both_ways(scaled, shift_z)
    own_low, own_high = both_ways(scaled, shift_x)
    a = masked[None]
    a = jnp.concatenate([a, swap(a, 2)], 0)
    a = jnp.concatenate([a, swap(a, 4)], 0)
    own_far = far_halves(own_low, own_high, shift_x)
    a = jnp.concatenate([a, swap(a, 8)], 0)
    a_far = swap(a, 24)
    a_core = swap(a, 1)
    a_far_core = swap(a_far, 1)

    sums_shape = jax.ShapeDtypeStruct((outs, wide + BLK), jnp.float32)
    acts_all, a_inv = call(
        acts_kernel,
        (where, count),
        (a, a_far, a_core, a_far_core),
        (
            jax.ShapeDtypeStruct((32, TOK_DEV, wide), jnp.bfloat16),
            jax.ShapeDtypeStruct((wide // BLK, BLK, BLK), jnp.float32),
        ),
    )
    z_far = far_halves(z_low, z_high, shift_z)
    near = jnp.concatenate([z_low, z_high], 0)
    near_low, near_high = both_ways(near, shift_x)
    sums = call(
        functools.partial(first_kernel, 0),
        (where,),
        (acts_all, scaled, own_low, own_high, *own_far),
        sums_shape,
    )
    near_far = far_halves(near_low, near_high, shift_x)
    far = jnp.concatenate(z_far, 0)
    far_low, far_high = both_ways(far, shift_x)
    sums = call(
        functools.partial(more_kernel, 1),
        (where,),
        (acts_all, near, near_low, near_high, *near_far, sums),
        sums_shape,
    )
    far_far = far_halves(far_low, far_high, shift_x)
    return call(
        functools.partial(last_kernel, 2),
        (where, count),
        (acts_all, a_inv, far, far_low, far_high, *far_far, sums),
        jax.ShapeDtypeStruct((wide, outs), jnp.bfloat16),
        scratch=(pltpu.VMEM((outs, wide + BLK), jnp.float32),),
    )


def solution(mesh):
    placed = (P("dp", "inv"), P("inv", "dp"), P(), P())
    return jax.shard_map(
        local, mesh=mesh, in_specs=placed, out_specs=P("inv", "dp"), check_vma=False
    )
```

time: 361 us -> 181 us (0.50)
  the two profiles are of different devices: /device:TPU:6 before, /device:TPU:32 now
where the time goes in v1:
time: 181 us; the launch traced here: 180 us
  starting transfers between devices  82 us (45%)
  waiting for transfers between devices  58.4 us (32%)
  Pallas kernels  23.7 us (13%)
  local copies, waits for them, and re-layouts  11 us (6%)
  other arithmetic  3.37 us (2%)
    ppermute x16, starting transfers between devices, hop(): return lax.ppermute(value, 'inv', pairs)  60.8 us
    ppermute x16, waiting for transfers between devices, hop(): return lax.ppermute(value, 'inv', pairs)  49.6 us
    pallas_call x4, Pallas kernels, call(): pl.pallas_call(kernel, out_shape=shapes, in_specs=[pl.BlockSpec(memory_sp...  23.7 us
    ppermute x6, starting transfers between devices, swap(): return lax.ppermute(value, 'dp', flip_dp(mask))  21.2 us
    ppermute x6, waiting for transfers between devices, swap(): return lax.ppermute(value, 'dp', flip_dp(mask))  8.85 us
    unnamed x42, local copies, waits for them, and re-layouts  5.27 us
    slice x8, local copies, waits for them, and re-layouts, far_halves(): return (hop(lower[:half], shift(1)), hop(upper[half:], shift(-1)))  3.68 us
  transfers between devices with their start and end apart: 22, of which 7 were waited for; matrix products, arithmetic and copies ran while one was open for 3% of the time, Pallas kernels for 7%

profile of v1, /device:TPU:32, one launch (start us, length us, event | category | flops | bytes accessed | tf_op | source)
XLA Modules:
  0.0 179.6 jit_solution(15553054307550371630)
XLA Ops:
  0.0 1.3 dynamic_slice.9
  1.3 0.6 compare_convert_fusion
  1.9 1.0 multiply_bitcast_fusion
  2.9 7.4 %collective-permute-start = (bf16[1,128,384]{2,1,0:T(8,128)(2,1)S(1)}, bf16[1,128,384]{2,1,0:T(8,128)(2,1)S(1)}, u32[]{:S(2)}, u32[]{:S(2)}) collective-permute-start(bf16[1,128,384]{2,1,0:T(8,128)(2,1)S(1)} %multiply_bitcast_fusion), channel_id=1, source_target_pairs={{0,32},{16,48},{32,0},{48,16},{64,96},{80,112},{96,64},{112,80},{1... | collective-permute-start | bytes 294920 | tf_op jit(solution)/shard_map/ppermute | solution.py:33
  10.3 2.6 %collective-permute-done = bf16[1,128,384]{2,1,0:T(8,128)(2,1)S(1)} collective-permute-done((bf16[1,128,384]{2,1,0:T(8,128)(2,1)S(1)}, bf16[1,128,384]{2,1,0:T(8,128)(2,1)S(1)}, u32[]{:S(2)}, u32[]{:S(2)}) %collective-permute-start) | collective-permute-done | bytes 98336 | tf_op jit(solution)/shard_map/ppermute | solution.py:33
  12.9 1.9 %collective-permute-start.1 = (bf16[2,128,384]{2,1,0:T(8,128)(2,1)S(1)}, bf16[2,128,384]{2,1,0:T(8,128)(2,1)S(1)}, u32[]{:S(2)}, u32[]{:S(2)}) collective-permute-start(bf16[2,128,384]{2,1,0:T(8,128)(2,1)S(1)} %pad_maximum_fusion.2), channel_id=1, source_target_pairs={{0,64},{16,80},{32,96},{48,112},{64,0},{80,16},{96,32},{112,48},{1... | collective-permute-start | bytes 589832 | tf_op jit(solution)/shard_map/ppermute | solution.py:33
  14.9 0.7 dynamic_slice.10
  15.6 6.3 %collective-permute-done.1 = bf16[2,128,384]{2,1,0:T(8,128)(2,1)S(1)} collective-permute-done((bf16[2,128,384]{2,1,0:T(8,128)(2,1)S(1)}, bf16[2,128,384]{2,1,0:T(8,128)(2,1)S(1)}, u32[]{:S(2)}, u32[]{:S(2)}) %collective-permute-start.1) | collective-permute-done | bytes 196640 | tf_op jit(solution)/shard_map/ppermute | solution.py:33
  21.9 3.5 %collective-permute-start.2 = (bf16[4,128,384]{2,1,0:T(8,128)(2,1)S(1)}, bf16[4,128,384]{2,1,0:T(8,128)(2,1)S(1)}, u32[]{:S(2)}, u32[]{:S(2)}) collective-permute-start(bf16[4,128,384]{2,1,0:T(8,128)(2,1)S(1)} %pad_maximum_fusion.1), channel_id=1, source_target_pairs={{0,128},{16,144},{32,160},{48,176},{64,192},{80,208},{96,224},{112... | collective-permute-start | bytes 1179656 | tf_op jit(solution)/shard_map/ppermute | solution.py:33
  25.4 0.8 fusion
  26.3 9.1 %collective-permute-start.6 = (bf16[256,768]{1,0:T(8,128)(2,1)S(1)}, bf16[256,768]{1,0:T(8,128)(2,1)S(1)}, u32[]{:S(2)}, u32[]{:S(2)}) collective-permute-start(bf16[256,768]{1,0:T(8,128)(2,1)S(1)} %broadcast_multiply_fusion.refs_0_), channel_id=1, source_target_pairs={{0,4},{1,5},{2,6},{3,7},{4,8},{5,9},{6,10},{7,11},{8,12},{9,13},{1... | collective-permute-start | bytes 1179656 | tf_op jit(solution)/shard_map/ppermute | solution.py:29
  35.4 2.9 %collective-permute-start.8 = (bf16[256,768]{1,0:T(8,128)(2,1)S(1)}, bf16[256,768]{1,0:T(8,128)(2,1)S(1)}, u32[]{:S(2)}, u32[]{:S(2)}) collective-permute-start(bf16[256,768]{1,0:T(8,128)(2,1)S(1)} %broadcast_multiply_fusion.refs_0_), channel_id=1, source_target_pairs={{0,12},{1,13},{2,14},{3,15},{4,0},{5,1},{6,2},{7,3},{8,4},{9,5},{1... | collective-permute-start | bytes 1179656 | tf_op jit(solution)/shard_map/ppermute | solution.py:29
  38.4 4.1 %collective-permute-start.3 = (bf16[8,128,384]{2,1,0:T(8,128)(2,1)S(1)}, bf16[8,128,384]{2,1,0:T(8,128)(2,1)S(1)}, u32[]{:S(2)}, u32[]{:S(2)}) collective-permute-start(bf16[8,128,384]{2,1,0:T(8,128)(2,1)S(1)} %pad_maximum_fusion.refs_0_), channel_id=1, source_target_pairs={{0,384},{16,400},{32,416},{48,432},{64,448},{80,464},{96,480},{112... | collective-permute-start | bytes 2359304 | tf_op jit(solution)/shard_map/ppermute | solution.py:33
  42.5 3.4 %collective-permute-start.18 = (bf16[256,768]{1,0:T(8,128)(2,1)S(1)}, bf16[256,768]{1,0:T(8,128)(2,1)S(1)}, u32[]{:S(2)}, u32[]{:S(2)}) collective-permute-start(bf16[256,768]{1,0:T(8,128)(2,1)S(1)} %broadcast_multiply_fusion.refs_0_), channel_id=1, source_target_pairs={{0,1},{1,2},{2,3},{3,0},{4,5},{5,6},{6,7},{7,4},{8,9},{9,10},{10,1... | collective-permute-start | bytes 1179656 | tf_op jit(solution)/shard_map/ppermute | solution.py:29
  45.9 7.5 %collective-permute-done.6 = bf16[256,768]{1,0:T(8,128)(2,1)S(1)} collective-permute-done((bf16[256,768]{1,0:T(8,128)(2,1)S(1)}, bf16[256,768]{1,0:T(8,128)(2,1)S(1)}, u32[]{:S(2)}, u32[]{:S(2)}) %collective-permute-start.6) | collective-permute-done | bytes 393248 | tf_op jit(solution)/shard_map/ppermute | solution.py:29
  53.4 8.5 %collective-permute-done.8 = bf16[256,768]{1,0:T(8,128)(2,1)S(1)} collective-permute-done((bf16[256,768]{1,0:T(8,128)(2,1)S(1)}, bf16[256,768]{1,0:T(8,128)(2,1)S(1)}, u32[]{:S(2)}, u32[]{:S(2)}) %collective-permute-start.8) | collective-permute-done | bytes 393248 | tf_op jit(solution)/shard_map/ppermute | solution.py:29
  62.0 3.4 %collective-permute-start.14 = (bf16[512,768]{1,0:T(8,128)(2,1)S(1)}, bf16[512,768]{1,0:T(8,128)(2,1)S(1)}, u32[]{:S(2)}, u32[]{:S(2)}) collective-permute-start(bf16[512,768]{1,0:T(8,128)(2,1)S(1)} %constant_dynamic-update-slice_fusion.2.refs_0_), channel_id=1, source_target_pairs={{0,1},{1,2},{2,3},{3,0},{4,5},{5,6},{6,7},{7,4},{8,9},{9,10},{10,1... | collective-permute-start | bytes 2359304 | tf_op jit(solution)/shard_map/ppermute | solution.py:29
  65.4 3.7 %collective-permute-start.15 = (bf16[512,768]{1,0:T(8,128)(2,1)S(1)}, bf16[512,768]{1,0:T(8,128)(2,1)S(1)}, u32[]{:S(2)}, u32[]{:S(2)}) collective-permute-start(bf16[512,768]{1,0:T(8,128)(2,1)S(1)} %constant_dynamic-update-slice_fusion.2.refs_0_), channel_id=1, source_target_pairs={{0,3},{1,0},{2,1},{3,2},{4,7},{5,4},{6,5},{7,6},{8,11},{9,8},{10,9... | collective-permute-start | bytes 2359304 | tf_op jit(solution)/shard_map/ppermute | solution.py:29
  69.0 7.2 %collective-permute-start.7 = (bf16[128,768]{1,0:T(8,128)(2,1)S(1)}, bf16[128,768]{1,0:T(8,128)(2,1)S(1)}, u32[]{:S(2)}, u32[]{:S(2)}) collective-permute-start(bf16[128,768]{1,0:T(8,128)(2,1)S(1)} %slice.32), channel_id=1, source_target_pairs={{0,4},{1,5},{2,6},{3,7},{4,8},{5,9},{6,10},{7,11},{8,12},{9,13},{1... | collective-permute-start | bytes 589832 | tf_op jit(solution)/shard_map/ppermute | solution.py:29
  76.3 2.6 %collective-permute-start.9 = (bf16[128,768]{1,0:T(8,128)(2,1)S(1)}, bf16[128,768]{1,0:T(8,128)(2,1)S(1)}, u32[]{:S(2)}, u32[]{:S(2)}) collective-permute-start(bf16[128,768]{1,0:T(8,128)(2,1)S(1)} %slice.33), channel_id=1, source_target_pairs={{0,12},{1,13},{2,14},{3,15},{4,0},{5,1},{6,2},{7,3},{8,4},{9,5},{1... | collective-permute-start | bytes 589832 | tf_op jit(solution)/shard_map/ppermute | solution.py:29
  78.9 4.3 %collective-permute-done.7 = bf16[128,768]{1,0:T(8,128)(2,1)S(1)} collective-permute-done((bf16[128,768]{1,0:T(8,128)(2,1)S(1)}, bf16[128,768]{1,0:T(8,128)(2,1)S(1)}, u32[]{:S(2)}, u32[]{:S(2)}) %collective-permute-start.7) | collective-permute-done | bytes 196640 | tf_op jit(solution)/shard_map/ppermute | solution.py:29
  83.1 3.4 %collective-permute-start.19 = (bf16[256,768]{1,0:T(8,128)(2,1)S(1)}, bf16[256,768]{1,0:T(8,128)(2,1)S(1)}, u32[]{:S(2)}, u32[]{:S(2)}) collective-permute-start(bf16[256,768]{1,0:T(8,128)(2,1)S(1)} %broadcast_multiply_fusion.refs_0_), channel_id=1, source_target_pairs={{0,3},{1,0},{2,1},{3,2},{4,7},{5,4},{6,5},{7,6},{8,11},{9,8},{10,9... | collective-permute-start | bytes 1179656 | tf_op jit(solution)/shard_map/ppermute | solution.py:29
  86.6 21.6 %collective-permute-done.9 = bf16[128,768]{1,0:T(8,128)(2,1)S(1)} collective-permute-done((bf16[128,768]{1,0:T(8,128)(2,1)S(1)}, bf16[128,768]{1,0:T(8,128)(2,1)S(1)}, u32[]{:S(2)}, u32[]{:S(2)}) %collective-permute-start.9) | collective-permute-done | bytes 196640 | tf_op jit(solution)/shard_map/ppermute | solution.py:29
  108.1 1.9 %collective-permute-start.4 = (bf16[8,128,384]{2,1,0:T(8,128)(2,1)S(1)}, bf16[8,128,384]{2,1,0:T(8,128)(2,1)S(1)}, u32[]{:S(2)}, u32[]{:S(2)}) collective-permute-start(bf16[8,128,384]{2,1,0:T(8,128)(2,1)S(1)} %pad_maximum_fusion.refs_0_), channel_id=1, source_target_pairs={{0,16},{16,0},{32,48},{48,32},{64,80},{80,64},{96,112},{112,96},{1... | collective-permute-start | bytes 2359304 | tf_op jit(solution)/shard_map/ppermute | solution.py:33
  110.1 2.4 %collective-permute-start.5 = (bf16[8,128,384]{2,1,0:T(8,128)(2,1)S(1)}, bf16[8,128,384]{2,1,0:T(8,128)(2,1)S(1)}, u32[]{:S(2)}, u32[]{:S(2)}) collective-permute-start(bf16[8,128,384]{2,1,0:T(8,128)(2,1)S(1)} %collective-permute-done.3.refs_1_), channel_id=1, source_target_pairs={{0,16},{16,0},{32,48},{48,32},{64,80},{80,64},{96,112},{112,96},{1... | collective-permute-start | bytes 2359304 | tf_op jit(solution)/shard_map/ppermute | solution.py:33
  112.6 2.3 %collective-permute-start.10 = (bf16[256,768]{1,0:T(8,128)(2,1)S(1)}, bf16[256,768]{1,0:T(8,128)(2,1)S(1)}, u32[]{:S(2)}, u32[]{:S(2)}) collective-permute-start(bf16[256,768]{1,0:T(8,128)(2,1)S(1)} %constant_dynamic-update-slice_fusion.refs_0_), channel_id=1, source_target_pairs={{0,1},{1,2},{2,3},{3,0},{4,5},{5,6},{6,7},{7,4},{8,9},{9,10},{10,1... | collective-permute-start | bytes 1179656 | tf_op jit(solution)/shard_map/ppermute | solution.py:29
  114.9 4.7 %collective-permute-start.11 = (bf16[256,768]{1,0:T(8,128)(2,1)S(1)}, bf16[256,768]{1,0:T(8,128)(2,1)S(1)}, u32[]{:S(2)}, u32[]{:S(2)}) collective-permute-start(bf16[256,768]{1,0:T(8,128)(2,1)S(1)} %constant_dynamic-update-slice_fusion.refs_0_), channel_id=1, source_target_pairs={{0,3},{1,0},{2,1},{3,2},{4,7},{5,4},{6,5},{7,6},{8,11},{9,8},{10,9... | collective-permute-start | bytes 1179656 | tf_op jit(solution)/shard_map/ppermute | solution.py:29
  119.7 1.9 %collective-permute-start.20 = (bf16[128,768]{1,0:T(8,128)(2,1)S(1)}, bf16[128,768]{1,0:T(8,128)(2,1)S(1)}, u32[]{:S(2)}, u32[]{:S(2)}) collective-permute-start(bf16[128,768]{1,0:T(8,128)(2,1)S(1)} %slice.38), channel_id=1, source_target_pairs={{0,1},{1,2},{2,3},{3,0},{4,5},{5,6},{6,7},{7,4},{8,9},{9,10},{10,1... | collective-permute-start | bytes 589832 | tf_op jit(solution)/shard_map/ppermute | solution.py:29
  121.6 0.8 slice.36
  122.4 0.8 slice.37
  123.2 7.7 %collective-permute-done.20.refs_3_ = bf16[128,768]{1,0:T(8,128)(2,1)S(1)} collective-permute-done((bf16[128,768]{1,0:T(8,128)(2,1)S(1)}, bf16[128,768]{1,0:T(8,128)(2,1)S(1)}, u32[]{:S(2)}, u32[]{:S(2)}) %collective-permute-start.20) | collective-permute-done | bytes 196640 | tf_op jit(solution)/shard_map/ppermute | solution.py:29
  130.9 1.9 %collective-permute-start.16 = (bf16[256,768]{1,0:T(8,128)(2,1)}, bf16[256,768]{1,0:T(8,128)(2,1)}, u32[]{:S(2)}, u32[]{:S(2)}) collective-permute-start(bf16[256,768]{1,0:T(8,128)(2,1)} %slice.36), channel_id=1, source_target_pairs={{0,1},{1,2},{2,3},{3,0},{4,5},{5,6},{6,7},{7,4},{8,9},{9,10},{10,1... | collective-permute-start | bytes 1179656 | tf_op jit(solution)/shard_map/ppermute | solution.py:29
  132.9 5.1 %collective-permute-start.17 = (bf16[256,768]{1,0:T(8,128)(2,1)}, bf16[256,768]{1,0:T(8,128)(2,1)}, u32[]{:S(2)}, u32[]{:S(2)}) collective-permute-start(bf16[256,768]{1,0:T(8,128)(2,1)} %slice.37), channel_id=1, source_target_pairs={{0,3},{1,0},{2,1},{3,2},{4,7},{5,4},{6,5},{7,6},{8,11},{9,8},{10,9... | collective-permute-start | bytes 1179656 | tf_op jit(solution)/shard_map/ppermute | solution.py:29
  138.0 0.7 slice.39
  138.7 1.9 %collective-permute-start.21 = (bf16[128,768]{1,0:T(8,128)(2,1)}, bf16[128,768]{1,0:T(8,128)(2,1)}, u32[]{:S(2)}, u32[]{:S(2)}) collective-permute-start(bf16[128,768]{1,0:T(8,128)(2,1)} %slice.39), channel_id=1, source_target_pairs={{0,3},{1,0},{2,1},{3,2},{4,7},{5,4},{6,5},{7,6},{8,11},{9,8},{10,9... | collective-permute-start | bytes 589832 | tf_op jit(solution)/shard_map/ppermute | solution.py:29
  140.7 0.7 slice.34
  141.3 0.7 slice.35
  142.1 0.9 copy-done.12
  143.0 3.9 %collective-permute-start.12 = (bf16[128,768]{1,0:T(8,128)(2,1)}, bf16[128,768]{1,0:T(8,128)(2,1)}, u32[]{:S(2)}, u32[]{:S(2)}) collective-permute-start(bf16[128,768]{1,0:T(8,128)(2,1)} %slice.34), channel_id=1, source_target_pairs={{0,1},{1,2},{2,3},{3,0},{4,5},{5,6},{6,7},{7,4},{8,9},{9,10},{10,1... | collective-permute-start | bytes 589832 | tf_op jit(solution)/shard_map/ppermute | solution.py:29
  146.9 0.9 copy-done.14
  147.8 3.3 %collective-permute-start.13 = (bf16[128,768]{1,0:T(8,128)(2,1)}, bf16[128,768]{1,0:T(8,128)(2,1)}, u32[]{:S(2)}, u32[]{:S(2)}) collective-permute-start(bf16[128,768]{1,0:T(8,128)(2,1)} %slice.35), channel_id=1, source_target_pairs={{0,3},{1,0},{2,1},{3,2},{4,7},{5,4},{6,5},{7,6},{8,11},{9,8},{10,9... | collective-permute-start | bytes 589832 | tf_op jit(solution)/shard_map/ppermute | solution.py:29
  152.4 1.1 copy-done.11
  153.5 1.1 copy-done.13
  154.6 1.1 copy-done.15
  155.8 6.2 %shard_map.46 = (bf16[32,128,384]{2,1,0:T(8,128)(2,1)S(1)}, f32[3,128,128]{2,1,0:T(8,128)S(1)}) custom-call(s32[3]{0:T(128)S(1)} %pad_add_fusion.where_ref, f32[1]{0:T(128)} %bitcast.3.count_ref, bf16[8,128,384]{2,1,0:T(8,128)(2,1)S(1)} %pad_maximum_fusion.refs_0_, bf16[8,128,384]{2,1,0:T(8,128)(2,1)S(1)} %copy-done.11, bf16[8,128,384]{2,1,0:T(8,128)(2,1)S(1)} %copy-done.13, ...), custom_call_target="tpu_custom_call" | custom-call | tf_op jit(solution)/shard_map/pallas_call | solution.py:206
  162.1 2.5 %shard_map.47.refs_5_ = f32[768,512]{1,0:T(8,128)S(1)} custom-call(s32[3]{0:T(128)S(1)} %pad_add_fusion.where_ref, bf16[32,128,384]{2,1,0:T(8,128)(2,1)S(1)} %get-tuple-element.7.acts_ref, bf16[256,768]{1,0:T(8,128)(2,1)S(1)} %broadcast_multiply_fusion.refs_0_, bf16[256,768]{1,0:T(8,128)(2,1)S(1)} %copy-done.1, bf16[256,768]{1,0:T(8,128)(2,1)S(1)} %copy-done.3, ...), custom_call_target="tpu_custom_call" | custom-call | tf_op jit(solution)/shard_map/pallas_call | solution.py:206
  164.6 3.9 %shard_map.48.refs_5_ = f32[768,512]{1,0:T(8,128)S(1)} custom-call(s32[3]{0:T(128)S(1)} %pad_add_fusion.where_ref, bf16[32,128,384]{2,1,0:T(8,128)(2,1)S(1)} %get-tuple-element.7.acts_ref, bf16[512,768]{1,0:T(8,128)(2,1)S(1)} %constant_dynamic-update-slice_fusion.2.refs_0_, bf16[512,768]{1,0:T(8,128)(2,1)S(1)} %collective-permute-done.14.refs_1_, ...), custom_call_target="tpu_custom_call" | custom-call | tf_op jit(solution)/shard_map/pallas_call | solution.py:206
  168.6 11.1 %shard_map.49 = bf16[384,768]{1,0:T(8,128)(2,1)} custom-call(s32[3]{0:T(128)S(1)} %pad_add_fusion.where_ref, f32[1]{0:T(128)} %bitcast.3.count_ref, bf16[32,128,384]{2,1,0:T(8,128)(2,1)S(1)} %get-tuple-element.7.acts_ref, f32[3,128,128]{2,1,0:T(8,128)S(1)} %get-tuple-element.8.inv_ref, bf16[256,768]{1,0:T(8,128)(2,1)S(1)} %copy-done.9, ...), custom_call_target="tpu_custom_call" | custom-call | tf_op jit(solution)/shard_map/pallas_call | solution.py:206
  (63 shorter events, 1.2 us)
Async XLA Ops:
  0.0 26.2 %copy-start.18 = (bf16[256,768]{1,0:T(8,128)(2,1)S(1)}, bf16[256,768]{1,0:T(8,128)(2,1)}, u32[]{:S(2)}) copy-start(bf16[256,768]{1,0:T(8,128)(2,1)} %param.5) | copy-start | bytes 1179652
  2.9 10.0 %collective-permute-start = (bf16[1,128,384]{2,1,0:T(8,128)(2,1)S(1)}, bf16[1,128,384]{2,1,0:T(8,128)(2,1)S(1)}, u32[]{:S(2)}, u32[]{:S(2)}) collective-permute-start(bf16[1,128,384]{2,1,0:T(8,128)(2,1)S(1)} %multiply_bitcast_fusion), channel_id=1, source_target_pairs={{0,32},{16,48},{32,0},{48,16},{64,96},{80,112},{96,64},{112,80},{1... | collective-permute-start | bytes 294920 | tf_op jit(solution)/shard_map/ppermute | solution.py:33
  12.9 8.9 %collective-permute-start.1 = (bf16[2,128,384]{2,1,0:T(8,128)(2,1)S(1)}, bf16[2,128,384]{2,1,0:T(8,128)(2,1)S(1)}, u32[]{:S(2)}, u32[]{:S(2)}) collective-permute-start(bf16[2,128,384]{2,1,0:T(8,128)(2,1)S(1)} %pad_maximum_fusion.2), channel_id=1, source_target_pairs={{0,64},{16,80},{32,96},{48,112},{64,0},{80,16},{96,32},{112,48},{1... | collective-permute-start | bytes 589832 | tf_op jit(solution)/shard_map/ppermute | solution.py:33
  21.9 16.4 %collective-permute-start.2 = (bf16[4,128,384]{2,1,0:T(8,128)(2,1)S(1)}, bf16[4,128,384]{2,1,0:T(8,128)(2,1)S(1)}, u32[]{:S(2)}, u32[]{:S(2)}) collective-permute-start(bf16[4,128,384]{2,1,0:T(8,128)(2,1)S(1)} %pad_maximum_fusion.1), channel_id=1, source_target_pairs={{0,128},{16,144},{32,160},{48,176},{64,192},{80,208},{96,224},{112... | collective-permute-start | bytes 1179656 | tf_op jit(solution)/shard_map/ppermute | solution.py:33
  26.3 27.1 %collective-permute-start.6 = (bf16[256,768]{1,0:T(8,128)(2,1)S(1)}, bf16[256,768]{1,0:T(8,128)(2,1)S(1)}, u32[]{:S(2)}, u32[]{:S(2)}) collective-permute-start(bf16[256,768]{1,0:T(8,128)(2,1)S(1)} %broadcast_multiply_fusion.refs_0_), channel_id=1, source_target_pairs={{0,4},{1,5},{2,6},{3,7},{4,8},{5,9},{6,10},{7,11},{8,12},{9,13},{1... | collective-permute-start | bytes 1179656 | tf_op jit(solution)/shard_map/ppermute | solution.py:29
  35.4 26.5 %collective-permute-start.8 = (bf16[256,768]{1,0:T(8,128)(2,1)S(1)}, bf16[256,768]{1,0:T(8,128)(2,1)S(1)}, u32[]{:S(2)}, u32[]{:S(2)}) collective-permute-start(bf16[256,768]{1,0:T(8,128)(2,1)S(1)} %broadcast_multiply_fusion.refs_0_), channel_id=1, source_target_pairs={{0,12},{1,13},{2,14},{3,15},{4,0},{5,1},{6,2},{7,3},{8,4},{9,5},{1... | collective-permute-start | bytes 1179656 | tf_op jit(solution)/shard_map/ppermute | solution.py:29
  38.4 71.7 %collective-permute-start.3 = (bf16[8,128,384]{2,1,0:T(8,128)(2,1)S(1)}, bf16[8,128,384]{2,1,0:T(8,128)(2,1)S(1)}, u32[]{:S(2)}, u32[]{:S(2)}) collective-permute-start(bf16[8,128,384]{2,1,0:T(8,128)(2,1)S(1)} %pad_maximum_fusion.refs_0_), channel_id=1, source_target_pairs={{0,384},{16,400},{32,416},{48,432},{64,448},{80,464},{96,480},{112... | collective-permute-start | bytes 2359304 | tf_op jit(solution)/shard_map/ppermute | solution.py:33
  42.5 33.7 %collective-permute-start.18 = (bf16[256,768]{1,0:T(8,128)(2,1)S(1)}, bf16[256,768]{1,0:T(8,128)(2,1)S(1)}, u32[]{:S(2)}, u32[]{:S(2)}) collective-permute-start(bf16[256,768]{1,0:T(8,128)(2,1)S(1)} %broadcast_multiply_fusion.refs_0_), channel_id=1, source_target_pairs={{0,1},{1,2},{2,3},{3,0},{4,5},{5,6},{6,7},{7,4},{8,9},{9,10},{10,1... | collective-permute-start | bytes 1179656 | tf_op jit(solution)/shard_map/ppermute | solution.py:29
  62.0 53.0 %collective-permute-start.14 = (bf16[512,768]{1,0:T(8,128)(2,1)S(1)}, bf16[512,768]{1,0:T(8,128)(2,1)S(1)}, u32[]{:S(2)}, u32[]{:S(2)}) collective-permute-start(bf16[512,768]{1,0:T(8,128)(2,1)S(1)} %constant_dynamic-update-slice_fusion.2.refs_0_), channel_id=1, source_target_pairs={{0,1},{1,2},{2,3},{3,0},{4,5},{5,6},{6,7},{7,4},{8,9},{9,10},{10,1... | collective-permute-start | bytes 2359304 | tf_op jit(solution)/shard_map/ppermute | solution.py:29
  65.4 54.3 %collective-permute-start.15 = (bf16[512,768]{1,0:T(8,128)(2,1)S(1)}, bf16[512,768]{1,0:T(8,128)(2,1)S(1)}, u32[]{:S(2)}, u32[]{:S(2)}) collective-permute-start(bf16[512,768]{1,0:T(8,128)(2,1)S(1)} %constant_dynamic-update-slice_fusion.2.refs_0_), channel_id=1, source_target_pairs={{0,3},{1,0},{2,1},{3,2},{4,7},{5,4},{6,5},{7,6},{8,11},{9,8},{10,9... | collective-permute-start | bytes 2359304 | tf_op jit(solution)/shard_map/ppermute | solution.py:29
  69.0 14.1 %collective-permute-start.7 = (bf16[128,768]{1,0:T(8,128)(2,1)S(1)}, bf16[128,768]{1,0:T(8,128)(2,1)S(1)}, u32[]{:S(2)}, u32[]{:S(2)}) collective-permute-start(bf16[128,768]{1,0:T(8,128)(2,1)S(1)} %slice.32), channel_id=1, source_target_pairs={{0,4},{1,5},{2,6},{3,7},{4,8},{5,9},{6,10},{7,11},{8,12},{9,13},{1... | collective-permute-start | bytes 589832 | tf_op jit(solution)/shard_map/ppermute | solution.py:29
  76.2 62.5 %copy-start = (bf16[256,768]{1,0:T(8,128)(2,1)}, bf16[256,768]{1,0:T(8,128)(2,1)S(1)}, u32[]{:S(2)}) copy-start(bf16[256,768]{1,0:T(8,128)(2,1)S(1)} %collective-permute-done.18.refs_1_) | copy-start | bytes 1179652
  76.3 31.9 %collective-permute-start.9 = (bf16[128,768]{1,0:T(8,128)(2,1)S(1)}, bf16[128,768]{1,0:T(8,128)(2,1)S(1)}, u32[]{:S(2)}, u32[]{:S(2)}) collective-permute-start(bf16[128,768]{1,0:T(8,128)(2,1)S(1)} %slice.33), channel_id=1, source_target_pairs={{0,12},{1,13},{2,14},{3,15},{4,0},{5,1},{6,2},{7,3},{8,4},{9,5},{1... | collective-permute-start | bytes 589832 | tf_op jit(solution)/shard_map/ppermute | solution.py:29
  83.1 29.4 %collective-permute-start.19 = (bf16[256,768]{1,0:T(8,128)(2,1)S(1)}, bf16[256,768]{1,0:T(8,128)(2,1)S(1)}, u32[]{:S(2)}, u32[]{:S(2)}) collective-permute-start(bf16[256,768]{1,0:T(8,128)(2,1)S(1)} %broadcast_multiply_fusion.refs_0_), channel_id=1, source_target_pairs={{0,3},{1,0},{2,1},{3,2},{4,7},{5,4},{6,5},{7,6},{8,11},{9,8},{10,9... | collective-permute-start | bytes 1179656 | tf_op jit(solution)/shard_map/ppermute | solution.py:29
  108.1 33.9 %collective-permute-start.4 = (bf16[8,128,384]{2,1,0:T(8,128)(2,1)S(1)}, bf16[8,128,384]{2,1,0:T(8,128)(2,1)S(1)}, u32[]{:S(2)}, u32[]{:S(2)}) collective-permute-start(bf16[8,128,384]{2,1,0:T(8,128)(2,1)S(1)} %pad_maximum_fusion.refs_0_), channel_id=1, source_target_pairs={{0,16},{16,0},{32,48},{48,32},{64,80},{80,64},{96,112},{112,96},{1... | collective-permute-start | bytes 2359304 | tf_op jit(solution)/shard_map/ppermute | solution.py:33
  110.1 28.6 %copy-start.10 = (bf16[8,128,384]{2,1,0:T(8,128)(2,1)}, bf16[8,128,384]{2,1,0:T(8,128)(2,1)S(1)}, u32[]{:S(2)}) copy-start(bf16[8,128,384]{2,1,0:T(8,128)(2,1)S(1)} %collective-permute-done.3.refs_1_) | copy-start | bytes 2359300
  110.1 36.8 %collective-permute-start.5 = (bf16[8,128,384]{2,1,0:T(8,128)(2,1)S(1)}, bf16[8,128,384]{2,1,0:T(8,128)(2,1)S(1)}, u32[]{:S(2)}, u32[]{:S(2)}) collective-permute-start(bf16[8,128,384]{2,1,0:T(8,128)(2,1)S(1)} %collective-permute-done.3.refs_1_), channel_id=1, source_target_pairs={{0,16},{16,0},{32,48},{48,32},{64,80},{80,64},{96,112},{112,96},{1... | collective-permute-start | bytes 2359304 | tf_op jit(solution)/shard_map/ppermute | solution.py:33
  112.5 29.5 %copy-start.8 = (bf16[256,768]{1,0:T(8,128)(2,1)}, bf16[256,768]{1,0:T(8,128)(2,1)S(1)}, u32[]{:S(2)}) copy-start(bf16[256,768]{1,0:T(8,128)(2,1)S(1)} %constant_dynamic-update-slice_fusion.refs_0_) | copy-start | bytes 1179652
  112.5 38.6 %copy-start.19 = (s32[32]{0:T(128)S(1)}, s32[32]{0:T(128)}, u32[]{:S(2)}) copy-start(s32[32]{0:T(128)} %param.7) | copy-start | bytes 388
  112.6 29.5 %copy-start.2 = (bf16[256,768]{1,0:T(8,128)(2,1)}, bf16[256,768]{1,0:T(8,128)(2,1)S(1)}, u32[]{:S(2)}) copy-start(bf16[256,768]{1,0:T(8,128)(2,1)S(1)} %collective-permute-done.19.refs_2_) | copy-start | bytes 1179652
  112.6 20.3 %collective-permute-start.10 = (bf16[256,768]{1,0:T(8,128)(2,1)S(1)}, bf16[256,768]{1,0:T(8,128)(2,1)S(1)}, u32[]{:S(2)}, u32[]{:S(2)}) collective-permute-start(bf16[256,768]{1,0:T(8,128)(2,1)S(1)} %constant_dynamic-update-slice_fusion.refs_0_), channel_id=1, source_target_pairs={{0,1},{1,2},{2,3},{3,0},{4,5},{5,6},{6,7},{7,4},{8,9},{9,10},{10,1... | collective-permute-start | bytes 1179656 | tf_op jit(solution)/shard_map/ppermute | solution.py:29
  114.9 23.8 %collective-permute-start.11 = (bf16[256,768]{1,0:T(8,128)(2,1)S(1)}, bf16[256,768]{1,0:T(8,128)(2,1)S(1)}, u32[]{:S(2)}, u32[]{:S(2)}) collective-permute-start(bf16[256,768]{1,0:T(8,128)(2,1)S(1)} %constant_dynamic-update-slice_fusion.refs_0_), channel_id=1, source_target_pairs={{0,3},{1,0},{2,1},{3,2},{4,7},{5,4},{6,5},{7,6},{8,11},{9,8},{10,9... | collective-permute-start | bytes 1179656 | tf_op jit(solution)/shard_map/ppermute | solution.py:29
  119.7 11.2 %collective-permute-start.20 = (bf16[128,768]{1,0:T(8,128)(2,1)S(1)}, bf16[128,768]{1,0:T(8,128)(2,1)S(1)}, u32[]{:S(2)}, u32[]{:S(2)}) collective-permute-start(bf16[128,768]{1,0:T(8,128)(2,1)S(1)} %slice.38), channel_id=1, source_target_pairs={{0,1},{1,2},{2,3},{3,0},{4,5},{5,6},{6,7},{7,4},{8,9},{9,10},{10,1... | collective-permute-start | bytes 589832 | tf_op jit(solution)/shard_map/ppermute | solution.py:29
  130.9 16.0 %copy-start.16 = (bf16[128,768]{1,0:T(8,128)(2,1)}, bf16[128,768]{1,0:T(8,128)(2,1)S(1)}, u32[]{:S(2)}) copy-start(bf16[128,768]{1,0:T(8,128)(2,1)S(1)} %collective-permute-done.20.refs_3_) | copy-start | bytes 589828
  130.9 33.7 %collective-permute-start.16 = (bf16[256,768]{1,0:T(8,128)(2,1)}, bf16[256,768]{1,0:T(8,128)(2,1)}, u32[]{:S(2)}, u32[]{:S(2)}) collective-permute-start(bf16[256,768]{1,0:T(8,128)(2,1)} %slice.36), channel_id=1, source_target_pairs={{0,1},{1,2},{2,3},{3,0},{4,5},{5,6},{6,7},{7,4},{8,9},{9,10},{10,1... | collective-permute-start | bytes 1179656 | tf_op jit(solution)/shard_map/ppermute | solution.py:29
  132.9 9.2 %copy-start.4 = (bf16[256,768]{1,0:T(8,128)(2,1)}, bf16[256,768]{1,0:T(8,128)(2,1)S(1)}, u32[]{:S(2)}) copy-start(bf16[256,768]{1,0:T(8,128)(2,1)S(1)} %collective-permute-done.10.refs_1_) | copy-start | bytes 1179652
  132.9 31.7 %collective-permute-start.17 = (bf16[256,768]{1,0:T(8,128)(2,1)}, bf16[256,768]{1,0:T(8,128)(2,1)}, u32[]{:S(2)}, u32[]{:S(2)}) collective-permute-start(bf16[256,768]{1,0:T(8,128)(2,1)} %slice.37), channel_id=1, source_target_pairs={{0,3},{1,0},{2,1},{3,2},{4,7},{5,4},{6,5},{7,6},{8,11},{9,8},{10,9... | collective-permute-start | bytes 1179656 | tf_op jit(solution)/shard_map/ppermute | solution.py:29
  138.7 8.2 %copy-start.6 = (bf16[256,768]{1,0:T(8,128)(2,1)}, bf16[256,768]{1,0:T(8,128)(2,1)S(1)}, u32[]{:S(2)}) copy-start(bf16[256,768]{1,0:T(8,128)(2,1)S(1)} %collective-permute-done.11.refs_2_) | copy-start | bytes 1179652
  138.7 23.3 %collective-permute-start.21 = (bf16[128,768]{1,0:T(8,128)(2,1)}, bf16[128,768]{1,0:T(8,128)(2,1)}, u32[]{:S(2)}, u32[]{:S(2)}) collective-permute-start(bf16[128,768]{1,0:T(8,128)(2,1)} %slice.39), channel_id=1, source_target_pairs={{0,3},{1,0},{2,1},{3,2},{4,7},{5,4},{6,5},{7,6},{8,11},{9,8},{10,9... | collective-permute-start | bytes 589832 | tf_op jit(solution)/shard_map/ppermute | solution.py:29
  142.1 0.9 copy-start.12
  143.0 25.5 %collective-permute-start.12 = (bf16[128,768]{1,0:T(8,128)(2,1)}, bf16[128,768]{1,0:T(8,128)(2,1)}, u32[]{:S(2)}, u32[]{:S(2)}) collective-permute-start(bf16[128,768]{1,0:T(8,128)(2,1)} %slice.34), channel_id=1, source_target_pairs={{0,1},{1,2},{2,3},{3,0},{4,5},{5,6},{6,7},{7,4},{8,9},{9,10},{10,1... | collective-permute-start | bytes 589832 | tf_op jit(solution)/shard_map/ppermute | solution.py:29
  146.9 0.9 copy-start.14
  147.8 20.7 %collective-permute-start.13 = (bf16[128,768]{1,0:T(8,128)(2,1)}, bf16[128,768]{1,0:T(8,128)(2,1)}, u32[]{:S(2)}, u32[]{:S(2)}) collective-permute-start(bf16[128,768]{1,0:T(8,128)(2,1)} %slice.35), channel_id=1, source_target_pairs={{0,3},{1,0},{2,1},{3,2},{4,7},{5,4},{6,5},{7,6},{8,11},{9,8},{10,9... | collective-permute-start | bytes 589832 | tf_op jit(solution)/shard_map/ppermute | solution.py:29
  152.4 1.1 copy-start.11
  153.5 1.1 copy-start.13
  154.6 1.1 copy-start.15
  155.8 6.3 %copy-start.1 = (bf16[256,768]{1,0:T(8,128)(2,1)S(1)}, bf16[256,768]{1,0:T(8,128)(2,1)}, u32[]{:S(2)}) copy-start(bf16[256,768]{1,0:T(8,128)(2,1)} %copy-done) | copy-start | bytes 1179652
  155.8 6.3 %copy-start.3 = (bf16[256,768]{1,0:T(8,128)(2,1)S(1)}, bf16[256,768]{1,0:T(8,128)(2,1)}, u32[]{:S(2)}) copy-start(bf16[256,768]{1,0:T(8,128)(2,1)} %copy-done.2) | copy-start | bytes 1179652
  155.8 6.3 %copy-start.17 = (bf16[128,768]{1,0:T(8,128)(2,1)S(1)}, bf16[128,768]{1,0:T(8,128)(2,1)}, u32[]{:S(2)}) copy-start(bf16[128,768]{1,0:T(8,128)(2,1)} %copy-done.16) | copy-start | bytes 589828
  164.6 4.0 %copy-start.5 = (bf16[256,768]{1,0:T(8,128)(2,1)S(1)}, bf16[256,768]{1,0:T(8,128)(2,1)}, u32[]{:S(2)}) copy-start(bf16[256,768]{1,0:T(8,128)(2,1)} %copy-done.4) | copy-start | bytes 1179652
  164.6 4.0 %copy-start.7 = (bf16[256,768]{1,0:T(8,128)(2,1)S(1)}, bf16[256,768]{1,0:T(8,128)(2,1)}, u32[]{:S(2)}) copy-start(bf16[256,768]{1,0:T(8,128)(2,1)} %copy-done.6) | copy-start | bytes 1179652
  164.6 4.0 %copy-start.9 = (bf16[256,768]{1,0:T(8,128)(2,1)S(1)}, bf16[256,768]{1,0:T(8,128)(2,1)}, u32[]{:S(2)}) copy-start(bf16[256,768]{1,0:T(8,128)(2,1)} %copy-done.8) | copy-start | bytes 1179652

commit v2 on v1

v2 whole, which is shorter than its diff:
```python
import functools

import jax
import jax.numpy as jnp
from jax import lax
from jax.experimental import pallas as pl
from jax.experimental.pallas import tpu as pltpu
from jax.sharding import PartitionSpec as P

BLK = 128
TOK_DEV = 128
DAMPING = 0.001
VMEM_LIMIT = 40 * 1024 * 1024


def shift_x(step):
    return [(i, i // 4 * 4 + (i + step) % 4) for i in range(16)]


def shift_z(step):
    return [(i, (i // 4 + step) % 4 * 4 + i % 4) for i in range(16)]


def flip_dp(mask):
    return [(j, j ^ mask) for j in range(32)]


def hop(value, pairs):
    return lax.ppermute(value, "inv", pairs)


def swap(value, mask):
    return lax.ppermute(value, "dp", flip_dp(mask))


def both_ways(value, shift):
    return hop(value, shift(1)), hop(value, shift(-1))


def flip_x(mask):
    return [(i, i ^ mask) for i in range(16)]


def doubled(value, first):
    near = hop(value, flip_x(first))
    far = hop(jnp.concatenate([value, near], 0), flip_x(first ^ 2))
    return value, near, far


def far_halves(lower, upper, shift):
    half = lower.shape[0] // 2
    return hop(lower[:half], shift(1)), hop(upper[half:], shift(-1))


def eye(order):
    rows = lax.broadcasted_iota(jnp.int32, (order, order), 0)
    cols = lax.broadcasted_iota(jnp.int32, (order, order), 1)
    return rows == cols


def split(value, parts):
    out = []
    for n in range(parts):
        top = value.astype(jnp.bfloat16)
        out.append(top)
        if n < parts - 1:
            value = value - top.astype(jnp.float32)
    return out


def wide_dot(a, b):
    return jnp.dot(a, b, preferred_element_type=jnp.float32)


def dot_split(a, b):
    high, low = split(a, 2)
    b_high, b_low = split(b, 2)
    right = jnp.concatenate(
        [
            jnp.concatenate([b_high, b_low], 1),
            jnp.concatenate([b_high, jnp.zeros_like(b_low)], 1),
        ],
        0,
    )
    both = wide_dot(jnp.concatenate([high, low], 1), right)
    return both[:, :BLK] + both[:, BLK:]


def dot32(a, b):
    a1, a2, a3 = split(a, 3)
    b1, b2, b3 = split(b, 3)
    right = jnp.concatenate([b1, b2], 1)
    both = wide_dot(
        jnp.concatenate([a1, a2], 1), jnp.concatenate([right, right], 0)
    )
    rest = wide_dot(
        jnp.concatenate([a1, a3], 1), jnp.concatenate([b3, b1], 0)
    )
    return both[:, :BLK] + (both[:, BLK:] + rest)


def newton(covs):
    unit = eye(BLK)
    ident = unit.astype(jnp.float32)
    prods, approxes = [], []
    for cov in covs:
        trace = jnp.sum(jnp.where(unit, cov, 0.0))
        damped = cov + (DAMPING * (trace / BLK)) * ident
        total = jnp.sum(jnp.where(unit, damped, 0.0))
        prod = damped / total
        prods.append(prod)
        approxes.append((2.0 * ident - prod) / total)
    prods = [2.0 * d - dot_split(d, d) for d in prods]
    for step in range(6):
        both = [
            jnp.concatenate([x, d], 0) for x, d in zip(approxes, prods, strict=True)
        ]
        both = [
            2.0 * b - dot_split(b, d) for b, d in zip(both, prods, strict=True)
        ]
        approxes = [b[:BLK] for b in both]
        prods = [b[BLK:] for b in both]
    return [
        2.0 * x - dot_split(x, d) for x, d in zip(approxes, prods, strict=True)
    ]


def position():
    inv = lax.axis_index("inv")
    return lax.axis_index("dp"), inv // 4, inv % 4


def live_tokens(tokens_ref):
    return sum(tokens_ref[n] for n in range(tokens_ref.shape[0])).astype(jnp.float32)


def prepare_kernel(
    tokens_hbm,
    exps_hbm,
    acts_hbm,
    grads_hbm,
    masked_ref,
    scaled_ref,
    tokens_ref,
    exps_ref,
    acts_ref,
    grads_ref,
    sems,
):
    copies = [
        pltpu.make_async_copy(source, target, sems.at[n])
        for n, (source, target) in enumerate(
            (
                (tokens_hbm, tokens_ref),
                (exps_hbm, exps_ref),
                (grads_hbm, grads_ref),
                (acts_hbm, acts_ref),
            )
        )
    ]
    for copy in copies:
        copy.start()
    for copy in copies:
        copy.wait()
    inv = lax.axis_index("inv")
    row = lax.broadcasted_iota(jnp.int32, acts_ref.shape, 0)
    live = row < tokens_ref[lax.axis_index("dp")]
    masked_ref[...] = jnp.where(live, acts_ref[...].astype(jnp.float32), 0.0).astype(
        jnp.bfloat16
    )
    slot = lax.broadcasted_iota(jnp.int32, (TOK_DEV, BLK), 0)
    for n in range(grads_ref.shape[0] // TOK_DEV):
        shard = inv * 2 + n
        exps = exps_ref[pl.ds(shard, 1), :].astype(jnp.float32)
        scale = jnp.exp2(-jnp.broadcast_to(exps, (BLK, TOK_DEV)).T)
        scale = jnp.where(slot < tokens_ref[shard], scale, 0.0)
        scale = scale.astype(jnp.bfloat16).astype(jnp.float32)
        rows = slice(n * TOK_DEV, (n + 1) * TOK_DEV)
        for f in range(grads_ref.shape[1] // BLK):
            cols = slice(f * BLK, (f + 1) * BLK)
            scaled_ref[rows, cols] = (
                grads_ref[rows, cols].astype(jnp.float32) * scale
            ).astype(jnp.bfloat16)


def halves_kernel(low_ref, high_ref, first_ref, second_ref):
    half = first_ref.shape[0]
    first_ref[...] = low_ref[:half, :]
    second_ref[...] = high_ref[half:, :]


def join_kernel(low_ref, high_ref, both_ref, first_ref, second_ref):
    rows = low_ref.shape[0]
    both_ref[:rows, :] = low_ref[...]
    both_ref[rows:, :] = high_ref[...]
    halves_kernel(low_ref, high_ref, first_ref, second_ref)


def acts_kernel(tokens_ref, own_ref, core_ref, acts_ref, inv_ref):
    mine = lax.axis_index("dp")
    _, slots, wide = acts_ref.shape
    blocks = wide // BLK
    covs = [jnp.zeros((BLK, BLK), jnp.float32) for _ in range(blocks)]
    for ref, at, core in ((own_ref, 0, 0), (own_ref, 8, 0), (core_ref, 0, 1), (core_ref, 8, 1)):
        for k in range(at, at + 8):
            acts_ref[mine ^ (k * 2 + core)] = ref[k]
        rows = ref[at : at + 8].reshape(8 * slots, wide)
        flipped = rows.T
        for b in range(blocks):
            cols = slice(b * BLK, (b + 1) * BLK)
            covs[b] += jnp.dot(
                flipped[cols], rows[:, cols], preferred_element_type=jnp.float32
            )
    count = live_tokens(tokens_ref)
    for b, inverse in enumerate(newton([c / count for c in covs])):
        inv_ref[b] = inverse


def add_rows(acts_ref, piece, zh, x, half, sums, first=False):
    token = (zh & 3) * 8 + (x & 3) * 2
    if half is None:
        rows = acts_ref[pl.ds(token, 2)].reshape(2 * TOK_DEV, acts_ref.shape[2])
    else:
        rows = acts_ref[token + half]
    wide = rows.shape[1]
    flipped = piece.T
    main = jnp.dot(flipped, rows, preferred_element_type=jnp.float32)
    cov = [
        jnp.dot(
            flipped[f * BLK : (f + 1) * BLK],
            piece[:, f * BLK : (f + 1) * BLK],
            preferred_element_type=jnp.float32,
        )
        for f in range(piece.shape[1] // BLK)
    ]
    cov = jnp.concatenate(cov, 0)
    if first:
        sums[:, :wide] = main
        sums[:, wide:] = cov
    else:
        sums[:, :wide] += main
        sums[:, wide:] += cov


def own_kernel(acts_ref, own, near, far, sums):
    _, zh, x = position()
    rows = 2 * TOK_DEV
    add_rows(acts_ref, own[...], zh, x, None, sums, True)
    add_rows(acts_ref, near[...], zh, x ^ 1, None, sums)
    add_rows(acts_ref, far[:rows, :], zh, x ^ 3, None, sums)
    add_rows(acts_ref, far[rows:, :], zh, x ^ 2, None, sums)


def near_kernel(acts_ref, own, low, high, far_low, far_high, before, sums):
    _, zh, x = position()
    rows = 2 * TOK_DEV
    sums[...] = before[...]
    for ref, at in ((own, x), (low, x - 1), (high, x + 1)):
        add_rows(acts_ref, ref[:rows, :], zh - 1, at, None, sums)
        add_rows(acts_ref, ref[rows:, :], zh + 1, at, None, sums)
    add_rows(acts_ref, far_low[...], zh - 1, x + 2, None, sums)
    add_rows(acts_ref, far_high[...], zh + 1, x + 2, None, sums)


def last_kernel(
    tokens_ref, acts_ref, inv_ref, own, low, high, far_low, far_high, before, out_ref, sums
):
    _, zh, x = position()
    sums[...] = before[...]
    for ref, at in ((own, x), (low, x - 1), (high, x + 1)):
        add_rows(acts_ref, ref[...], zh + 2, at, None, sums)
    add_rows(acts_ref, far_low[...], zh + 2, x + 2, 0, sums)
    add_rows(acts_ref, far_high[...], zh + 2, x + 2, 1, sums)
    wide = acts_ref.shape[2]
    count = live_tokens(tokens_ref)
    outs = sums.shape[0]
    blocks = outs // BLK
    inverse = newton(
        [sums[f * BLK : (f + 1) * BLK, wide:] / count for f in range(blocks)]
    )
    lefts = []
    for b in range(wide // BLK):
        grad = sums[:, b * BLK : (b + 1) * BLK] / count
        lefts.append(dot32(grad, inv_ref[b].T))
    for f in range(blocks):
        rows = slice(f * BLK, (f + 1) * BLK)
        left = jnp.concatenate([part[rows].T for part in lefts], 0)
        out_ref[:, rows] = dot32(left, inverse[f]).astype(jnp.bfloat16)


def call(kernel, smem, vmem, shapes, micros, scratch=()):
    return pl.pallas_call(
        kernel,
        out_shape=shapes,
        in_specs=[pl.BlockSpec(memory_space=pltpu.SMEM)] * len(smem)
        + [pl.BlockSpec(memory_space=pltpu.VMEM)] * len(vmem),
        out_specs=jax.tree.map(
            lambda _: pl.BlockSpec(memory_space=pltpu.VMEM), shapes
        ),
        scratch_shapes=list(scratch),
        compiler_params=pltpu.CompilerParams(vmem_limit_bytes=VMEM_LIMIT),
        cost_estimate=pl.CostEstimate(
            flops=int(micros * 1.15e9), bytes_accessed=0, transcendentals=0
        ),
    )(*smem, *vmem)


def local(acts, grads_out, scale_exp, shard_tokens):
    rows, outs = grads_out.shape
    wide = acts.shape[1]
    sixteen = jnp.bfloat16
    exps = scale_exp.reshape(-1, TOK_DEV)
    operands = (shard_tokens, exps, acts, grads_out)
    masked, scaled = pl.pallas_call(
        prepare_kernel,
        out_shape=(
            jax.ShapeDtypeStruct(acts.shape, sixteen),
            jax.ShapeDtypeStruct(grads_out.shape, sixteen),
        ),
        in_specs=[pl.BlockSpec(memory_space=pltpu.HBM)] * 4,
        out_specs=(pl.BlockSpec(memory_space=pltpu.VMEM),) * 2,
        scratch_shapes=[pltpu.SMEM(shard_tokens.shape, jnp.int32)]
        + [pltpu.VMEM(v.shape, v.dtype) for v in (exps, acts, grads_out)]
        + [pltpu.SemaphoreType.DMA((4,))],
        compiler_params=pltpu.CompilerParams(vmem_limit_bytes=60 * 1024 * 1024),
    )(*operands)
    z_low, z_high = both_ways(scaled, shift_z)
    far_parts = far_halves(z_low, z_high, shift_z)
    own = doubled(scaled, 1)
    near = jnp.concatenate([z_low, z_high], 0)
    far = jnp.concatenate(far_parts, 0)
    far_low, far_high = both_ways(far, shift_x)
    a = masked[None]
    a = jnp.concatenate([a] + [swap(a, 2 * k) for k in (1, 2, 3)], 0)
    a = jnp.concatenate([a] + [swap(a, 8 * k) for k in (1, 2, 3)], 0)
    a, near = lax.optimization_barrier((a, near))
    a_core = swap(a, 1)
    near_low, near_high = both_ways(near, shift_x)
    near_far = far_halves(near_low, near_high, shift_x)
    acts_all, a_inv = call(
        acts_kernel,
        (shard_tokens,),
        (a, a_core),
        (
            jax.ShapeDtypeStruct((32, TOK_DEV, wide), sixteen),
            jax.ShapeDtypeStruct((wide // BLK, BLK, BLK), jnp.float32),
        ),
        4,
    )
    sums_shape = jax.ShapeDtypeStruct((outs, wide + BLK), jnp.float32)
    sums = call(own_kernel, (), (acts_all, *own), sums_shape, 2)
    far_low, far_high, near_far = lax.optimization_barrier(
        (far_low, far_high, near_far)
    )
    far_far = far_halves(far_low, far_high, shift_x)
    sums = call(
        near_kernel,
        (),
        (acts_all, near, near_low, near_high, *near_far, sums),
        sums_shape,
        2,
    )
    return call(
        last_kernel,
        (shard_tokens,),
        (acts_all, a_inv, far, far_low, far_high, *far_far, sums),
        jax.ShapeDtypeStruct((wide, outs), sixteen),
        10,
        scratch=(pltpu.VMEM((outs, wide + BLK), jnp.float32),),
    )


def solution(mesh):
    placed = (P("dp", "inv"), P("inv", "dp"), P(), P())
    return jax.shard_map(
        local, mesh=mesh, in_specs=placed, out_specs=P("inv", "dp"), check_vma=False
    )
```

time: 181 us -> 153 us (0.85)
  the two profiles are of different devices: /device:TPU:32 before, /device:TPU:6 now
where the time goes in v2:
time: 153 us; the launch traced here: 152 us
  starting transfers between devices  78.8 us (52%)
  waiting for transfers between devices  54 us (35%)
  Pallas kernels  16.6 us (11%)
    ppermute x14, starting transfers between devices, hop(): return lax.ppermute(value, 'inv', pairs)  55.5 us
    ppermute x14, waiting for transfers between devices, hop(): return lax.ppermute(value, 'inv', pairs)  53.9 us
    ppermute x7, starting transfers between devices, swap(): return lax.ppermute(value, 'dp', flip_dp(mask))  23.3 us
    pallas_call x4, Pallas kernels, call(): pl.pallas_call(kernel, out_shape=shapes, in_specs=[pl.BlockSpec(memory_sp...  14.6 us
  transfers between devices with their start and end apart: 21, of which 9 were waited for; matrix products, arithmetic and copies ran while one was open for 2% of the time, Pallas kernels for 5%

profile of v2, /device:TPU:6, one launch (start us, length us, event | category | flops | bytes accessed | tf_op | source)
XLA Modules:
  0.0 152.2 jit_solution(5593376131382350613)
XLA Ops:
  0.0 2.0 %shard_map.46 = (bf16[128,384]{1,0:T(8,128)(2,1)}, bf16[256,768]{1,0:T(8,128)(2,1)}) custom-call(s32[32]{0:T(128)} %tokens_ref.3, s32[32,128]{1,0:T(8,128)} %bitcast.7, bf16[128,384]{1,0:T(8,128)(2,1)} %acts_hbm.1, bf16[256,768]{1,0:T(8,128)(2,1)} %grads_hbm.1), custom_call_target="tpu_custom_call" | custom-call | tf_op jit(solution)/shard_map/pallas_call | solution.py:314
  2.0 3.8 %collective-permute-start = (bf16[1,128,384]{2,1,0:T(8,128)(2,1)}, bf16[1,128,384]{2,1,0:T(8,128)(2,1)S(1)}, u32[]{:S(2)}, u32[]{:S(2)}) collective-permute-start(bf16[1,128,384]{2,1,0:T(8,128)(2,1)} %bitcast.3), channel_id=1, source_target_pairs={{0,32},{16,48},{32,0},{48,16},{64,96},{80,112},{96,64},{112,80},{1... | collective-permute-start | bytes 294920 | tf_op jit(solution)/shard_map/ppermute | solution.py:33
  5.8 5.2 %collective-permute-start.1 = (bf16[1,128,384]{2,1,0:T(8,128)(2,1)}, bf16[1,128,384]{2,1,0:T(8,128)(2,1)S(1)}, u32[]{:S(2)}, u32[]{:S(2)}) collective-permute-start(bf16[1,128,384]{2,1,0:T(8,128)(2,1)} %bitcast.4), channel_id=1, source_target_pairs={{0,64},{16,80},{32,96},{48,112},{64,0},{80,16},{96,32},{112,48},{1... | collective-permute-start | bytes 294920 | tf_op jit(solution)/shard_map/ppermute | solution.py:33
  11.0 1.9 %collective-permute-start.2 = (bf16[1,128,384]{2,1,0:T(8,128)(2,1)}, bf16[1,128,384]{2,1,0:T(8,128)(2,1)S(1)}, u32[]{:S(2)}, u32[]{:S(2)}) collective-permute-start(bf16[1,128,384]{2,1,0:T(8,128)(2,1)} %bitcast.5), channel_id=1, source_target_pairs={{0,96},{16,112},{32,64},{48,80},{64,32},{80,48},{96,0},{112,16},{1... | collective-permute-start | bytes 294920 | tf_op jit(solution)/shard_map/ppermute | solution.py:33
  13.0 9.1 %collective-permute-start.6 = (bf16[256,768]{1,0:T(8,128)(2,1)}, bf16[256,768]{1,0:T(8,128)(2,1)S(1)}, u32[]{:S(2)}, u32[]{:S(2)}) collective-permute-start(bf16[256,768]{1,0:T(8,128)(2,1)} %get-tuple-element.16.own), channel_id=1, source_target_pairs={{0,4},{1,5},{2,6},{3,7},{4,8},{5,9},{6,10},{7,11},{8,12},{9,13},{1... | collective-permute-start | bytes 1179656 | tf_op jit(solution)/shard_map/ppermute | solution.py:29
  22.1 4.7 %collective-permute-start.7 = (bf16[256,768]{1,0:T(8,128)(2,1)}, bf16[256,768]{1,0:T(8,128)(2,1)S(1)}, u32[]{:S(2)}, u32[]{:S(2)}) collective-permute-start(bf16[256,768]{1,0:T(8,128)(2,1)} %get-tuple-element.16.own), channel_id=1, source_target_pairs={{0,12},{1,13},{2,14},{3,15},{4,0},{5,1},{6,2},{7,3},{8,4},{9,5},{1... | collective-permute-start | bytes 1179656 | tf_op jit(solution)/shard_map/ppermute | solution.py:29
  26.8 0.9 constant_dynamic-update-slice_fusion.6
  27.7 0.0 collective-permute-done
  27.7 0.0 collective-permute-done.2
  27.7 1.0 pad_maximum_fusion.2
  28.7 3.5 %collective-permute-start.3 = (bf16[4,128,384]{2,1,0:T(8,128)(2,1)S(1)}, bf16[4,128,384]{2,1,0:T(8,128)(2,1)S(1)}, u32[]{:S(2)}, u32[]{:S(2)}) collective-permute-start(bf16[4,128,384]{2,1,0:T(8,128)(2,1)S(1)} %pad_maximum_fusion.2), channel_id=1, source_target_pairs={{0,128},{16,144},{32,160},{48,176},{64,192},{80,208},{96,224},{112... | collective-permute-start | bytes 1179656 | tf_op jit(solution)/shard_map/ppermute | solution.py:33
  32.2 4.8 %collective-permute-start.4 = (bf16[4,128,384]{2,1,0:T(8,128)(2,1)S(1)}, bf16[4,128,384]{2,1,0:T(8,128)(2,1)S(1)}, u32[]{:S(2)}, u32[]{:S(2)}) collective-permute-start(bf16[4,128,384]{2,1,0:T(8,128)(2,1)S(1)} %pad_maximum_fusion.2), channel_id=1, source_target_pairs={{0,256},{16,272},{32,288},{48,304},{64,320},{80,336},{96,352},{112... | collective-permute-start | bytes 1179656 | tf_op jit(solution)/shard_map/ppermute | solution.py:33
  37.0 2.1 %collective-permute-start.5 = (bf16[4,128,384]{2,1,0:T(8,128)(2,1)S(1)}, bf16[4,128,384]{2,1,0:T(8,128)(2,1)S(1)}, u32[]{:S(2)}, u32[]{:S(2)}) collective-permute-start(bf16[4,128,384]{2,1,0:T(8,128)(2,1)S(1)} %pad_maximum_fusion.2), channel_id=1, source_target_pairs={{0,384},{16,400},{32,416},{48,432},{64,448},{80,464},{96,480},{112... | collective-permute-start | bytes 1179656 | tf_op jit(solution)/shard_map/ppermute | solution.py:33
  39.2 2.2 %collective-permute-done.6 = bf16[256,768]{1,0:T(8,128)(2,1)S(1)} collective-permute-done((bf16[256,768]{1,0:T(8,128)(2,1)}, bf16[256,768]{1,0:T(8,128)(2,1)S(1)}, u32[]{:S(2)}, u32[]{:S(2)}) %collective-permute-start.6) | collective-permute-done | bytes 393248 | tf_op jit(solution)/shard_map/ppermute | solution.py:29
  41.4 22.1 %collective-permute-done.7 = bf16[256,768]{1,0:T(8,128)(2,1)S(1)} collective-permute-done((bf16[256,768]{1,0:T(8,128)(2,1)}, bf16[256,768]{1,0:T(8,128)(2,1)S(1)}, u32[]{:S(2)}, u32[]{:S(2)}) %collective-permute-start.7) | collective-permute-done | bytes 393248 | tf_op jit(solution)/shard_map/ppermute | solution.py:29
  63.5 0.1 pad_maximum_fusion.own
  63.6 0.0 copy-start
  63.6 0.0 collective-permute-done.3
  63.6 0.1 constant_dynamic-update-slice_fusion.2
  63.7 0.1 constant_dynamic-update-slice_fusion.1
  63.7 0.0 collective-permute-done.5
  63.8 0.1 constant_dynamic-update-slice_fusion.own_ref
  63.8 1.9 %collective-permute-start.8 = (bf16[16,128,384]{2,1,0:T(8,128)(2,1)S(1)}, bf16[16,128,384]{2,1,0:T(8,128)(2,1)S(1)}, u32[]{:S(2)}, u32[]{:S(2)}) collective-permute-start(bf16[16,128,384]{2,1,0:T(8,128)(2,1)S(1)} %constant_dynamic-update-slice_fusion.own_ref), channel_id=1, source_target_pairs={{0,16},{16,0},{32,48},{48,32},{64,80},{80,64},{96,112},{112,96},{1... | collective-permute-start | bytes 4718600 | tf_op jit(solution)/shard_map/ppermute | solution.py:33
  65.8 2.4 %collective-permute-start.13 = (bf16[512,768]{1,0:T(8,128)(2,1)S(1)}, bf16[512,768]{1,0:T(8,128)(2,1)S(1)}, u32[]{:S(2)}, u32[]{:S(2)}) collective-permute-start(bf16[512,768]{1,0:T(8,128)(2,1)S(1)} %pad_maximum_fusion.own), channel_id=1, source_target_pairs={{0,1},{1,2},{2,3},{3,0},{4,5},{5,6},{6,7},{7,4},{8,9},{9,10},{10,1... | collective-permute-start | bytes 2359304 | tf_op jit(solution)/shard_map/ppermute | solution.py:29
  68.2 3.5 %collective-permute-start.15 = (bf16[512,768]{1,0:T(8,128)(2,1)S(1)}, bf16[512,768]{1,0:T(8,128)(2,1)S(1)}, u32[]{:S(2)}, u32[]{:S(2)}) collective-permute-start(bf16[512,768]{1,0:T(8,128)(2,1)S(1)} %pad_maximum_fusion.own), channel_id=1, source_target_pairs={{0,3},{1,0},{2,1},{3,2},{4,7},{5,4},{6,5},{7,6},{8,11},{9,8},{10,9... | collective-permute-start | bytes 2359304 | tf_op jit(solution)/shard_map/ppermute | solution.py:29
  71.6 7.4 %collective-permute-start.9 = (bf16[128,768]{1,0:T(8,128)(2,1)S(1)}, bf16[128,768]{1,0:T(8,128)(2,1)S(1)}, u32[]{:S(2)}, u32[]{:S(2)}) collective-permute-start(bf16[128,768]{1,0:T(8,128)(2,1)S(1)} %slice.24), channel_id=1, source_target_pairs={{0,4},{1,5},{2,6},{3,7},{4,8},{5,9},{6,10},{7,11},{8,12},{9,13},{1... | collective-permute-start | bytes 589832 | tf_op jit(solution)/shard_map/ppermute | solution.py:29
  79.1 2.3 %collective-permute-start.10 = (bf16[128,768]{1,0:T(8,128)(2,1)S(1)}, bf16[128,768]{1,0:T(8,128)(2,1)S(1)}, u32[]{:S(2)}, u32[]{:S(2)}) collective-permute-start(bf16[128,768]{1,0:T(8,128)(2,1)S(1)} %slice.25), channel_id=1, source_target_pairs={{0,12},{1,13},{2,14},{3,15},{4,0},{5,1},{6,2},{7,3},{8,4},{9,5},{1... | collective-permute-start | bytes 589832 | tf_op jit(solution)/shard_map/ppermute | solution.py:29
  81.4 4.5 %collective-permute-done.9 = bf16[128,768]{1,0:T(8,128)(2,1)S(1)} collective-permute-done((bf16[128,768]{1,0:T(8,128)(2,1)S(1)}, bf16[128,768]{1,0:T(8,128)(2,1)S(1)}, u32[]{:S(2)}, u32[]{:S(2)}) %collective-permute-start.9) | collective-permute-done | bytes 196640 | tf_op jit(solution)/shard_map/ppermute | solution.py:29
  86.0 2.7 %collective-permute-start.19 = (bf16[256,768]{1,0:T(8,128)(2,1)S(1)}, bf16[256,768]{1,0:T(8,128)(2,1)S(1)}, u32[]{:S(2)}, u32[]{:S(2)}) collective-permute-start(bf16[256,768]{1,0:T(8,128)(2,1)S(1)} %copy-done), channel_id=1, source_target_pairs={{0,1},{1,0},{2,3},{3,2},{4,5},{5,4},{6,7},{7,6},{8,9},{9,8},{10,11... | collective-permute-start | bytes 1179656 | tf_op jit(solution)/shard_map/ppermute | solution.py:29
  88.7 8.6 %collective-permute-done.10 = bf16[128,768]{1,0:T(8,128)(2,1)S(1)} collective-permute-done((bf16[128,768]{1,0:T(8,128)(2,1)S(1)}, bf16[128,768]{1,0:T(8,128)(2,1)S(1)}, u32[]{:S(2)}, u32[]{:S(2)}) %collective-permute-start.10) | collective-permute-done | bytes 196640 | tf_op jit(solution)/shard_map/ppermute | solution.py:29
  97.4 3.6 %collective-permute-start.11 = (bf16[256,768]{1,0:T(8,128)(2,1)S(1)}, bf16[256,768]{1,0:T(8,128)(2,1)S(1)}, u32[]{:S(2)}, u32[]{:S(2)}) collective-permute-start(bf16[256,768]{1,0:T(8,128)(2,1)S(1)} %constant_dynamic-update-slice_fusion.7.own), channel_id=1, source_target_pairs={{0,1},{1,2},{2,3},{3,0},{4,5},{5,6},{6,7},{7,4},{8,9},{9,10},{10,1... | collective-permute-start | bytes 1179656 | tf_op jit(solution)/shard_map/ppermute | solution.py:29
  101.0 2.2 %collective-permute-start.12 = (bf16[256,768]{1,0:T(8,128)(2,1)S(1)}, bf16[256,768]{1,0:T(8,128)(2,1)S(1)}, u32[]{:S(2)}, u32[]{:S(2)}) collective-permute-start(bf16[256,768]{1,0:T(8,128)(2,1)S(1)} %constant_dynamic-update-slice_fusion.7.own), channel_id=1, source_target_pairs={{0,3},{1,0},{2,1},{3,2},{4,7},{5,4},{6,5},{7,6},{8,11},{9,8},{10,9... | collective-permute-start | bytes 1179656 | tf_op jit(solution)/shard_map/ppermute | solution.py:29
  103.3 0.0 copy-start.1
  103.3 4.8 %collective-permute-start.14 = (bf16[256,768]{1,0:T(8,128)(2,1)S(1)}, bf16[256,768]{1,0:T(8,128)(2,1)S(1)}, u32[]{:S(2)}, u32[]{:S(2)}) collective-permute-start(bf16[256,768]{1,0:T(8,128)(2,1)S(1)} %slice.26), channel_id=1, source_target_pairs={{0,1},{1,2},{2,3},{3,0},{4,5},{5,6},{6,7},{7,4},{8,9},{9,10},{10,1... | collective-permute-start | bytes 1179656 | tf_op jit(solution)/shard_map/ppermute | solution.py:29
  108.2 1.9 %collective-permute-start.16 = (bf16[256,768]{1,0:T(8,128)(2,1)S(1)}, bf16[256,768]{1,0:T(8,128)(2,1)S(1)}, u32[]{:S(2)}, u32[]{:S(2)}) collective-permute-start(bf16[256,768]{1,0:T(8,128)(2,1)S(1)} %slice.27), channel_id=1, source_target_pairs={{0,3},{1,0},{2,1},{3,2},{4,7},{5,4},{6,5},{7,6},{8,11},{9,8},{10,9... | collective-permute-start | bytes 1179656 | tf_op jit(solution)/shard_map/ppermute | solution.py:29
  110.1 0.1 pad_maximum_fusion.1
  110.1 1.1 collective-permute-done.11.low
  111.2 4.8 %collective-permute-start.20 = (bf16[512,768]{1,0:T(8,128)(2,1)S(1)}, bf16[512,768]{1,0:T(8,128)(2,1)S(1)}, u32[]{:S(2)}, u32[]{:S(2)}) collective-permute-start(bf16[512,768]{1,0:T(8,128)(2,1)S(1)} %pad_maximum_fusion.1), channel_id=1, source_target_pairs={{0,3},{1,2},{2,1},{3,0},{4,7},{5,6},{6,5},{7,4},{8,11},{9,10},{10,... | collective-permute-start | bytes 2359304 | tf_op jit(solution)/shard_map/ppermute | solution.py:29
  116.0 0.1 collective-permute-done.12.high
  116.1 2.8 %collective-permute-done.14.far_low = bf16[256,768]{1,0:T(8,128)(2,1)S(1)} collective-permute-done((bf16[256,768]{1,0:T(8,128)(2,1)S(1)}, bf16[256,768]{1,0:T(8,128)(2,1)S(1)}, u32[]{:S(2)}, u32[]{:S(2)}) %collective-permute-start.14) | collective-permute-done | bytes 393248 | tf_op jit(solution)/shard_map/ppermute | solution.py:29
  118.9 5.7 %collective-permute-done.16.far_high = bf16[256,768]{1,0:T(8,128)(2,1)S(1)} collective-permute-done((bf16[256,768]{1,0:T(8,128)(2,1)S(1)}, bf16[256,768]{1,0:T(8,128)(2,1)S(1)}, u32[]{:S(2)}, u32[]{:S(2)}) %collective-permute-start.16) | collective-permute-done | bytes 393248 | tf_op jit(solution)/shard_map/ppermute | solution.py:29
  124.6 1.9 %collective-permute-start.17 = (bf16[128,768]{1,0:T(8,128)(2,1)S(1)}, bf16[128,768]{1,0:T(8,128)(2,1)S(1)}, u32[]{:S(2)}, u32[]{:S(2)}) collective-permute-start(bf16[128,768]{1,0:T(8,128)(2,1)S(1)} %slice.22), channel_id=1, source_target_pairs={{0,1},{1,2},{2,3},{3,0},{4,5},{5,6},{6,7},{7,4},{8,9},{9,10},{10,1... | collective-permute-start | bytes 589832 | tf_op jit(solution)/shard_map/ppermute | solution.py:29
  126.5 4.1 %collective-permute-start.18 = (bf16[128,768]{1,0:T(8,128)(2,1)S(1)}, bf16[128,768]{1,0:T(8,128)(2,1)S(1)}, u32[]{:S(2)}, u32[]{:S(2)}) collective-permute-start(bf16[128,768]{1,0:T(8,128)(2,1)S(1)} %slice.23), channel_id=1, source_target_pairs={{0,3},{1,0},{2,1},{3,2},{4,7},{5,4},{6,5},{7,6},{8,11},{9,8},{10,9... | collective-permute-start | bytes 589832 | tf_op jit(solution)/shard_map/ppermute | solution.py:29
  130.6 3.8 %shard_map.47 = (bf16[32,128,384]{2,1,0:T(8,128)(2,1)S(1)}, f32[3,128,128]{2,1,0:T(8,128)S(1)}) custom-call(s32[32]{0:T(128)S(1)} %copy-done.1, bf16[16,128,384]{2,1,0:T(8,128)(2,1)S(1)} %constant_dynamic-update-slice_fusion.own_ref, bf16[16,128,384]{2,1,0:T(8,128)(2,1)S(1)} %collective-permute-done.8.core_ref), custom_call_target="tpu_custom_call" | custom-call | flops 4600000000 | tf_op jit(solution)/shard_map/pallas_call | solution.py:292
  134.5 6.9 %collective-permute-done.20.far = bf16[512,768]{1,0:T(8,128)(2,1)S(1)} collective-permute-done((bf16[512,768]{1,0:T(8,128)(2,1)S(1)}, bf16[512,768]{1,0:T(8,128)(2,1)S(1)}, u32[]{:S(2)}, u32[]{:S(2)}) %collective-permute-start.20) | collective-permute-done | bytes 786464 | tf_op jit(solution)/shard_map/ppermute | solution.py:29
  141.4 1.4 shard_map.48.before
  142.8 2.7 %shard_map.49.before = f32[768,512]{1,0:T(8,128)S(1)} custom-call(bf16[32,128,384]{2,1,0:T(8,128)(2,1)S(1)} %get-tuple-element.18.acts_ref, bf16[512,768]{1,0:T(8,128)(2,1)S(1)} %pad_maximum_fusion.own, bf16[512,768]{1,0:T(8,128)(2,1)S(1)} %collective-permute-done.13.low, bf16[512,768]{1,0:T(8,128)(2,1)S(1)} %collective-permute-done.15.high, ...), custom_call_target="tpu_custom_call" | custom-call | flops 2300000000 | tf_op jit(solution)/shard_map/pallas_call | solution.py:292
  145.5 6.7 %shard_map.50 = bf16[384,768]{1,0:T(8,128)(2,1)} custom-call(s32[32]{0:T(128)S(1)} %copy-done.1, bf16[32,128,384]{2,1,0:T(8,128)(2,1)S(1)} %get-tuple-element.18.acts_ref, f32[3,128,128]{2,1,0:T(8,128)S(1)} %get-tuple-element.19.inv_ref, bf16[256,768]{1,0:T(8,128)(2,1)S(1)} %constant_dynamic-update-slice_fusion.7.own, ...), custom_call_target="tpu_custom_call" | custom-call | flops 11500000256 | tf_op jit(solution)/shard_map/pallas_call | solution.py:292
  (21 shorter events, 0.2 us)
Async XLA Ops:
  2.0 25.7 %collective-permute-start = (bf16[1,128,384]{2,1,0:T(8,128)(2,1)}, bf16[1,128,384]{2,1,0:T(8,128)(2,1)S(1)}, u32[]{:S(2)}, u32[]{:S(2)}) collective-permute-start(bf16[1,128,384]{2,1,0:T(8,128)(2,1)} %bitcast.3), channel_id=1, source_target_pairs={{0,32},{16,48},{32,0},{48,16},{64,96},{80,112},{96,64},{112,80},{1... | collective-permute-start | bytes 294920 | tf_op jit(solution)/shard_map/ppermute | solution.py:33
  5.8 21.9 %collective-permute-start.1 = (bf16[1,128,384]{2,1,0:T(8,128)(2,1)}, bf16[1,128,384]{2,1,0:T(8,128)(2,1)S(1)}, u32[]{:S(2)}, u32[]{:S(2)}) collective-permute-start(bf16[1,128,384]{2,1,0:T(8,128)(2,1)} %bitcast.4), channel_id=1, source_target_pairs={{0,64},{16,80},{32,96},{48,112},{64,0},{80,16},{96,32},{112,48},{1... | collective-permute-start | bytes 294920 | tf_op jit(solution)/shard_map/ppermute | solution.py:33
  11.0 16.7 %collective-permute-start.2 = (bf16[1,128,384]{2,1,0:T(8,128)(2,1)}, bf16[1,128,384]{2,1,0:T(8,128)(2,1)S(1)}, u32[]{:S(2)}, u32[]{:S(2)}) collective-permute-start(bf16[1,128,384]{2,1,0:T(8,128)(2,1)} %bitcast.5), channel_id=1, source_target_pairs={{0,96},{16,112},{32,64},{48,80},{64,32},{80,48},{96,0},{112,16},{1... | collective-permute-start | bytes 294920 | tf_op jit(solution)/shard_map/ppermute | solution.py:33
  13.0 28.5 %collective-permute-start.6 = (bf16[256,768]{1,0:T(8,128)(2,1)}, bf16[256,768]{1,0:T(8,128)(2,1)S(1)}, u32[]{:S(2)}, u32[]{:S(2)}) collective-permute-start(bf16[256,768]{1,0:T(8,128)(2,1)} %get-tuple-element.16.own), channel_id=1, source_target_pairs={{0,4},{1,5},{2,6},{3,7},{4,8},{5,9},{6,10},{7,11},{8,12},{9,13},{1... | collective-permute-start | bytes 1179656 | tf_op jit(solution)/shard_map/ppermute | solution.py:29
  22.1 41.5 %collective-permute-start.7 = (bf16[256,768]{1,0:T(8,128)(2,1)}, bf16[256,768]{1,0:T(8,128)(2,1)S(1)}, u32[]{:S(2)}, u32[]{:S(2)}) collective-permute-start(bf16[256,768]{1,0:T(8,128)(2,1)} %get-tuple-element.16.own), channel_id=1, source_target_pairs={{0,12},{1,13},{2,14},{3,15},{4,0},{5,1},{6,2},{7,3},{8,4},{9,5},{1... | collective-permute-start | bytes 1179656 | tf_op jit(solution)/shard_map/ppermute | solution.py:29
  28.7 34.9 %collective-permute-start.3 = (bf16[4,128,384]{2,1,0:T(8,128)(2,1)S(1)}, bf16[4,128,384]{2,1,0:T(8,128)(2,1)S(1)}, u32[]{:S(2)}, u32[]{:S(2)}) collective-permute-start(bf16[4,128,384]{2,1,0:T(8,128)(2,1)S(1)} %pad_maximum_fusion.2), channel_id=1, source_target_pairs={{0,128},{16,144},{32,160},{48,176},{64,192},{80,208},{96,224},{112... | collective-permute-start | bytes 1179656 | tf_op jit(solution)/shard_map/ppermute | solution.py:33
  32.2 31.5 %collective-permute-start.4 = (bf16[4,128,384]{2,1,0:T(8,128)(2,1)S(1)}, bf16[4,128,384]{2,1,0:T(8,128)(2,1)S(1)}, u32[]{:S(2)}, u32[]{:S(2)}) collective-permute-start(bf16[4,128,384]{2,1,0:T(8,128)(2,1)S(1)} %pad_maximum_fusion.2), channel_id=1, source_target_pairs={{0,256},{16,272},{32,288},{48,304},{64,320},{80,336},{96,352},{112... | collective-permute-start | bytes 1179656 | tf_op jit(solution)/shard_map/ppermute | solution.py:33
  37.0 26.7 %collective-permute-start.5 = (bf16[4,128,384]{2,1,0:T(8,128)(2,1)S(1)}, bf16[4,128,384]{2,1,0:T(8,128)(2,1)S(1)}, u32[]{:S(2)}, u32[]{:S(2)}) collective-permute-start(bf16[4,128,384]{2,1,0:T(8,128)(2,1)S(1)} %pad_maximum_fusion.2), channel_id=1, source_target_pairs={{0,384},{16,400},{32,416},{48,432},{64,448},{80,464},{96,480},{112... | collective-permute-start | bytes 1179656 | tf_op jit(solution)/shard_map/ppermute | solution.py:33
  63.6 22.4 %copy-start = (bf16[256,768]{1,0:T(8,128)(2,1)S(1)}, bf16[256,768]{1,0:T(8,128)(2,1)}, u32[]{:S(2)}) copy-start(bf16[256,768]{1,0:T(8,128)(2,1)} %get-tuple-element.16.own) | copy-start | bytes 1179652
  63.8 66.8 %collective-permute-start.8 = (bf16[16,128,384]{2,1,0:T(8,128)(2,1)S(1)}, bf16[16,128,384]{2,1,0:T(8,128)(2,1)S(1)}, u32[]{:S(2)}, u32[]{:S(2)}) collective-permute-start(bf16[16,128,384]{2,1,0:T(8,128)(2,1)S(1)} %constant_dynamic-update-slice_fusion.own_ref), channel_id=1, source_target_pairs={{0,16},{16,0},{32,48},{48,32},{64,80},{80,64},{96,112},{112,96},{1... | collective-permute-start | bytes 4718600 | tf_op jit(solution)/shard_map/ppermute | solution.py:33
  65.8 35.2 %collective-permute-start.13 = (bf16[512,768]{1,0:T(8,128)(2,1)S(1)}, bf16[512,768]{1,0:T(8,128)(2,1)S(1)}, u32[]{:S(2)}, u32[]{:S(2)}) collective-permute-start(bf16[512,768]{1,0:T(8,128)(2,1)S(1)} %pad_maximum_fusion.own), channel_id=1, source_target_pairs={{0,1},{1,2},{2,3},{3,0},{4,5},{5,6},{6,7},{7,4},{8,9},{9,10},{10,1... | collective-permute-start | bytes 2359304 | tf_op jit(solution)/shard_map/ppermute | solution.py:29
  68.2 35.1 %collective-permute-start.15 = (bf16[512,768]{1,0:T(8,128)(2,1)S(1)}, bf16[512,768]{1,0:T(8,128)(2,1)S(1)}, u32[]{:S(2)}, u32[]{:S(2)}) collective-permute-start(bf16[512,768]{1,0:T(8,128)(2,1)S(1)} %pad_maximum_fusion.own), channel_id=1, source_target_pairs={{0,3},{1,0},{2,1},{3,2},{4,7},{5,4},{6,5},{7,6},{8,11},{9,8},{10,9... | collective-permute-start | bytes 2359304 | tf_op jit(solution)/shard_map/ppermute | solution.py:29
  71.6 14.3 %collective-permute-start.9 = (bf16[128,768]{1,0:T(8,128)(2,1)S(1)}, bf16[128,768]{1,0:T(8,128)(2,1)S(1)}, u32[]{:S(2)}, u32[]{:S(2)}) collective-permute-start(bf16[128,768]{1,0:T(8,128)(2,1)S(1)} %slice.24), channel_id=1, source_target_pairs={{0,4},{1,5},{2,6},{3,7},{4,8},{5,9},{6,10},{7,11},{8,12},{9,13},{1... | collective-permute-start | bytes 589832 | tf_op jit(solution)/shard_map/ppermute | solution.py:29
  79.1 18.3 %collective-permute-start.10 = (bf16[128,768]{1,0:T(8,128)(2,1)S(1)}, bf16[128,768]{1,0:T(8,128)(2,1)S(1)}, u32[]{:S(2)}, u32[]{:S(2)}) collective-permute-start(bf16[128,768]{1,0:T(8,128)(2,1)S(1)} %slice.25), channel_id=1, source_target_pairs={{0,12},{1,13},{2,14},{3,15},{4,0},{5,1},{6,2},{7,3},{8,4},{9,5},{1... | collective-permute-start | bytes 589832 | tf_op jit(solution)/shard_map/ppermute | solution.py:29
  86.0 22.2 %collective-permute-start.19 = (bf16[256,768]{1,0:T(8,128)(2,1)S(1)}, bf16[256,768]{1,0:T(8,128)(2,1)S(1)}, u32[]{:S(2)}, u32[]{:S(2)}) collective-permute-start(bf16[256,768]{1,0:T(8,128)(2,1)S(1)} %copy-done), channel_id=1, source_target_pairs={{0,1},{1,0},{2,3},{3,2},{4,5},{5,4},{6,7},{7,6},{8,9},{9,8},{10,11... | collective-permute-start | bytes 1179656 | tf_op jit(solution)/shard_map/ppermute | solution.py:29
  97.4 13.9 %collective-permute-start.11 = (bf16[256,768]{1,0:T(8,128)(2,1)S(1)}, bf16[256,768]{1,0:T(8,128)(2,1)S(1)}, u32[]{:S(2)}, u32[]{:S(2)}) collective-permute-start(bf16[256,768]{1,0:T(8,128)(2,1)S(1)} %constant_dynamic-update-slice_fusion.7.own), channel_id=1, source_target_pairs={{0,1},{1,2},{2,3},{3,0},{4,5},{5,6},{6,7},{7,4},{8,9},{9,10},{10,1... | collective-permute-start | bytes 1179656 | tf_op jit(solution)/shard_map/ppermute | solution.py:29
  101.0 15.1 %collective-permute-start.12 = (bf16[256,768]{1,0:T(8,128)(2,1)S(1)}, bf16[256,768]{1,0:T(8,128)(2,1)S(1)}, u32[]{:S(2)}, u32[]{:S(2)}) collective-permute-start(bf16[256,768]{1,0:T(8,128)(2,1)S(1)} %constant_dynamic-update-slice_fusion.7.own), channel_id=1, source_target_pairs={{0,3},{1,0},{2,1},{3,2},{4,7},{5,4},{6,5},{7,6},{8,11},{9,8},{10,9... | collective-permute-start | bytes 1179656 | tf_op jit(solution)/shard_map/ppermute | solution.py:29
  103.3 27.4 %copy-start.1 = (s32[32]{0:T(128)S(1)}, s32[32]{0:T(128)}, u32[]{:S(2)}) copy-start(s32[32]{0:T(128)} %tokens_ref.3) | copy-start | bytes 388
  103.3 15.6 %collective-permute-start.14 = (bf16[256,768]{1,0:T(8,128)(2,1)S(1)}, bf16[256,768]{1,0:T(8,128)(2,1)S(1)}, u32[]{:S(2)}, u32[]{:S(2)}) collective-permute-start(bf16[256,768]{1,0:T(8,128)(2,1)S(1)} %slice.26), channel_id=1, source_target_pairs={{0,1},{1,2},{2,3},{3,0},{4,5},{5,6},{6,7},{7,4},{8,9},{9,10},{10,1... | collective-permute-start | bytes 1179656 | tf_op jit(solution)/shard_map/ppermute | solution.py:29
  108.2 16.4 %collective-permute-start.16 = (bf16[256,768]{1,0:T(8,128)(2,1)S(1)}, bf16[256,768]{1,0:T(8,128)(2,1)S(1)}, u32[]{:S(2)}, u32[]{:S(2)}) collective-permute-start(bf16[256,768]{1,0:T(8,128)(2,1)S(1)} %slice.27), channel_id=1, source_target_pairs={{0,3},{1,0},{2,1},{3,2},{4,7},{5,4},{6,5},{7,6},{8,11},{9,8},{10,9... | collective-permute-start | bytes 1179656 | tf_op jit(solution)/shard_map/ppermute | solution.py:29
  111.2 30.1 %collective-permute-start.20 = (bf16[512,768]{1,0:T(8,128)(2,1)S(1)}, bf16[512,768]{1,0:T(8,128)(2,1)S(1)}, u32[]{:S(2)}, u32[]{:S(2)}) collective-permute-start(bf16[512,768]{1,0:T(8,128)(2,1)S(1)} %pad_maximum_fusion.1), channel_id=1, source_target_pairs={{0,3},{1,2},{2,1},{3,0},{4,7},{5,6},{6,5},{7,4},{8,11},{9,10},{10,... | collective-permute-start | bytes 2359304 | tf_op jit(solution)/shard_map/ppermute | solution.py:29
  124.6 21.0 %collective-permute-start.17 = (bf16[128,768]{1,0:T(8,128)(2,1)S(1)}, bf16[128,768]{1,0:T(8,128)(2,1)S(1)}, u32[]{:S(2)}, u32[]{:S(2)}) collective-permute-start(bf16[128,768]{1,0:T(8,128)(2,1)S(1)} %slice.22), channel_id=1, source_target_pairs={{0,1},{1,2},{2,3},{3,0},{4,5},{5,6},{6,7},{7,4},{8,9},{9,10},{10,1... | collective-permute-start | bytes 589832 | tf_op jit(solution)/shard_map/ppermute | solution.py:29
  126.5 19.0 %collective-permute-start.18 = (bf16[128,768]{1,0:T(8,128)(2,1)S(1)}, bf16[128,768]{1,0:T(8,128)(2,1)S(1)}, u32[]{:S(2)}, u32[]{:S(2)}) collective-permute-start(bf16[128,768]{1,0:T(8,128)(2,1)S(1)} %slice.23), channel_id=1, source_target_pairs={{0,3},{1,0},{2,1},{3,2},{4,7},{5,4},{6,5},{7,6},{8,11},{9,8},{10,9... | collective-permute-start | bytes 589832 | tf_op jit(solution)/shard_map/ppermute | solution.py:29

commit v3 on v2

--- a/solution.py
+++ b/solution.py
@@ -242,24 +242,17 @@
         sums[:, wide:] += cov
 
 
-def own_kernel(acts_ref, own, near, far, sums):
+def near_kernel(acts_ref, own, low, high, far_low, far_high, sums):
     _, zh, x = position()
-    rows = 2 * TOK_DEV
-    add_rows(acts_ref, own[...], zh, x, None, sums, True)
-    add_rows(acts_ref, near[...], zh, x ^ 1, None, sums)
-    add_rows(acts_ref, far[:rows, :], zh, x ^ 3, None, sums)
-    add_rows(acts_ref, far[rows:, :], zh, x ^ 2, None, sums)
-
-
-def near_kernel(acts_ref, own, low, high, far_low, far_high, before, sums):
-    _, zh, x = position()
-    rows = 2 * TOK_DEV
-    sums[...] = before[...]
+    half = TOK_DEV
     for ref, at in ((own, x), (low, x - 1), (high, x + 1)):
-        add_rows(acts_ref, ref[:rows, :], zh - 1, at, None, sums)
-        add_rows(acts_ref, ref[rows:, :], zh + 1, at, None, sums)
-    add_rows(acts_ref, far_low[...], zh - 1, x + 2, None, sums)
-    add_rows(acts_ref, far_high[...], zh + 1, x + 2, None, sums)
+        for n in range(3):
+            piece = ref[2 * n * half : 2 * (n + 1) * half, :]
+            add_rows(acts_ref, piece, zh + n - 1, at, None, sums, ref is own and not n)
+    add_rows(acts_ref, far_low[: 2 * half, :], zh - 1, x + 2, None, sums)
+    add_rows(acts_ref, far_low[2 * half :, :], zh, x + 2, 0, sums)
+    add_rows(acts_ref, far_high[:half, :], zh, x + 2, 1, sums)
+    add_rows(acts_ref, far_high[half:, :], zh + 1, x + 2, None, sums)
 
 
 def last_kernel(
@@ -326,8 +319,7 @@
     )(*operands)
     z_low, z_high = both_ways(scaled, shift_z)
     far_parts = far_halves(z_low, z_high, shift_z)
-    own = doubled(scaled, 1)
-    near = jnp.concatenate([z_low, z_high], 0)
+    near = jnp.concatenate([z_low, scaled, z_high], 0)
     far = jnp.concatenate(far_parts, 0)
     far_low, far_high = both_ways(far, shift_x)
     a = masked[None]
@@ -348,7 +340,6 @@
         4,
     )
     sums_shape = jax.ShapeDtypeStruct((outs, wide + BLK), jnp.float32)
-    sums = call(own_kernel, (), (acts_all, *own), sums_shape, 2)
     far_low, far_high, near_far = lax.optimization_barrier(
         (far_low, far_high, near_far)
     )
@@ -356,7 +347,7 @@
     sums = call(
         near_kernel,
         (),
-        (acts_all, near, near_low, near_high, *near_far, sums),
+        (acts_all, near, near_low, near_high, *near_far),
         sums_shape,
         2,
     )

time: 153 us -> 145 us (0.948)
  the two profiles are of different devices: /device:TPU:6 before, /device:TPU:160 now
where the time goes in v3:
time: 145 us; the launch traced here: 144 us
  starting transfers between devices  70.4 us (49%)
  waiting for transfers between devices  54.4 us (38%)
  Pallas kernels  16.5 us (11%)
    ppermute x12, starting transfers between devices, hop(): return lax.ppermute(value, 'inv', pairs)  48.4 us
    ppermute x7, waiting for transfers between devices, swap(): return lax.ppermute(value, 'dp', flip_dp(mask))  30.2 us
    ppermute x12, waiting for transfers between devices, hop(): return lax.ppermute(value, 'inv', pairs)  24.2 us
    ppermute x7, starting transfers between devices, swap(): return lax.ppermute(value, 'dp', flip_dp(mask))  22 us
    pallas_call x3, Pallas kernels, call(): pl.pallas_call(kernel, out_shape=shapes, in_specs=[pl.BlockSpec(memory_sp...  14.6 us
  transfers between devices with their start and end apart: 19, of which 6 were waited for; matrix products, arithmetic and copies ran while one was open for 2% of the time, Pallas kernels for 5%

profile of v3, /device:TPU:160, one launch (start us, length us, event | category | flops | bytes accessed | tf_op | source)
XLA Modules:
  0.0 144.1 jit_solution(9621320361929900421)
XLA Ops:
  0.0 2.0 %shard_map.46 = (bf16[128,384]{1,0:T(8,128)(2,1)}, bf16[256,768]{1,0:T(8,128)(2,1)}) custom-call(s32[32]{0:T(128)} %tokens_ref.3, s32[32,128]{1,0:T(8,128)} %bitcast.7, bf16[128,384]{1,0:T(8,128)(2,1)} %acts_hbm.1, bf16[256,768]{1,0:T(8,128)(2,1)} %grads_hbm.1), custom_call_target="tpu_custom_call" | custom-call | tf_op jit(solution)/shard_map/pallas_call | solution.py:307
  2.0 0.0 copy-start.1
  2.0 2.1 %collective-permute-start = (bf16[1,128,384]{2,1,0:T(8,128)(2,1)}, bf16[1,128,384]{2,1,0:T(8,128)(2,1)S(1)}, u32[]{:S(2)}, u32[]{:S(2)}) collective-permute-start(bf16[1,128,384]{2,1,0:T(8,128)(2,1)} %bitcast.3), channel_id=1, source_target_pairs={{0,32},{16,48},{32,0},{48,16},{64,96},{80,112},{96,64},{112,80},{1... | collective-permute-start | bytes 294920 | tf_op jit(solution)/shard_map/ppermute | solution.py:33
  4.2 5.2 %collective-permute-start.1 = (bf16[1,128,384]{2,1,0:T(8,128)(2,1)}, bf16[1,128,384]{2,1,0:T(8,128)(2,1)S(1)}, u32[]{:S(2)}, u32[]{:S(2)}) collective-permute-start(bf16[1,128,384]{2,1,0:T(8,128)(2,1)} %bitcast.4), channel_id=1, source_target_pairs={{0,64},{16,80},{32,96},{48,112},{64,0},{80,16},{96,32},{112,48},{1... | collective-permute-start | bytes 294920 | tf_op jit(solution)/shard_map/ppermute | solution.py:33
  9.4 2.4 %collective-permute-start.2 = (bf16[1,128,384]{2,1,0:T(8,128)(2,1)}, bf16[1,128,384]{2,1,0:T(8,128)(2,1)S(1)}, u32[]{:S(2)}, u32[]{:S(2)}) collective-permute-start(bf16[1,128,384]{2,1,0:T(8,128)(2,1)} %bitcast.5), channel_id=1, source_target_pairs={{0,96},{16,112},{32,64},{48,80},{64,32},{80,48},{96,0},{112,16},{1... | collective-permute-start | bytes 294920 | tf_op jit(solution)/shard_map/ppermute | solution.py:33
  11.7 3.8 %collective-permute-start.7 = (bf16[256,768]{1,0:T(8,128)(2,1)}, bf16[256,768]{1,0:T(8,128)(2,1)S(1)}, u32[]{:S(2)}, u32[]{:S(2)}) collective-permute-start(bf16[256,768]{1,0:T(8,128)(2,1)} %get-tuple-element.16), channel_id=1, source_target_pairs={{0,12},{1,13},{2,14},{3,15},{4,0},{5,1},{6,2},{7,3},{8,4},{9,5},{1... | collective-permute-start | bytes 1179656 | tf_op jit(solution)/shard_map/ppermute | solution.py:29
  15.5 6.0 %collective-permute-start.6 = (bf16[256,768]{1,0:T(8,128)(2,1)}, bf16[256,768]{1,0:T(8,128)(2,1)S(1)}, u32[]{:S(2)}, u32[]{:S(2)}) collective-permute-start(bf16[256,768]{1,0:T(8,128)(2,1)} %get-tuple-element.16), channel_id=1, source_target_pairs={{0,4},{1,5},{2,6},{3,7},{4,8},{5,9},{6,10},{7,11},{8,12},{9,13},{1... | collective-permute-start | bytes 1179656 | tf_op jit(solution)/shard_map/ppermute | solution.py:29
  21.5 0.9 constant_dynamic-update-slice_fusion.6
  22.4 0.0 collective-permute-done
  22.4 0.0 collective-permute-done.1
  22.4 20.4 %collective-permute-done.2 = bf16[1,128,384]{2,1,0:T(8,128)(2,1)S(1)} collective-permute-done((bf16[1,128,384]{2,1,0:T(8,128)(2,1)}, bf16[1,128,384]{2,1,0:T(8,128)(2,1)S(1)}, u32[]{:S(2)}, u32[]{:S(2)}) %collective-permute-start.2) | collective-permute-done | bytes 98336 | tf_op jit(solution)/shard_map/ppermute | solution.py:33
  42.9 1.0 pad_maximum_fusion.1
  43.9 3.5 %collective-permute-start.3 = (bf16[4,128,384]{2,1,0:T(8,128)(2,1)S(1)}, bf16[4,128,384]{2,1,0:T(8,128)(2,1)S(1)}, u32[]{:S(2)}, u32[]{:S(2)}) collective-permute-start(bf16[4,128,384]{2,1,0:T(8,128)(2,1)S(1)} %pad_maximum_fusion.1), channel_id=1, source_target_pairs={{0,128},{16,144},{32,160},{48,176},{64,192},{80,208},{96,224},{112... | collective-permute-start | bytes 1179656 | tf_op jit(solution)/shard_map/ppermute | solution.py:33
  47.3 4.8 %collective-permute-start.4 = (bf16[4,128,384]{2,1,0:T(8,128)(2,1)S(1)}, bf16[4,128,384]{2,1,0:T(8,128)(2,1)S(1)}, u32[]{:S(2)}, u32[]{:S(2)}) collective-permute-start(bf16[4,128,384]{2,1,0:T(8,128)(2,1)S(1)} %pad_maximum_fusion.1), channel_id=1, source_target_pairs={{0,256},{16,272},{32,288},{48,304},{64,320},{80,336},{96,352},{112... | collective-permute-start | bytes 1179656 | tf_op jit(solution)/shard_map/ppermute | solution.py:33
  52.2 2.1 %collective-permute-start.5 = (bf16[4,128,384]{2,1,0:T(8,128)(2,1)S(1)}, bf16[4,128,384]{2,1,0:T(8,128)(2,1)S(1)}, u32[]{:S(2)}, u32[]{:S(2)}) collective-permute-start(bf16[4,128,384]{2,1,0:T(8,128)(2,1)S(1)} %pad_maximum_fusion.1), channel_id=1, source_target_pairs={{0,384},{16,400},{32,416},{48,432},{64,448},{80,464},{96,480},{112... | collective-permute-start | bytes 1179656 | tf_op jit(solution)/shard_map/ppermute | solution.py:33
  54.4 0.0 collective-permute-done.7
  54.4 0.0 collective-permute-done.6
  54.4 0.1 pad_maximum_fusion.own
  54.5 0.0 collective-permute-done.3
  54.5 0.1 constant_dynamic-update-slice_fusion.2
  54.6 5.7 %collective-permute-done.4 = bf16[4,128,384]{2,1,0:T(8,128)(2,1)S(1)} collective-permute-done((bf16[4,128,384]{2,1,0:T(8,128)(2,1)S(1)}, bf16[4,128,384]{2,1,0:T(8,128)(2,1)S(1)}, u32[]{:S(2)}, u32[]{:S(2)}) %collective-permute-start.4) | collective-permute-done | bytes 393248 | tf_op jit(solution)/shard_map/ppermute | solution.py:33
  60.3 0.1 constant_dynamic-update-slice_fusion.1
  60.4 4.0 %collective-permute-done.5 = bf16[4,128,384]{2,1,0:T(8,128)(2,1)S(1)} collective-permute-done((bf16[4,128,384]{2,1,0:T(8,128)(2,1)S(1)}, bf16[4,128,384]{2,1,0:T(8,128)(2,1)S(1)}, u32[]{:S(2)}, u32[]{:S(2)}) %collective-permute-start.5) | collective-permute-done | bytes 393248 | tf_op jit(solution)/shard_map/ppermute | solution.py:33
  64.4 0.1 constant_dynamic-update-slice_fusion.own_ref
  64.5 1.9 %collective-permute-start.8 = (bf16[16,128,384]{2,1,0:T(8,128)(2,1)S(1)}, bf16[16,128,384]{2,1,0:T(8,128)(2,1)S(1)}, u32[]{:S(2)}, u32[]{:S(2)}) collective-permute-start(bf16[16,128,384]{2,1,0:T(8,128)(2,1)S(1)} %constant_dynamic-update-slice_fusion.own_ref), channel_id=1, source_target_pairs={{0,16},{16,0},{32,48},{48,32},{64,80},{80,64},{96,112},{112,96},{1... | collective-permute-start | bytes 4718600 | tf_op jit(solution)/shard_map/ppermute | solution.py:33
  66.4 3.4 %collective-permute-start.13 = (bf16[768,768]{1,0:T(8,128)(2,1)S(1)}, bf16[768,768]{1,0:T(8,128)(2,1)S(1)}, u32[]{:S(2)}, u32[]{:S(2)}) collective-permute-start(bf16[768,768]{1,0:T(8,128)(2,1)S(1)} %pad_maximum_fusion.own), channel_id=1, source_target_pairs={{0,1},{1,2},{2,3},{3,0},{4,5},{5,6},{6,7},{7,4},{8,9},{9,10},{10,1... | collective-permute-start | bytes 3538952 | tf_op jit(solution)/shard_map/ppermute | solution.py:29
  69.8 3.7 %collective-permute-start.15 = (bf16[768,768]{1,0:T(8,128)(2,1)S(1)}, bf16[768,768]{1,0:T(8,128)(2,1)S(1)}, u32[]{:S(2)}, u32[]{:S(2)}) collective-permute-start(bf16[768,768]{1,0:T(8,128)(2,1)S(1)} %pad_maximum_fusion.own), channel_id=1, source_target_pairs={{0,3},{1,0},{2,1},{3,2},{4,7},{5,4},{6,5},{7,6},{8,11},{9,8},{10,9... | collective-permute-start | bytes 3538952 | tf_op jit(solution)/shard_map/ppermute | solution.py:29
  73.5 7.1 %collective-permute-start.9 = (bf16[128,768]{1,0:T(8,128)(2,1)S(1)}, bf16[128,768]{1,0:T(8,128)(2,1)S(1)}, u32[]{:S(2)}, u32[]{:S(2)}) collective-permute-start(bf16[128,768]{1,0:T(8,128)(2,1)S(1)} %slice.24), channel_id=1, source_target_pairs={{0,4},{1,5},{2,6},{3,7},{4,8},{5,9},{6,10},{7,11},{8,12},{9,13},{1... | collective-permute-start | bytes 589832 | tf_op jit(solution)/shard_map/ppermute | solution.py:29
  80.6 0.0 copy-start
  80.6 2.6 %collective-permute-start.10 = (bf16[128,768]{1,0:T(8,128)(2,1)S(1)}, bf16[128,768]{1,0:T(8,128)(2,1)S(1)}, u32[]{:S(2)}, u32[]{:S(2)}) collective-permute-start(bf16[128,768]{1,0:T(8,128)(2,1)S(1)} %slice.25), channel_id=1, source_target_pairs={{0,12},{1,13},{2,14},{3,15},{4,0},{5,1},{6,2},{7,3},{8,4},{9,5},{1... | collective-permute-start | bytes 589832 | tf_op jit(solution)/shard_map/ppermute | solution.py:29
  83.3 14.6 %collective-permute-done.13.low = bf16[768,768]{1,0:T(8,128)(2,1)S(1)} collective-permute-done((bf16[768,768]{1,0:T(8,128)(2,1)S(1)}, bf16[768,768]{1,0:T(8,128)(2,1)S(1)}, u32[]{:S(2)}, u32[]{:S(2)}) %collective-permute-start.13) | collective-permute-done | bytes 1179680 | tf_op jit(solution)/shard_map/ppermute | solution.py:29
  97.9 2.2 %collective-permute-start.14 = (bf16[384,768]{1,0:T(8,128)(2,1)S(1)}, bf16[384,768]{1,0:T(8,128)(2,1)S(1)}, u32[]{:S(2)}, u32[]{:S(2)}) collective-permute-start(bf16[384,768]{1,0:T(8,128)(2,1)S(1)} %slice.26), channel_id=1, source_target_pairs={{0,1},{1,2},{2,3},{3,0},{4,5},{5,6},{6,7},{7,4},{8,9},{9,10},{10,1... | collective-permute-start | bytes 1769480 | tf_op jit(solution)/shard_map/ppermute | solution.py:29
  100.1 0.0 collective-permute-done.15.high
  100.2 4.9 %collective-permute-start.16 = (bf16[384,768]{1,0:T(8,128)(2,1)S(1)}, bf16[384,768]{1,0:T(8,128)(2,1)S(1)}, u32[]{:S(2)}, u32[]{:S(2)}) collective-permute-start(bf16[384,768]{1,0:T(8,128)(2,1)S(1)} %slice.27), channel_id=1, source_target_pairs={{0,3},{1,0},{2,1},{3,2},{4,7},{5,4},{6,5},{7,6},{8,11},{9,8},{10,9... | collective-permute-start | bytes 1769480 | tf_op jit(solution)/shard_map/ppermute | solution.py:29
  105.0 0.0 collective-permute-done.9
  105.1 0.0 collective-permute-done.10
  105.1 1.9 %collective-permute-start.11 = (bf16[256,768]{1,0:T(8,128)(2,1)S(1)}, bf16[256,768]{1,0:T(8,128)(2,1)S(1)}, u32[]{:S(2)}, u32[]{:S(2)}) collective-permute-start(bf16[256,768]{1,0:T(8,128)(2,1)S(1)} %constant_dynamic-update-slice_fusion.7.own), channel_id=1, source_target_pairs={{0,1},{1,2},{2,3},{3,0},{4,5},{5,6},{6,7},{7,4},{8,9},{9,10},{10,1... | collective-permute-start | bytes 1179656 | tf_op jit(solution)/shard_map/ppermute | solution.py:29
  107.0 5.1 %collective-permute-start.12 = (bf16[256,768]{1,0:T(8,128)(2,1)S(1)}, bf16[256,768]{1,0:T(8,128)(2,1)S(1)}, u32[]{:S(2)}, u32[]{:S(2)}) collective-permute-start(bf16[256,768]{1,0:T(8,128)(2,1)S(1)} %constant_dynamic-update-slice_fusion.7.own), channel_id=1, source_target_pairs={{0,3},{1,0},{2,1},{3,2},{4,7},{5,4},{6,5},{7,6},{8,11},{9,8},{10,9... | collective-permute-start | bytes 1179656 | tf_op jit(solution)/shard_map/ppermute | solution.py:29
  112.2 3.8 %shard_map.47 = (bf16[32,128,384]{2,1,0:T(8,128)(2,1)S(1)}, f32[3,128,128]{2,1,0:T(8,128)S(1)}) custom-call(s32[32]{0:T(128)S(1)} %copy-done, bf16[16,128,384]{2,1,0:T(8,128)(2,1)S(1)} %constant_dynamic-update-slice_fusion.own_ref, bf16[16,128,384]{2,1,0:T(8,128)(2,1)S(1)} %collective-permute-done.8.core_ref), custom_call_target="tpu_custom_call" | custom-call | flops 4600000000 | tf_op jit(solution)/shard_map/pallas_call | solution.py:285
  116.0 8.3 %collective-permute-done.11.low = bf16[256,768]{1,0:T(8,128)(2,1)S(1)} collective-permute-done((bf16[256,768]{1,0:T(8,128)(2,1)S(1)}, bf16[256,768]{1,0:T(8,128)(2,1)S(1)}, u32[]{:S(2)}, u32[]{:S(2)}) %collective-permute-start.11) | collective-permute-done | bytes 393248 | tf_op jit(solution)/shard_map/ppermute | solution.py:29
  124.4 1.2 collective-permute-done.12.high
  125.6 0.0 collective-permute-done.14.far_low
  125.6 0.0 collective-permute-done.16.far_high
  125.7 2.9 %collective-permute-start.17 = (bf16[128,768]{1,0:T(8,128)(2,1)S(1)}, bf16[128,768]{1,0:T(8,128)(2,1)S(1)}, u32[]{:S(2)}, u32[]{:S(2)}) collective-permute-start(bf16[128,768]{1,0:T(8,128)(2,1)S(1)} %slice.22), channel_id=1, source_target_pairs={{0,1},{1,2},{2,3},{3,0},{4,5},{5,6},{6,7},{7,4},{8,9},{9,10},{10,1... | collective-permute-start | bytes 589832 | tf_op jit(solution)/shard_map/ppermute | solution.py:29
  128.6 4.8 %collective-permute-start.18 = (bf16[128,768]{1,0:T(8,128)(2,1)S(1)}, bf16[128,768]{1,0:T(8,128)(2,1)S(1)}, u32[]{:S(2)}, u32[]{:S(2)}) collective-permute-start(bf16[128,768]{1,0:T(8,128)(2,1)S(1)} %slice.23), channel_id=1, source_target_pairs={{0,3},{1,0},{2,1},{3,2},{4,7},{5,4},{6,5},{7,6},{8,11},{9,8},{10,9... | collective-permute-start | bytes 589832 | tf_op jit(solution)/shard_map/ppermute | solution.py:29
  133.4 4.0 %shard_map.48.before = f32[768,512]{1,0:T(8,128)S(1)} custom-call(bf16[32,128,384]{2,1,0:T(8,128)(2,1)S(1)} %get-tuple-element.18.acts_ref, bf16[768,768]{1,0:T(8,128)(2,1)S(1)} %pad_maximum_fusion.own, bf16[768,768]{1,0:T(8,128)(2,1)S(1)} %collective-permute-done.13.low, bf16[768,768]{1,0:T(8,128)(2,1)S(1)} %collective-permute-done.15.high, ...), custom_call_target="tpu_custom_call" | custom-call | flops 2300000000 | tf_op jit(solution)/shard_map/pallas_call | solution.py:285
  137.4 0.0 collective-permute-done.18.far_high
  137.5 6.7 %shard_map.49 = bf16[384,768]{1,0:T(8,128)(2,1)} custom-call(s32[32]{0:T(128)S(1)} %copy-done, bf16[32,128,384]{2,1,0:T(8,128)(2,1)S(1)} %get-tuple-element.18.acts_ref, f32[3,128,128]{2,1,0:T(8,128)S(1)} %get-tuple-element.19.inv_ref, bf16[256,768]{1,0:T(8,128)(2,1)S(1)} %constant_dynamic-update-slice_fusion.7.own, ...), custom_call_target="tpu_custom_call" | custom-call | flops 11500000256 | tf_op jit(solution)/shard_map/pallas_call | solution.py:285
  (15 shorter events, 0.2 us)
Async XLA Ops:
  2.0 52.4 %copy-start.1 = (bf16[256,768]{1,0:T(8,128)(2,1)S(1)}, bf16[256,768]{1,0:T(8,128)(2,1)}, u32[]{:S(2)}) copy-start(bf16[256,768]{1,0:T(8,128)(2,1)} %get-tuple-element.16) | copy-start | bytes 1179652
  2.0 20.4 %collective-permute-start = (bf16[1,128,384]{2,1,0:T(8,128)(2,1)}, bf16[1,128,384]{2,1,0:T(8,128)(2,1)S(1)}, u32[]{:S(2)}, u32[]{:S(2)}) collective-permute-start(bf16[1,128,384]{2,1,0:T(8,128)(2,1)} %bitcast.3), channel_id=1, source_target_pairs={{0,32},{16,48},{32,0},{48,16},{64,96},{80,112},{96,64},{112,80},{1... | collective-permute-start | bytes 294920 | tf_op jit(solution)/shard_map/ppermute | solution.py:33
  4.2 18.3 %collective-permute-start.1 = (bf16[1,128,384]{2,1,0:T(8,128)(2,1)}, bf16[1,128,384]{2,1,0:T(8,128)(2,1)S(1)}, u32[]{:S(2)}, u32[]{:S(2)}) collective-permute-start(bf16[1,128,384]{2,1,0:T(8,128)(2,1)} %bitcast.4), channel_id=1, source_target_pairs={{0,64},{16,80},{32,96},{48,112},{64,0},{80,16},{96,32},{112,48},{1... | collective-permute-start | bytes 294920 | tf_op jit(solution)/shard_map/ppermute | solution.py:33
  9.4 33.5 %collective-permute-start.2 = (bf16[1,128,384]{2,1,0:T(8,128)(2,1)}, bf16[1,128,384]{2,1,0:T(8,128)(2,1)S(1)}, u32[]{:S(2)}, u32[]{:S(2)}) collective-permute-start(bf16[1,128,384]{2,1,0:T(8,128)(2,1)} %bitcast.5), channel_id=1, source_target_pairs={{0,96},{16,112},{32,64},{48,80},{64,32},{80,48},{96,0},{112,16},{1... | collective-permute-start | bytes 294920 | tf_op jit(solution)/shard_map/ppermute | solution.py:33
  11.7 42.6 %collective-permute-start.7 = (bf16[256,768]{1,0:T(8,128)(2,1)}, bf16[256,768]{1,0:T(8,128)(2,1)S(1)}, u32[]{:S(2)}, u32[]{:S(2)}) collective-permute-start(bf16[256,768]{1,0:T(8,128)(2,1)} %get-tuple-element.16), channel_id=1, source_target_pairs={{0,12},{1,13},{2,14},{3,15},{4,0},{5,1},{6,2},{7,3},{8,4},{9,5},{1... | collective-permute-start | bytes 1179656 | tf_op jit(solution)/shard_map/ppermute | solution.py:29
  15.5 38.9 %collective-permute-start.6 = (bf16[256,768]{1,0:T(8,128)(2,1)}, bf16[256,768]{1,0:T(8,128)(2,1)S(1)}, u32[]{:S(2)}, u32[]{:S(2)}) collective-permute-start(bf16[256,768]{1,0:T(8,128)(2,1)} %get-tuple-element.16), channel_id=1, source_target_pairs={{0,4},{1,5},{2,6},{3,7},{4,8},{5,9},{6,10},{7,11},{8,12},{9,13},{1... | collective-permute-start | bytes 1179656 | tf_op jit(solution)/shard_map/ppermute | solution.py:29
  43.9 10.6 %collective-permute-start.3 = (bf16[4,128,384]{2,1,0:T(8,128)(2,1)S(1)}, bf16[4,128,384]{2,1,0:T(8,128)(2,1)S(1)}, u32[]{:S(2)}, u32[]{:S(2)}) collective-permute-start(bf16[4,128,384]{2,1,0:T(8,128)(2,1)S(1)} %pad_maximum_fusion.1), channel_id=1, source_target_pairs={{0,128},{16,144},{32,160},{48,176},{64,192},{80,208},{96,224},{112... | collective-permute-start | bytes 1179656 | tf_op jit(solution)/shard_map/ppermute | solution.py:33
  47.3 12.9 %collective-permute-start.4 = (bf16[4,128,384]{2,1,0:T(8,128)(2,1)S(1)}, bf16[4,128,384]{2,1,0:T(8,128)(2,1)S(1)}, u32[]{:S(2)}, u32[]{:S(2)}) collective-permute-start(bf16[4,128,384]{2,1,0:T(8,128)(2,1)S(1)} %pad_maximum_fusion.1), channel_id=1, source_target_pairs={{0,256},{16,272},{32,288},{48,304},{64,320},{80,336},{96,352},{112... | collective-permute-start | bytes 1179656 | tf_op jit(solution)/shard_map/ppermute | solution.py:33
  52.2 12.2 %collective-permute-start.5 = (bf16[4,128,384]{2,1,0:T(8,128)(2,1)S(1)}, bf16[4,128,384]{2,1,0:T(8,128)(2,1)S(1)}, u32[]{:S(2)}, u32[]{:S(2)}) collective-permute-start(bf16[4,128,384]{2,1,0:T(8,128)(2,1)S(1)} %pad_maximum_fusion.1), channel_id=1, source_target_pairs={{0,384},{16,400},{32,416},{48,432},{64,448},{80,464},{96,480},{112... | collective-permute-start | bytes 1179656 | tf_op jit(solution)/shard_map/ppermute | solution.py:33
  64.5 47.7 %collective-permute-start.8 = (bf16[16,128,384]{2,1,0:T(8,128)(2,1)S(1)}, bf16[16,128,384]{2,1,0:T(8,128)(2,1)S(1)}, u32[]{:S(2)}, u32[]{:S(2)}) collective-permute-start(bf16[16,128,384]{2,1,0:T(8,128)(2,1)S(1)} %constant_dynamic-update-slice_fusion.own_ref), channel_id=1, source_target_pairs={{0,16},{16,0},{32,48},{48,32},{64,80},{80,64},{96,112},{112,96},{1... | collective-permute-start | bytes 4718600 | tf_op jit(solution)/shard_map/ppermute | solution.py:33
  66.4 31.5 %collective-permute-start.13 = (bf16[768,768]{1,0:T(8,128)(2,1)S(1)}, bf16[768,768]{1,0:T(8,128)(2,1)S(1)}, u32[]{:S(2)}, u32[]{:S(2)}) collective-permute-start(bf16[768,768]{1,0:T(8,128)(2,1)S(1)} %pad_maximum_fusion.own), channel_id=1, source_target_pairs={{0,1},{1,2},{2,3},{3,0},{4,5},{5,6},{6,7},{7,4},{8,9},{9,10},{10,1... | collective-permute-start | bytes 3538952 | tf_op jit(solution)/shard_map/ppermute | solution.py:29
  69.8 30.3 %collective-permute-start.15 = (bf16[768,768]{1,0:T(8,128)(2,1)S(1)}, bf16[768,768]{1,0:T(8,128)(2,1)S(1)}, u32[]{:S(2)}, u32[]{:S(2)}) collective-permute-start(bf16[768,768]{1,0:T(8,128)(2,1)S(1)} %pad_maximum_fusion.own), channel_id=1, source_target_pairs={{0,3},{1,0},{2,1},{3,2},{4,7},{5,4},{6,5},{7,6},{8,11},{9,8},{10,9... | collective-permute-start | bytes 3538952 | tf_op jit(solution)/shard_map/ppermute | solution.py:29
  73.5 31.6 %collective-permute-start.9 = (bf16[128,768]{1,0:T(8,128)(2,1)S(1)}, bf16[128,768]{1,0:T(8,128)(2,1)S(1)}, u32[]{:S(2)}, u32[]{:S(2)}) collective-permute-start(bf16[128,768]{1,0:T(8,128)(2,1)S(1)} %slice.24), channel_id=1, source_target_pairs={{0,4},{1,5},{2,6},{3,7},{4,8},{5,9},{6,10},{7,11},{8,12},{9,13},{1... | collective-permute-start | bytes 589832 | tf_op jit(solution)/shard_map/ppermute | solution.py:29
  80.6 31.6 %copy-start = (s32[32]{0:T(128)S(1)}, s32[32]{0:T(128)}, u32[]{:S(2)}) copy-start(s32[32]{0:T(128)} %tokens_ref.3) | copy-start | bytes 388
  80.6 24.4 %collective-permute-start.10 = (bf16[128,768]{1,0:T(8,128)(2,1)S(1)}, bf16[128,768]{1,0:T(8,128)(2,1)S(1)}, u32[]{:S(2)}, u32[]{:S(2)}) collective-permute-start(bf16[128,768]{1,0:T(8,128)(2,1)S(1)} %slice.25), channel_id=1, source_target_pairs={{0,12},{1,13},{2,14},{3,15},{4,0},{5,1},{6,2},{7,3},{8,4},{9,5},{1... | collective-permute-start | bytes 589832 | tf_op jit(solution)/shard_map/ppermute | solution.py:29
  97.9 27.7 %collective-permute-start.14 = (bf16[384,768]{1,0:T(8,128)(2,1)S(1)}, bf16[384,768]{1,0:T(8,128)(2,1)S(1)}, u32[]{:S(2)}, u32[]{:S(2)}) collective-permute-start(bf16[384,768]{1,0:T(8,128)(2,1)S(1)} %slice.26), channel_id=1, source_target_pairs={{0,1},{1,2},{2,3},{3,0},{4,5},{5,6},{6,7},{7,4},{8,9},{9,10},{10,1... | collective-permute-start | bytes 1769480 | tf_op jit(solution)/shard_map/ppermute | solution.py:29
  100.2 25.5 %collective-permute-start.16 = (bf16[384,768]{1,0:T(8,128)(2,1)S(1)}, bf16[384,768]{1,0:T(8,128)(2,1)S(1)}, u32[]{:S(2)}, u32[]{:S(2)}) collective-permute-start(bf16[384,768]{1,0:T(8,128)(2,1)S(1)} %slice.27), channel_id=1, source_target_pairs={{0,3},{1,0},{2,1},{3,2},{4,7},{5,4},{6,5},{7,6},{8,11},{9,8},{10,9... | collective-permute-start | bytes 1769480 | tf_op jit(solution)/shard_map/ppermute | solution.py:29
  105.1 19.3 %collective-permute-start.11 = (bf16[256,768]{1,0:T(8,128)(2,1)S(1)}, bf16[256,768]{1,0:T(8,128)(2,1)S(1)}, u32[]{:S(2)}, u32[]{:S(2)}) collective-permute-start(bf16[256,768]{1,0:T(8,128)(2,1)S(1)} %constant_dynamic-update-slice_fusion.7.own), channel_id=1, source_target_pairs={{0,1},{1,2},{2,3},{3,0},{4,5},{5,6},{6,7},{7,4},{8,9},{9,10},{10,1... | collective-permute-start | bytes 1179656 | tf_op jit(solution)/shard_map/ppermute | solution.py:29
  107.0 18.6 %collective-permute-start.12 = (bf16[256,768]{1,0:T(8,128)(2,1)S(1)}, bf16[256,768]{1,0:T(8,128)(2,1)S(1)}, u32[]{:S(2)}, u32[]{:S(2)}) collective-permute-start(bf16[256,768]{1,0:T(8,128)(2,1)S(1)} %constant_dynamic-update-slice_fusion.7.own), channel_id=1, source_target_pairs={{0,3},{1,0},{2,1},{3,2},{4,7},{5,4},{6,5},{7,6},{8,11},{9,8},{10,9... | collective-permute-start | bytes 1179656 | tf_op jit(solution)/shard_map/ppermute | solution.py:29
  125.7 11.8 %collective-permute-start.17 = (bf16[128,768]{1,0:T(8,128)(2,1)S(1)}, bf16[128,768]{1,0:T(8,128)(2,1)S(1)}, u32[]{:S(2)}, u32[]{:S(2)}) collective-permute-start(bf16[128,768]{1,0:T(8,128)(2,1)S(1)} %slice.22), channel_id=1, source_target_pairs={{0,1},{1,2},{2,3},{3,0},{4,5},{5,6},{6,7},{7,4},{8,9},{9,10},{10,1... | collective-permute-start | bytes 589832 | tf_op jit(solution)/shard_map/ppermute | solution.py:29
  128.6 8.8 %collective-permute-start.18 = (bf16[128,768]{1,0:T(8,128)(2,1)S(1)}, bf16[128,768]{1,0:T(8,128)(2,1)S(1)}, u32[]{:S(2)}, u32[]{:S(2)}) collective-permute-start(bf16[128,768]{1,0:T(8,128)(2,1)S(1)} %slice.23), channel_id=1, source_target_pairs={{0,3},{1,0},{2,1},{3,2},{4,7},{5,4},{6,5},{7,6},{8,11},{9,8},{10,9... | collective-permute-start | bytes 589832 | tf_op jit(solution)/shard_map/ppermute | solution.py:29

commit v4 on v3

--- a/solution.py
+++ b/solution.py
@@ -35,16 +35,6 @@
 
 def both_ways(value, shift):
     return hop(value, shift(1)), hop(value, shift(-1))
-
-
-def flip_x(mask):
-    return [(i, i ^ mask) for i in range(16)]
-
-
-def doubled(value, first):
-    near = hop(value, flip_x(first))
-    far = hop(jnp.concatenate([value, near], 0), flip_x(first ^ 2))
-    return value, near, far
 
 
 def far_halves(lower, upper, shift):
@@ -134,53 +124,13 @@
     return sum(tokens_ref[n] for n in range(tokens_ref.shape[0])).astype(jnp.float32)
 
 
-def prepare_kernel(
-    tokens_hbm,
-    exps_hbm,
-    acts_hbm,
-    grads_hbm,
-    masked_ref,
-    scaled_ref,
-    tokens_ref,
-    exps_ref,
-    acts_ref,
-    grads_ref,
-    sems,
-):
-    copies = [
-        pltpu.make_async_copy(source, target, sems.at[n])
-        for n, (source, target) in enumerate(
-            (
-                (tokens_hbm, tokens_ref),
-                (exps_hbm, exps_ref),
-                (grads_hbm, grads_ref),
-                (acts_hbm, acts_ref),
-            )
-        )
-    ]
-    for copy in copies:
-        copy.start()
-    for copy in copies:
-        copy.wait()
-    inv = lax.axis_index("inv")
-    row = lax.broadcasted_iota(jnp.int32, acts_ref.shape, 0)
-    live = row < tokens_ref[lax.axis_index("dp")]
-    masked_ref[...] = jnp.where(live, acts_ref[...].astype(jnp.float32), 0.0).astype(
-        jnp.bfloat16
-    )
+def weights_kernel(tokens_ref, exps_ref, weights_ref):
     slot = lax.broadcasted_iota(jnp.int32, (TOK_DEV, BLK), 0)
-    for n in range(grads_ref.shape[0] // TOK_DEV):
-        shard = inv * 2 + n
-        exps = exps_ref[pl.ds(shard, 1), :].astype(jnp.float32)
+    for shard in range(weights_ref.shape[0]):
+        exps = exps_ref[shard : shard + 1, :].astype(jnp.float32)
         scale = jnp.exp2(-jnp.broadcast_to(exps, (BLK, TOK_DEV)).T)
         scale = jnp.where(slot < tokens_ref[shard], scale, 0.0)
-        scale = scale.astype(jnp.bfloat16).astype(jnp.float32)
-        rows = slice(n * TOK_DEV, (n + 1) * TOK_DEV)
-        for f in range(grads_ref.shape[1] // BLK):
-            cols = slice(f * BLK, (f + 1) * BLK)
-            scaled_ref[rows, cols] = (
-                grads_ref[rows, cols].astype(jnp.float32) * scale
-            ).astype(jnp.bfloat16)
+        weights_ref[shard] = scale.astype(jnp.bfloat16)
 
 
 def halves_kernel(low_ref, high_ref, first_ref, second_ref):
@@ -201,10 +151,15 @@
     _, slots, wide = acts_ref.shape
     blocks = wide // BLK
     covs = [jnp.zeros((BLK, BLK), jnp.float32) for _ in range(blocks)]
+    slot = lax.broadcasted_iota(jnp.int32, (slots, wide), 0)
     for ref, at, core in ((own_ref, 0, 0), (own_ref, 8, 0), (core_ref, 0, 1), (core_ref, 8, 1)):
+        live = []
         for k in range(at, at + 8):
-            acts_ref[mine ^ (k * 2 + core)] = ref[k]
-        rows = ref[at : at + 8].reshape(8 * slots, wide)
+            shard = mine ^ (k * 2 + core)
+            part = jnp.where(slot < tokens_ref[shard], ref[k].astype(jnp.float32), 0.0)
+            live.append(part.astype(jnp.bfloat16))
+            acts_ref[shard] = live[-1]
+        rows = jnp.concatenate(live, 0)
         flipped = rows.T
         for b in range(blocks):
             cols = slice(b * BLK, (b + 1) * BLK)
@@ -216,12 +171,15 @@
         inv_ref[b] = inverse
 
 
-def add_rows(acts_ref, piece, zh, x, half, sums, first=False):
+def add_rows(acts_ref, weights_ref, piece, zh, x, half, sums, first=False):
     token = (zh & 3) * 8 + (x & 3) * 2
     if half is None:
         rows = acts_ref[pl.ds(token, 2)].reshape(2 * TOK_DEV, acts_ref.shape[2])
+        weight = weights_ref[pl.ds(token, 2)].reshape(2 * TOK_DEV, BLK)
     else:
         rows = acts_ref[token + half]
+        weight = weights_ref[token + half]
+    piece = piece * jnp.concatenate([weight] * (piece.shape[1] // BLK), 1)
     wide = rows.shape[1]
     flipped = piece.T
     main = jnp.dot(flipped, rows, preferred_element_type=jnp.float32)
@@ -242,28 +200,55 @@
         sums[:, wide:] += cov
 
 
-def near_kernel(acts_ref, own, low, high, far_low, far_high, sums):
+def mixed_kernel(low_ref, high_ref, top_ref, bottom_ref, first_ref, second_ref):
+    half, quarter = low_ref.shape[0] // 2, top_ref.shape[0]
+    first_ref[:half, :] = low_ref[:half, :]
+    second_ref[:half, :] = high_ref[half:, :]
+    for ref in (first_ref, second_ref):
+        ref[half : half + quarter, :] = top_ref[...]
+        ref[half + quarter :, :] = bottom_ref[...]
+
+
+def rest_kernel(low_ref, high_ref, first_ref, second_ref):
+    half = first_ref.shape[0]
+    first_ref[...] = low_ref[3 * half : 4 * half, :]
+    second_ref[...] = high_ref[4 * half :, :]
+
+
+def near_kernel(
+    acts_ref, weights_ref, own, low, high, far_low, far_high, top, bottom, sums
+):
     _, zh, x = position()
     half = TOK_DEV
     for ref, at in ((own, x), (low, x - 1), (high, x + 1)):
         for n in range(3):
             piece = ref[2 * n * half : 2 * (n + 1) * half, :]
-            add_rows(acts_ref, piece, zh + n - 1, at, None, sums, ref is own and not n)
-    add_rows(acts_ref, far_low[: 2 * half, :], zh - 1, x + 2, None, sums)
-    add_rows(acts_ref, far_low[2 * half :, :], zh, x + 2, 0, sums)
-    add_rows(acts_ref, far_high[:half, :], zh, x + 2, 1, sums)
-    add_rows(acts_ref, far_high[half:, :], zh + 1, x + 2, None, sums)
+            add_rows(acts_ref, weights_ref, piece, zh + n - 1, at, None, sums, ref is own and not n)
+    add_rows(acts_ref, weights_ref, far_low[: 2 * half, :], zh - 1, x + 2, None, sums)
+    add_rows(acts_ref, weights_ref, far_low[2 * half : 3 * half, :], zh, x + 2, 0, sums)
+    add_rows(acts_ref, weights_ref, far_high[:half, :], zh, x + 2, 1, sums)
+    add_rows(acts_ref, weights_ref, far_high[half : 3 * half, :], zh + 1, x + 2, None, sums)
+    add_rows(acts_ref, weights_ref, top[...], zh + 2, x, 0, sums)
+    add_rows(acts_ref, weights_ref, bottom[...], zh + 2, x, 1, sums)
+    for ref, at in ((far_low, x - 1), (far_high, x + 1)):
+        add_rows(acts_ref, weights_ref, ref[3 * half :, :], zh + 2, at, None, sums)
 
 
 def last_kernel(
-    tokens_ref, acts_ref, inv_ref, own, low, high, far_low, far_high, before, out_ref, sums
+    tokens_ref,
+    acts_ref,
+    weights_ref,
+    inv_ref,
+    far_low,
+    far_high,
+    before,
+    out_ref,
+    sums,
 ):
     _, zh, x = position()
     sums[...] = before[...]
-    for ref, at in ((own, x), (low, x - 1), (high, x + 1)):
-        add_rows(acts_ref, ref[...], zh + 2, at, None, sums)
-    add_rows(acts_ref, far_low[...], zh + 2, x + 2, 0, sums)
-    add_rows(acts_ref, far_high[...], zh + 2, x + 2, 1, sums)
+    add_rows(acts_ref, weights_ref, far_low[...], zh + 2, x + 2, 0, sums)
+    add_rows(acts_ref, weights_ref, far_high[...], zh + 2, x + 2, 1, sums)
     wide = acts_ref.shape[2]
     count = live_tokens(tokens_ref)
     outs = sums.shape[0]
@@ -302,33 +287,27 @@
     rows, outs = grads_out.shape
     wide = acts.shape[1]
     sixteen = jnp.bfloat16
-    exps = scale_exp.reshape(-1, TOK_DEV)
-    operands = (shard_tokens, exps, acts, grads_out)
-    masked, scaled = pl.pallas_call(
-        prepare_kernel,
-        out_shape=(
-            jax.ShapeDtypeStruct(acts.shape, sixteen),
-            jax.ShapeDtypeStruct(grads_out.shape, sixteen),
-        ),
-        in_specs=[pl.BlockSpec(memory_space=pltpu.HBM)] * 4,
-        out_specs=(pl.BlockSpec(memory_space=pltpu.VMEM),) * 2,
-        scratch_shapes=[pltpu.SMEM(shard_tokens.shape, jnp.int32)]
-        + [pltpu.VMEM(v.shape, v.dtype) for v in (exps, acts, grads_out)]
-        + [pltpu.SemaphoreType.DMA((4,))],
-        compiler_params=pltpu.CompilerParams(vmem_limit_bytes=60 * 1024 * 1024),
-    )(*operands)
-    z_low, z_high = both_ways(scaled, shift_z)
+    weights = call(
+        weights_kernel,
+        (shard_tokens,),
+        (scale_exp.reshape(-1, TOK_DEV),),
+        jax.ShapeDtypeStruct((shard_tokens.shape[0], TOK_DEV, BLK), sixteen),
+        2,
+    )
+    z_low, z_high = both_ways(grads_out, shift_z)
     far_parts = far_halves(z_low, z_high, shift_z)
-    near = jnp.concatenate([z_low, scaled, z_high], 0)
-    far = jnp.concatenate(far_parts, 0)
-    far_low, far_high = both_ways(far, shift_x)
-    a = masked[None]
+    near = jnp.concatenate([z_low, grads_out, z_high], 0)
+    a = acts[None]
     a = jnp.concatenate([a] + [swap(a, 2 * k) for k in (1, 2, 3)], 0)
     a = jnp.concatenate([a] + [swap(a, 8 * k) for k in (1, 2, 3)], 0)
-    a, near = lax.optimization_barrier((a, near))
+    a, _ = lax.optimization_barrier((a, near))
     a_core = swap(a, 1)
     near_low, near_high = both_ways(near, shift_x)
-    near_far = far_halves(near_low, near_high, shift_x)
+    mixed = jax.ShapeDtypeStruct((near.shape[0] // 2 + rows, outs), sixteen)
+    first, second = call(
+        mixed_kernel, (), (near_low, near_high, *far_parts), (mixed, mixed), 1
+    )
+    mixed_low, mixed_high = hop(first, shift_x(1)), hop(second, shift_x(-1))
     acts_all, a_inv = call(
         acts_kernel,
         (shard_tokens,),
@@ -340,21 +319,22 @@
         4,
     )
     sums_shape = jax.ShapeDtypeStruct((outs, wide + BLK), jnp.float32)
-    far_low, far_high, near_far = lax.optimization_barrier(
-        (far_low, far_high, near_far)
-    )
-    far_far = far_halves(far_low, far_high, shift_x)
+    far_half = jax.ShapeDtypeStruct((rows // 2, outs), sixteen)
+    first, second = call(
+        rest_kernel, (), (mixed_low, mixed_high), (far_half, far_half), 1
+    )
+    far_far = hop(first, shift_x(1)), hop(second, shift_x(-1))
     sums = call(
         near_kernel,
         (),
-        (acts_all, near, near_low, near_high, *near_far),
+        (acts_all, weights, near, near_low, near_high, mixed_low, mixed_high, *far_parts),
         sums_shape,
         2,
     )
     return call(
         last_kernel,
         (shard_tokens,),
-        (acts_all, a_inv, far, far_low, far_high, *far_far, sums),
+        (acts_all, weights, a_inv, *far_far, sums),
         jax.ShapeDtypeStruct((wide, outs), sixteen),
         10,
         scratch=(pltpu.VMEM((outs, wide + BLK), jnp.float32),),

time: 145 us -> 143 us (0.986)
  the two profiles are of different devices: /device:TPU:160 before, /device:TPU:6 now
where the time goes in v4:
time: 143 us; the launch traced here: 141 us
  starting transfers between devices  66.2 us (46%)
  waiting for transfers between devices  55.6 us (39%)
  Pallas kernels  16.8 us (12%)
    ppermute x10, waiting for transfers between devices, hop(): return lax.ppermute(value, 'inv', pairs)  55.6 us
    ppermute x10, starting transfers between devices, hop(): return lax.ppermute(value, 'inv', pairs)  43.4 us
    ppermute x7, starting transfers between devices, swap(): return lax.ppermute(value, 'dp', flip_dp(mask))  22.8 us
    pallas_call x6, Pallas kernels, call(): pl.pallas_call(kernel, out_shape=shapes, in_specs=[pl.BlockSpec(memory_sp...  16.8 us
  transfers between devices with their start and end apart: 17, of which 6 were waited for; matrix products, arithmetic and copies ran while one was open for 2% of the time, Pallas kernels for 8%

profile of v4, /device:TPU:6, one launch (start us, length us, event | category | flops | bytes accessed | tf_op | source)
XLA Modules:
  0.0 141.2 jit_solution(8397767414185494591)
XLA Ops:
  0.0 6.7 %collective-permute-start.2 = (bf16[1,128,384]{2,1,0:T(8,128)(2,1)}, bf16[1,128,384]{2,1,0:T(8,128)(2,1)S(1)}, u32[]{:S(2)}, u32[]{:S(2)}) collective-permute-start(bf16[1,128,384]{2,1,0:T(8,128)(2,1)} %bitcast.4), channel_id=1, source_target_pairs={{0,96},{16,112},{32,64},{48,80},{64,32},{80,48},{96,0},{112,16},{1... | collective-permute-start | bytes 294920 | tf_op jit(solution)/shard_map/ppermute | solution.py:33
  6.7 1.9 %collective-permute-start.1 = (bf16[1,128,384]{2,1,0:T(8,128)(2,1)}, bf16[1,128,384]{2,1,0:T(8,128)(2,1)S(1)}, u32[]{:S(2)}, u32[]{:S(2)}) collective-permute-start(bf16[1,128,384]{2,1,0:T(8,128)(2,1)} %bitcast.5), channel_id=1, source_target_pairs={{0,64},{16,80},{32,96},{48,112},{64,0},{80,16},{96,32},{112,48},{1... | collective-permute-start | bytes 294920 | tf_op jit(solution)/shard_map/ppermute | solution.py:33
  8.6 2.5 %collective-permute-start = (bf16[1,128,384]{2,1,0:T(8,128)(2,1)}, bf16[1,128,384]{2,1,0:T(8,128)(2,1)S(1)}, u32[]{:S(2)}, u32[]{:S(2)}) collective-permute-start(bf16[1,128,384]{2,1,0:T(8,128)(2,1)} %bitcast.6), channel_id=1, source_target_pairs={{0,32},{16,48},{32,0},{48,16},{64,96},{80,112},{96,64},{112,80},{1... | collective-permute-start | bytes 294920 | tf_op jit(solution)/shard_map/ppermute | solution.py:33
  11.1 9.1 %collective-permute-start.6 = (bf16[256,768]{1,0:T(8,128)(2,1)}, bf16[256,768]{1,0:T(8,128)(2,1)S(1)}, u32[]{:S(2)}, u32[]{:S(2)}) collective-permute-start(bf16[256,768]{1,0:T(8,128)(2,1)} %param.5), channel_id=1, source_target_pairs={{0,4},{1,5},{2,6},{3,7},{4,8},{5,9},{6,10},{7,11},{8,12},{9,13},{1... | collective-permute-start | bytes 1179656 | tf_op jit(solution)/shard_map/ppermute | solution.py:29
  20.2 4.7 %collective-permute-start.7 = (bf16[256,768]{1,0:T(8,128)(2,1)}, bf16[256,768]{1,0:T(8,128)(2,1)S(1)}, u32[]{:S(2)}, u32[]{:S(2)}) collective-permute-start(bf16[256,768]{1,0:T(8,128)(2,1)} %param.5), channel_id=1, source_target_pairs={{0,12},{1,13},{2,14},{3,15},{4,0},{5,1},{6,2},{7,3},{8,4},{9,5},{1... | collective-permute-start | bytes 1179656 | tf_op jit(solution)/shard_map/ppermute | solution.py:29
  24.9 0.9 constant_dynamic-update-slice_fusion.6
  25.8 0.0 collective-permute-done.2
  25.9 0.0 collective-permute-done.1
  25.9 0.0 collective-permute-done
  25.9 1.0 pad_maximum_fusion
  26.8 4.9 %collective-permute-start.5 = (bf16[4,128,384]{2,1,0:T(8,128)(2,1)S(1)}, bf16[4,128,384]{2,1,0:T(8,128)(2,1)S(1)}, u32[]{:S(2)}, u32[]{:S(2)}) collective-permute-start(bf16[4,128,384]{2,1,0:T(8,128)(2,1)S(1)} %pad_maximum_fusion), channel_id=1, source_target_pairs={{0,384},{16,400},{32,416},{48,432},{64,448},{80,464},{96,480},{112... | collective-permute-start | bytes 1179656 | tf_op jit(solution)/shard_map/ppermute | solution.py:33
  31.8 2.5 %collective-permute-start.4 = (bf16[4,128,384]{2,1,0:T(8,128)(2,1)S(1)}, bf16[4,128,384]{2,1,0:T(8,128)(2,1)S(1)}, u32[]{:S(2)}, u32[]{:S(2)}) collective-permute-start(bf16[4,128,384]{2,1,0:T(8,128)(2,1)S(1)} %pad_maximum_fusion), channel_id=1, source_target_pairs={{0,256},{16,272},{32,288},{48,304},{64,320},{80,336},{96,352},{112... | collective-permute-start | bytes 1179656 | tf_op jit(solution)/shard_map/ppermute | solution.py:33
  34.3 2.4 %collective-permute-start.3 = (bf16[4,128,384]{2,1,0:T(8,128)(2,1)S(1)}, bf16[4,128,384]{2,1,0:T(8,128)(2,1)S(1)}, u32[]{:S(2)}, u32[]{:S(2)}) collective-permute-start(bf16[4,128,384]{2,1,0:T(8,128)(2,1)S(1)} %pad_maximum_fusion), channel_id=1, source_target_pairs={{0,128},{16,144},{32,160},{48,176},{64,192},{80,208},{96,224},{112... | collective-permute-start | bytes 1179656 | tf_op jit(solution)/shard_map/ppermute | solution.py:33
  36.8 4.4 %collective-permute-done.6 = bf16[256,768]{1,0:T(8,128)(2,1)S(1)} collective-permute-done((bf16[256,768]{1,0:T(8,128)(2,1)}, bf16[256,768]{1,0:T(8,128)(2,1)S(1)}, u32[]{:S(2)}, u32[]{:S(2)}) %collective-permute-start.6) | collective-permute-done | bytes 393248 | tf_op jit(solution)/shard_map/ppermute | solution.py:29
  41.2 0.0 copy-done.2
  41.2 20.8 %collective-permute-done.7 = bf16[256,768]{1,0:T(8,128)(2,1)S(1)} collective-permute-done((bf16[256,768]{1,0:T(8,128)(2,1)}, bf16[256,768]{1,0:T(8,128)(2,1)S(1)}, u32[]{:S(2)}, u32[]{:S(2)}) %collective-permute-start.7) | collective-permute-done | bytes 393248 | tf_op jit(solution)/shard_map/ppermute | solution.py:29
  62.0 2.7 %collective-permute-start.10 = (bf16[768,768]{1,0:T(8,128)(2,1)S(1)}, bf16[768,768]{1,0:T(8,128)(2,1)S(1)}, u32[]{:S(2)}, u32[]{:S(2)}) collective-permute-start(bf16[768,768]{1,0:T(8,128)(2,1)S(1)} %constant_dynamic-update-slice_fusion.7.own), channel_id=1, source_target_pairs={{0,3},{1,0},{2,1},{3,2},{4,7},{5,4},{6,5},{7,6},{8,11},{9,8},{10,9... | collective-permute-start | bytes 3538952 | tf_op jit(solution)/shard_map/ppermute | solution.py:29
  64.8 4.3 %collective-permute-start.9 = (bf16[768,768]{1,0:T(8,128)(2,1)S(1)}, bf16[768,768]{1,0:T(8,128)(2,1)S(1)}, u32[]{:S(2)}, u32[]{:S(2)}) collective-permute-start(bf16[768,768]{1,0:T(8,128)(2,1)S(1)} %constant_dynamic-update-slice_fusion.7.own), channel_id=1, source_target_pairs={{0,1},{1,2},{2,3},{3,0},{4,5},{5,6},{6,7},{7,4},{8,9},{9,10},{10,1... | collective-permute-start | bytes 3538952 | tf_op jit(solution)/shard_map/ppermute | solution.py:29
  69.1 0.0 collective-permute-done.3
  69.1 0.1 constant_dynamic-update-slice_fusion.2
  69.2 0.0 collective-permute-done.4
  69.2 0.1 constant_dynamic-update-slice_fusion.1
  69.3 0.0 collective-permute-done.5
  69.3 0.1 constant_dynamic-update-slice_fusion.own_ref
  69.4 1.9 %collective-permute-start.8 = (bf16[16,128,384]{2,1,0:T(8,128)(2,1)S(1)}, bf16[16,128,384]{2,1,0:T(8,128)(2,1)S(1)}, u32[]{:S(2)}, u32[]{:S(2)}) collective-permute-start(bf16[16,128,384]{2,1,0:T(8,128)(2,1)S(1)} %constant_dynamic-update-slice_fusion.own_ref), channel_id=1, source_target_pairs={{0,16},{16,0},{32,48},{48,32},{64,80},{80,64},{96,112},{112,96},{1... | collective-permute-start | bytes 4718600 | tf_op jit(solution)/shard_map/ppermute | solution.py:33
  71.3 7.2 %collective-permute-start.11 = (bf16[128,768]{1,0:T(8,128)(2,1)S(1)}, bf16[128,768]{1,0:T(8,128)(2,1)S(1)}, u32[]{:S(2)}, u32[]{:S(2)}) collective-permute-start(bf16[128,768]{1,0:T(8,128)(2,1)S(1)} %slice.8), channel_id=1, source_target_pairs={{0,4},{1,5},{2,6},{3,7},{4,8},{5,9},{6,10},{7,11},{8,12},{9,13},{1... | collective-permute-start | bytes 589832 | tf_op jit(solution)/shard_map/ppermute | solution.py:29
  78.5 0.0 copy-start
  78.6 0.0 copy-start.1
  78.6 2.5 %collective-permute-start.12 = (bf16[128,768]{1,0:T(8,128)(2,1)S(1)}, bf16[128,768]{1,0:T(8,128)(2,1)S(1)}, u32[]{:S(2)}, u32[]{:S(2)}) collective-permute-start(bf16[128,768]{1,0:T(8,128)(2,1)S(1)} %slice.9), channel_id=1, source_target_pairs={{0,12},{1,13},{2,14},{3,15},{4,0},{5,1},{6,2},{7,3},{8,4},{9,5},{1... | collective-permute-start | bytes 589832 | tf_op jit(solution)/shard_map/ppermute | solution.py:29
  81.1 10.6 %collective-permute-done.11.top_ref.top = bf16[128,768]{1,0:T(8,128)(2,1)S(1)} collective-permute-done((bf16[128,768]{1,0:T(8,128)(2,1)S(1)}, bf16[128,768]{1,0:T(8,128)(2,1)S(1)}, u32[]{:S(2)}, u32[]{:S(2)}) %collective-permute-start.11) | collective-permute-done | bytes 196640 | tf_op jit(solution)/shard_map/ppermute | solution.py:29
  91.7 2.8 %collective-permute-done.12.bottom_ref.bottom = bf16[128,768]{1,0:T(8,128)(2,1)S(1)} collective-permute-done((bf16[128,768]{1,0:T(8,128)(2,1)S(1)}, bf16[128,768]{1,0:T(8,128)(2,1)S(1)}, u32[]{:S(2)}, u32[]{:S(2)}) %collective-permute-start.12) | collective-permute-done | bytes 196640 | tf_op jit(solution)/shard_map/ppermute | solution.py:29
  94.5 0.0 collective-permute-done.10.high_ref.high
  94.5 0.0 collective-permute-done.9.low_ref.low
  94.5 0.1 shard_map.48
  94.6 4.8 %collective-permute-start.13 = (bf16[640,768]{1,0:T(8,128)(2,1)S(1)}, bf16[640,768]{1,0:T(8,128)(2,1)S(1)}, u32[]{:S(2)}, u32[]{:S(2)}) collective-permute-start(bf16[640,768]{1,0:T(8,128)(2,1)S(1)} %get-tuple-element.15), channel_id=1, source_target_pairs={{0,1},{1,2},{2,3},{3,0},{4,5},{5,6},{6,7},{7,4},{8,9},{9,10},{10,1... | collective-permute-start | bytes 2949128 | tf_op jit(solution)/shard_map/ppermute | solution.py:29
  99.4 1.9 %collective-permute-start.14 = (bf16[640,768]{1,0:T(8,128)(2,1)S(1)}, bf16[640,768]{1,0:T(8,128)(2,1)S(1)}, u32[]{:S(2)}, u32[]{:S(2)}) collective-permute-start(bf16[640,768]{1,0:T(8,128)(2,1)S(1)} %get-tuple-element.16), channel_id=1, source_target_pairs={{0,3},{1,0},{2,1},{3,2},{4,7},{5,4},{6,5},{7,6},{8,11},{9,8},{10,9... | collective-permute-start | bytes 2949128 | tf_op jit(solution)/shard_map/ppermute | solution.py:29
  101.4 0.0 copy-done
  101.4 1.2 shard_map.47.weights_ref
  102.6 0.0 collective-permute-done.8.core_ref
  102.6 4.6 %shard_map.46 = (bf16[32,128,384]{2,1,0:T(8,128)(2,1)S(1)}, f32[3,128,128]{2,1,0:T(8,128)S(1)}) custom-call(s32[32]{0:T(128)S(1)} %copy-done.1, bf16[16,128,384]{2,1,0:T(8,128)(2,1)S(1)} %constant_dynamic-update-slice_fusion.own_ref, bf16[16,128,384]{2,1,0:T(8,128)(2,1)S(1)} %collective-permute-done.8.core_ref), custom_call_target="tpu_custom_call" | custom-call | flops 4600000000 | tf_op jit(solution)/shard_map/pallas_call | solution.py:270
  107.2 13.0 %collective-permute-done.13.low_ref.far_low = bf16[640,768]{1,0:T(8,128)(2,1)S(1)} collective-permute-done((bf16[640,768]{1,0:T(8,128)(2,1)S(1)}, bf16[640,768]{1,0:T(8,128)(2,1)S(1)}, u32[]{:S(2)}, u32[]{:S(2)}) %collective-permute-start.13) | collective-permute-done | bytes 983072 | tf_op jit(solution)/shard_map/ppermute | solution.py:29
  120.2 4.0 %collective-permute-done.14.high_ref.far_high = bf16[640,768]{1,0:T(8,128)(2,1)S(1)} collective-permute-done((bf16[640,768]{1,0:T(8,128)(2,1)S(1)}, bf16[640,768]{1,0:T(8,128)(2,1)S(1)}, u32[]{:S(2)}, u32[]{:S(2)}) %collective-permute-start.14) | collective-permute-done | bytes 983072 | tf_op jit(solution)/shard_map/ppermute | solution.py:29
  124.3 1.9 %collective-permute-start.15 = (bf16[128,768]{1,0:T(8,128)(2,1)S(1)}, bf16[128,768]{1,0:T(8,128)(2,1)S(1)}, u32[]{:S(2)}, u32[]{:S(2)}) collective-permute-start(bf16[128,768]{1,0:T(8,128)(2,1)S(1)} %get-tuple-element.17), channel_id=1, source_target_pairs={{0,1},{1,2},{2,3},{3,0},{4,5},{5,6},{6,7},{7,4},{8,9},{9,10},{10,1... | collective-permute-start | bytes 589832 | tf_op jit(solution)/shard_map/ppermute | solution.py:29
  126.2 4.1 %collective-permute-start.16 = (bf16[128,768]{1,0:T(8,128)(2,1)S(1)}, bf16[128,768]{1,0:T(8,128)(2,1)S(1)}, u32[]{:S(2)}, u32[]{:S(2)}) collective-permute-start(bf16[128,768]{1,0:T(8,128)(2,1)S(1)} %get-tuple-element.18), channel_id=1, source_target_pairs={{0,3},{1,0},{2,1},{3,2},{4,7},{5,4},{6,5},{7,6},{8,11},{9,8},{10,9... | collective-permute-start | bytes 589832 | tf_op jit(solution)/shard_map/ppermute | solution.py:29
  130.3 5.1 %shard_map.50.before = f32[768,512]{1,0:T(8,128)S(1)} custom-call(bf16[32,128,384]{2,1,0:T(8,128)(2,1)S(1)} %get-tuple-element.13.acts_ref, bf16[32,128,128]{2,1,0:T(8,128)(2,1)S(1)} %shard_map.47.weights_ref, bf16[768,768]{1,0:T(8,128)(2,1)S(1)} %constant_dynamic-update-slice_fusion.7.own, bf16[768,768]{1,0:T(8,128)(2,1)S(1)} %collective-permute-done.9.low_ref.low, ...), custom_call_target="tpu_custom_call" | custom-call | flops 2300000000 | tf_op jit(solution)/shard_map/pallas_call | solution.py:270
  135.5 0.0 collective-permute-done.15.far_low
  135.5 0.0 collective-permute-done.16.far_high
  135.5 5.7 %shard_map.51 = bf16[384,768]{1,0:T(8,128)(2,1)} custom-call(s32[32]{0:T(128)S(1)} %copy-done.1, bf16[32,128,384]{2,1,0:T(8,128)(2,1)S(1)} %get-tuple-element.13.acts_ref, bf16[32,128,128]{2,1,0:T(8,128)(2,1)S(1)} %shard_map.47.weights_ref, f32[3,128,128]{2,1,0:T(8,128)S(1)} %get-tuple-element.14.inv_ref, ...), custom_call_target="tpu_custom_call" | custom-call | flops 11500000256 | tf_op jit(solution)/shard_map/pallas_call | solution.py:270
  (11 shorter events, 0.2 us)
Async XLA Ops:
  0.0 41.2 %copy-start.2 = (bf16[256,768]{1,0:T(8,128)(2,1)S(1)}, bf16[256,768]{1,0:T(8,128)(2,1)}, u32[]{:S(2)}) copy-start(bf16[256,768]{1,0:T(8,128)(2,1)} %param.5) | copy-start | bytes 1179652
  0.0 25.8 %collective-permute-start.2 = (bf16[1,128,384]{2,1,0:T(8,128)(2,1)}, bf16[1,128,384]{2,1,0:T(8,128)(2,1)S(1)}, u32[]{:S(2)}, u32[]{:S(2)}) collective-permute-start(bf16[1,128,384]{2,1,0:T(8,128)(2,1)} %bitcast.4), channel_id=1, source_target_pairs={{0,96},{16,112},{32,64},{48,80},{64,32},{80,48},{96,0},{112,16},{1... | collective-permute-start | bytes 294920 | tf_op jit(solution)/shard_map/ppermute | solution.py:33
  6.7 19.2 %collective-permute-start.1 = (bf16[1,128,384]{2,1,0:T(8,128)(2,1)}, bf16[1,128,384]{2,1,0:T(8,128)(2,1)S(1)}, u32[]{:S(2)}, u32[]{:S(2)}) collective-permute-start(bf16[1,128,384]{2,1,0:T(8,128)(2,1)} %bitcast.5), channel_id=1, source_target_pairs={{0,64},{16,80},{32,96},{48,112},{64,0},{80,16},{96,32},{112,48},{1... | collective-permute-start | bytes 294920 | tf_op jit(solution)/shard_map/ppermute | solution.py:33
  8.6 17.3 %collective-permute-start = (bf16[1,128,384]{2,1,0:T(8,128)(2,1)}, bf16[1,128,384]{2,1,0:T(8,128)(2,1)S(1)}, u32[]{:S(2)}, u32[]{:S(2)}) collective-permute-start(bf16[1,128,384]{2,1,0:T(8,128)(2,1)} %bitcast.6), channel_id=1, source_target_pairs={{0,32},{16,48},{32,0},{48,16},{64,96},{80,112},{96,64},{112,80},{1... | collective-permute-start | bytes 294920 | tf_op jit(solution)/shard_map/ppermute | solution.py:33
  11.1 30.1 %collective-permute-start.6 = (bf16[256,768]{1,0:T(8,128)(2,1)}, bf16[256,768]{1,0:T(8,128)(2,1)S(1)}, u32[]{:S(2)}, u32[]{:S(2)}) collective-permute-start(bf16[256,768]{1,0:T(8,128)(2,1)} %param.5), channel_id=1, source_target_pairs={{0,4},{1,5},{2,6},{3,7},{4,8},{5,9},{6,10},{7,11},{8,12},{9,13},{1... | collective-permute-start | bytes 1179656 | tf_op jit(solution)/shard_map/ppermute | solution.py:29
  20.2 41.8 %collective-permute-start.7 = (bf16[256,768]{1,0:T(8,128)(2,1)}, bf16[256,768]{1,0:T(8,128)(2,1)S(1)}, u32[]{:S(2)}, u32[]{:S(2)}) collective-permute-start(bf16[256,768]{1,0:T(8,128)(2,1)} %param.5), channel_id=1, source_target_pairs={{0,12},{1,13},{2,14},{3,15},{4,0},{5,1},{6,2},{7,3},{8,4},{9,5},{1... | collective-permute-start | bytes 1179656 | tf_op jit(solution)/shard_map/ppermute | solution.py:29
  26.8 42.4 %collective-permute-start.5 = (bf16[4,128,384]{2,1,0:T(8,128)(2,1)S(1)}, bf16[4,128,384]{2,1,0:T(8,128)(2,1)S(1)}, u32[]{:S(2)}, u32[]{:S(2)}) collective-permute-start(bf16[4,128,384]{2,1,0:T(8,128)(2,1)S(1)} %pad_maximum_fusion), channel_id=1, source_target_pairs={{0,384},{16,400},{32,416},{48,432},{64,448},{80,464},{96,480},{112... | collective-permute-start | bytes 1179656 | tf_op jit(solution)/shard_map/ppermute | solution.py:33
  31.8 37.4 %collective-permute-start.4 = (bf16[4,128,384]{2,1,0:T(8,128)(2,1)S(1)}, bf16[4,128,384]{2,1,0:T(8,128)(2,1)S(1)}, u32[]{:S(2)}, u32[]{:S(2)}) collective-permute-start(bf16[4,128,384]{2,1,0:T(8,128)(2,1)S(1)} %pad_maximum_fusion), channel_id=1, source_target_pairs={{0,256},{16,272},{32,288},{48,304},{64,320},{80,336},{96,352},{112... | collective-permute-start | bytes 1179656 | tf_op jit(solution)/shard_map/ppermute | solution.py:33
  34.3 34.8 %collective-permute-start.3 = (bf16[4,128,384]{2,1,0:T(8,128)(2,1)S(1)}, bf16[4,128,384]{2,1,0:T(8,128)(2,1)S(1)}, u32[]{:S(2)}, u32[]{:S(2)}) collective-permute-start(bf16[4,128,384]{2,1,0:T(8,128)(2,1)S(1)} %pad_maximum_fusion), channel_id=1, source_target_pairs={{0,128},{16,144},{32,160},{48,176},{64,192},{80,208},{96,224},{112... | collective-permute-start | bytes 1179656 | tf_op jit(solution)/shard_map/ppermute | solution.py:33
  62.0 32.5 %collective-permute-start.10 = (bf16[768,768]{1,0:T(8,128)(2,1)S(1)}, bf16[768,768]{1,0:T(8,128)(2,1)S(1)}, u32[]{:S(2)}, u32[]{:S(2)}) collective-permute-start(bf16[768,768]{1,0:T(8,128)(2,1)S(1)} %constant_dynamic-update-slice_fusion.7.own), channel_id=1, source_target_pairs={{0,3},{1,0},{2,1},{3,2},{4,7},{5,4},{6,5},{7,6},{8,11},{9,8},{10,9... | collective-permute-start | bytes 3538952 | tf_op jit(solution)/shard_map/ppermute | solution.py:29
  64.8 29.7 %collective-permute-start.9 = (bf16[768,768]{1,0:T(8,128)(2,1)S(1)}, bf16[768,768]{1,0:T(8,128)(2,1)S(1)}, u32[]{:S(2)}, u32[]{:S(2)}) collective-permute-start(bf16[768,768]{1,0:T(8,128)(2,1)S(1)} %constant_dynamic-update-slice_fusion.7.own), channel_id=1, source_target_pairs={{0,1},{1,2},{2,3},{3,0},{4,5},{5,6},{6,7},{7,4},{8,9},{9,10},{10,1... | collective-permute-start | bytes 3538952 | tf_op jit(solution)/shard_map/ppermute | solution.py:29
  69.4 33.2 %collective-permute-start.8 = (bf16[16,128,384]{2,1,0:T(8,128)(2,1)S(1)}, bf16[16,128,384]{2,1,0:T(8,128)(2,1)S(1)}, u32[]{:S(2)}, u32[]{:S(2)}) collective-permute-start(bf16[16,128,384]{2,1,0:T(8,128)(2,1)S(1)} %constant_dynamic-update-slice_fusion.own_ref), channel_id=1, source_target_pairs={{0,16},{16,0},{32,48},{48,32},{64,80},{80,64},{96,112},{112,96},{1... | collective-permute-start | bytes 4718600 | tf_op jit(solution)/shard_map/ppermute | solution.py:33
  71.3 20.4 %collective-permute-start.11 = (bf16[128,768]{1,0:T(8,128)(2,1)S(1)}, bf16[128,768]{1,0:T(8,128)(2,1)S(1)}, u32[]{:S(2)}, u32[]{:S(2)}) collective-permute-start(bf16[128,768]{1,0:T(8,128)(2,1)S(1)} %slice.8), channel_id=1, source_target_pairs={{0,4},{1,5},{2,6},{3,7},{4,8},{5,9},{6,10},{7,11},{8,12},{9,13},{1... | collective-permute-start | bytes 589832 | tf_op jit(solution)/shard_map/ppermute | solution.py:29
  78.5 22.8 %copy-start = (s32[4096]{0:T(1024)S(1)}, s32[4096]{0:T(1024)}, u32[]{:S(2)}) copy-start(s32[4096]{0:T(1024)} %param.6) | copy-start | bytes 49156
  78.6 22.8 %copy-start.1 = (s32[32]{0:T(128)S(1)}, s32[32]{0:T(128)}, u32[]{:S(2)}) copy-start(s32[32]{0:T(128)} %tokens_ref.5) | copy-start | bytes 388
  78.6 15.9 %collective-permute-start.12 = (bf16[128,768]{1,0:T(8,128)(2,1)S(1)}, bf16[128,768]{1,0:T(8,128)(2,1)S(1)}, u32[]{:S(2)}, u32[]{:S(2)}) collective-permute-start(bf16[128,768]{1,0:T(8,128)(2,1)S(1)} %slice.9), channel_id=1, source_target_pairs={{0,12},{1,13},{2,14},{3,15},{4,0},{5,1},{6,2},{7,3},{8,4},{9,5},{1... | collective-permute-start | bytes 589832 | tf_op jit(solution)/shard_map/ppermute | solution.py:29
  94.6 25.6 %collective-permute-start.13 = (bf16[640,768]{1,0:T(8,128)(2,1)S(1)}, bf16[640,768]{1,0:T(8,128)(2,1)S(1)}, u32[]{:S(2)}, u32[]{:S(2)}) collective-permute-start(bf16[640,768]{1,0:T(8,128)(2,1)S(1)} %get-tuple-element.15), channel_id=1, source_target_pairs={{0,1},{1,2},{2,3},{3,0},{4,5},{5,6},{6,7},{7,4},{8,9},{9,10},{10,1... | collective-permute-start | bytes 2949128 | tf_op jit(solution)/shard_map/ppermute | solution.py:29
  99.4 24.8 %collective-permute-start.14 = (bf16[640,768]{1,0:T(8,128)(2,1)S(1)}, bf16[640,768]{1,0:T(8,128)(2,1)S(1)}, u32[]{:S(2)}, u32[]{:S(2)}) collective-permute-start(bf16[640,768]{1,0:T(8,128)(2,1)S(1)} %get-tuple-element.16), channel_id=1, source_target_pairs={{0,3},{1,0},{2,1},{3,2},{4,7},{5,4},{6,5},{7,6},{8,11},{9,8},{10,9... | collective-permute-start | bytes 2949128 | tf_op jit(solution)/shard_map/ppermute | solution.py:29
  124.3 11.2 %collective-permute-start.15 = (bf16[128,768]{1,0:T(8,128)(2,1)S(1)}, bf16[128,768]{1,0:T(8,128)(2,1)S(1)}, u32[]{:S(2)}, u32[]{:S(2)}) collective-permute-start(bf16[128,768]{1,0:T(8,128)(2,1)S(1)} %get-tuple-element.17), channel_id=1, source_target_pairs={{0,1},{1,2},{2,3},{3,0},{4,5},{5,6},{6,7},{7,4},{8,9},{9,10},{10,1... | collective-permute-start | bytes 589832 | tf_op jit(solution)/shard_map/ppermute | solution.py:29
  126.2 9.3 %collective-permute-start.16 = (bf16[128,768]{1,0:T(8,128)(2,1)S(1)}, bf16[128,768]{1,0:T(8,128)(2,1)S(1)}, u32[]{:S(2)}, u32[]{:S(2)}) collective-permute-start(bf16[128,768]{1,0:T(8,128)(2,1)S(1)} %get-tuple-element.18), channel_id=1, source_target_pairs={{0,3},{1,0},{2,1},{3,2},{4,7},{5,4},{6,5},{7,6},{8,11},{9,8},{10,9... | collective-permute-start | bytes 589832 | tf_op jit(solution)/shard_map/ppermute | solution.py:29

commit v5 on v4

--- a/solution.py
+++ b/solution.py
@@ -1,5 +1,3 @@
-import functools
-
 import jax
 import jax.numpy as jnp
 from jax import lax
@@ -146,7 +144,9 @@
     halves_kernel(low_ref, high_ref, first_ref, second_ref)
 
 
-def acts_kernel(tokens_ref, own_ref, core_ref, acts_ref, inv_ref):
+def acts_kernel(
+    tokens_ref, own_ref, core_ref, weights_ref, near, low, high, acts_ref, inv_ref, sums
+):
     mine = lax.axis_index("dp")
     _, slots, wide = acts_ref.shape
     blocks = wide // BLK
@@ -169,9 +169,10 @@
     count = live_tokens(tokens_ref)
     for b, inverse in enumerate(newton([c / count for c in covs])):
         inv_ref[b] = inverse
-
-
-def add_rows(acts_ref, weights_ref, piece, zh, x, half, sums, first=False):
+    add_near(acts_ref, weights_ref, near, low, high, sums)
+
+
+def add_rows(acts_ref, weights_ref, piece, zh, x, half, sums, first=False, base=None):
     token = (zh & 3) * 8 + (x & 3) * 2
     if half is None:
         rows = acts_ref[pl.ds(token, 2)].reshape(2 * TOK_DEV, acts_ref.shape[2])
@@ -196,8 +197,9 @@
         sums[:, :wide] = main
         sums[:, wide:] = cov
     else:
-        sums[:, :wide] += main
-        sums[:, wide:] += cov
+        base = sums if base is None else base
+        sums[:, :wide] = base[:, :wide] + main
+        sums[:, wide:] = base[:, wide:] + cov
 
 
 def mixed_kernel(low_ref, high_ref, top_ref, bottom_ref, first_ref, second_ref):
@@ -215,23 +217,32 @@
     second_ref[...] = high_ref[4 * half :, :]
 
 
-def near_kernel(
-    acts_ref, weights_ref, own, low, high, far_low, far_high, top, bottom, sums
+def add_near(acts_ref, weights_ref, own, low, high, sums):
+    _, zh, x = position()
+    step = 2 * TOK_DEV
+    for ref, at in ((own, x), (low, x - 1), (high, x + 1)):
+        for n in range(3):
+            piece = ref[n * step : (n + 1) * step, :]
+            start = ref is own and not n
+            add_rows(acts_ref, weights_ref, piece, zh + n - 1, at, None, sums, start)
+
+
+def mixed_sums_kernel(
+    acts_ref, weights_ref, far_low, far_high, top, bottom, before, sums
 ):
     _, zh, x = position()
     half = TOK_DEV
-    for ref, at in ((own, x), (low, x - 1), (high, x + 1)):
-        for n in range(3):
-            piece = ref[2 * n * half : 2 * (n + 1) * half, :]
-            add_rows(acts_ref, weights_ref, piece, zh + n - 1, at, None, sums, ref is own and not n)
-    add_rows(acts_ref, weights_ref, far_low[: 2 * half, :], zh - 1, x + 2, None, sums)
-    add_rows(acts_ref, weights_ref, far_low[2 * half : 3 * half, :], zh, x + 2, 0, sums)
-    add_rows(acts_ref, weights_ref, far_high[:half, :], zh, x + 2, 1, sums)
-    add_rows(acts_ref, weights_ref, far_high[half : 3 * half, :], zh + 1, x + 2, None, sums)
-    add_rows(acts_ref, weights_ref, top[...], zh + 2, x, 0, sums)
-    add_rows(acts_ref, weights_ref, bottom[...], zh + 2, x, 1, sums)
-    for ref, at in ((far_low, x - 1), (far_high, x + 1)):
-        add_rows(acts_ref, weights_ref, ref[3 * half :, :], zh + 2, at, None, sums)
+    base = before
+    for piece, z, at in (
+        (far_low[: 2 * half, :], zh - 1, x + 2),
+        (jnp.concatenate([far_low[2 * half : 3 * half, :], far_high[:half, :]], 0), zh, x + 2),
+        (far_high[half : 3 * half, :], zh + 1, x + 2),
+        (jnp.concatenate([top[...], bottom[...]], 0), zh + 2, x),
+        (far_low[3 * half :, :], zh + 2, x - 1),
+        (far_high[3 * half :, :], zh + 2, x + 1),
+    ):
+        add_rows(acts_ref, weights_ref, piece, z, at, None, sums, base=base)
+        base = None
 
 
 def last_kernel(
@@ -246,9 +257,10 @@
     sums,
 ):
     _, zh, x = position()
-    sums[...] = before[...]
-    add_rows(acts_ref, weights_ref, far_low[...], zh + 2, x + 2, 0, sums)
-    add_rows(acts_ref, weights_ref, far_high[...], zh + 2, x + 2, 1, sums)
+    piece = jnp.concatenate([far_low[...], far_high[...]], 0)
+    add_rows(
+        acts_ref, weights_ref, piece, zh + 2, x + 2, None, sums, base=before
+    )
     wide = acts_ref.shape[2]
     count = live_tokens(tokens_ref)
     outs = sums.shape[0]
@@ -308,26 +320,27 @@
         mixed_kernel, (), (near_low, near_high, *far_parts), (mixed, mixed), 1
     )
     mixed_low, mixed_high = hop(first, shift_x(1)), hop(second, shift_x(-1))
-    acts_all, a_inv = call(
+    sums_shape = jax.ShapeDtypeStruct((outs, wide + BLK), jnp.float32)
+    acts_all, a_inv, sums = call(
         acts_kernel,
         (shard_tokens,),
-        (a, a_core),
+        (a, a_core, weights, near, near_low, near_high),
         (
             jax.ShapeDtypeStruct((32, TOK_DEV, wide), sixteen),
             jax.ShapeDtypeStruct((wide // BLK, BLK, BLK), jnp.float32),
+            sums_shape,
         ),
         4,
     )
-    sums_shape = jax.ShapeDtypeStruct((outs, wide + BLK), jnp.float32)
     far_half = jax.ShapeDtypeStruct((rows // 2, outs), sixteen)
     first, second = call(
         rest_kernel, (), (mixed_low, mixed_high), (far_half, far_half), 1
     )
     far_far = hop(first, shift_x(1)), hop(second, shift_x(-1))
     sums = call(
-        near_kernel,
+        mixed_sums_kernel,
         (),
-        (acts_all, weights, near, near_low, near_high, mixed_low, mixed_high, *far_parts),
+        (acts_all, weights, mixed_low, mixed_high, *far_parts, sums),
         sums_shape,
         2,
     )

time: 143 us -> 142 us (level)
  transfers between devices with their start and end apart: 17 -> 17, of which waited for: 6 -> 7; matrix products, arithmetic and copies ran while one was open for 2% -> 2% of each run, Pallas kernels for 8% -> 8%
where the time goes in v5:
time: 142 us; the launch traced here: 141 us
  starting transfers between devices  66.2 us (47%)
  waiting for transfers between devices  55 us (39%)
  Pallas kernels  16.8 us (12%)
    ppermute x10, waiting for transfers between devices, hop(): return lax.ppermute(value, 'inv', pairs)  55 us
    ppermute x10, starting transfers between devices, hop(): return lax.ppermute(value, 'inv', pairs)  43.4 us
    ppermute x7, starting transfers between devices, swap(): return lax.ppermute(value, 'dp', flip_dp(mask))  22.8 us
    pallas_call x6, Pallas kernels, call(): pl.pallas_call(kernel, out_shape=shapes, in_specs=[pl.BlockSpec(memory_sp...  16.8 us
  transfers between devices with their start and end apart: 17, of which 7 were waited for; matrix products, arithmetic and copies ran while one was open for 2% of the time, Pallas kernels for 8%

profile of v5, /device:TPU:6, one launch (start us, length us, event | category | flops | bytes accessed | tf_op | source)
XLA Modules:
  0.0 140.6 jit_solution(1878782570898140099)
XLA Ops:
  0.0 6.7 %collective-permute-start.2 = (bf16[1,128,384]{2,1,0:T(8,128)(2,1)}, bf16[1,128,384]{2,1,0:T(8,128)(2,1)S(1)}, u32[]{:S(2)}, u32[]{:S(2)}) collective-permute-start(bf16[1,128,384]{2,1,0:T(8,128)(2,1)} %bitcast.4), channel_id=1, source_target_pairs={{0,96},{16,112},{32,64},{48,80},{64,32},{80,48},{96,0},{112,16},{1... | collective-permute-start | bytes 294920 | tf_op jit(solution)/shard_map/ppermute | solution.py:31
  6.7 1.9 %collective-permute-start.1 = (bf16[1,128,384]{2,1,0:T(8,128)(2,1)}, bf16[1,128,384]{2,1,0:T(8,128)(2,1)S(1)}, u32[]{:S(2)}, u32[]{:S(2)}) collective-permute-start(bf16[1,128,384]{2,1,0:T(8,128)(2,1)} %bitcast.5), channel_id=1, source_target_pairs={{0,64},{16,80},{32,96},{48,112},{64,0},{80,16},{96,32},{112,48},{1... | collective-permute-start | bytes 294920 | tf_op jit(solution)/shard_map/ppermute | solution.py:31
  8.6 2.5 %collective-permute-start = (bf16[1,128,384]{2,1,0:T(8,128)(2,1)}, bf16[1,128,384]{2,1,0:T(8,128)(2,1)S(1)}, u32[]{:S(2)}, u32[]{:S(2)}) collective-permute-start(bf16[1,128,384]{2,1,0:T(8,128)(2,1)} %bitcast.6), channel_id=1, source_target_pairs={{0,32},{16,48},{32,0},{48,16},{64,96},{80,112},{96,64},{112,80},{1... | collective-permute-start | bytes 294920 | tf_op jit(solution)/shard_map/ppermute | solution.py:31
  11.1 9.1 %collective-permute-start.6 = (bf16[256,768]{1,0:T(8,128)(2,1)}, bf16[256,768]{1,0:T(8,128)(2,1)S(1)}, u32[]{:S(2)}, u32[]{:S(2)}) collective-permute-start(bf16[256,768]{1,0:T(8,128)(2,1)} %param.5), channel_id=1, source_target_pairs={{0,4},{1,5},{2,6},{3,7},{4,8},{5,9},{6,10},{7,11},{8,12},{9,13},{1... | collective-permute-start | bytes 1179656 | tf_op jit(solution)/shard_map/ppermute | solution.py:27
  20.2 4.7 %collective-permute-start.7 = (bf16[256,768]{1,0:T(8,128)(2,1)}, bf16[256,768]{1,0:T(8,128)(2,1)S(1)}, u32[]{:S(2)}, u32[]{:S(2)}) collective-permute-start(bf16[256,768]{1,0:T(8,128)(2,1)} %param.5), channel_id=1, source_target_pairs={{0,12},{1,13},{2,14},{3,15},{4,0},{5,1},{6,2},{7,3},{8,4},{9,5},{1... | collective-permute-start | bytes 1179656 | tf_op jit(solution)/shard_map/ppermute | solution.py:27
  24.9 0.9 constant_dynamic-update-slice_fusion.6
  25.8 0.0 collective-permute-done.2
  25.9 0.0 collective-permute-done.1
  25.9 0.0 collective-permute-done
  25.9 1.0 pad_maximum_fusion
  26.8 4.9 %collective-permute-start.5 = (bf16[4,128,384]{2,1,0:T(8,128)(2,1)S(1)}, bf16[4,128,384]{2,1,0:T(8,128)(2,1)S(1)}, u32[]{:S(2)}, u32[]{:S(2)}) collective-permute-start(bf16[4,128,384]{2,1,0:T(8,128)(2,1)S(1)} %pad_maximum_fusion), channel_id=1, source_target_pairs={{0,384},{16,400},{32,416},{48,432},{64,448},{80,464},{96,480},{112... | collective-permute-start | bytes 1179656 | tf_op jit(solution)/shard_map/ppermute | solution.py:31
  31.8 2.5 %collective-permute-start.4 = (bf16[4,128,384]{2,1,0:T(8,128)(2,1)S(1)}, bf16[4,128,384]{2,1,0:T(8,128)(2,1)S(1)}, u32[]{:S(2)}, u32[]{:S(2)}) collective-permute-start(bf16[4,128,384]{2,1,0:T(8,128)(2,1)S(1)} %pad_maximum_fusion), channel_id=1, source_target_pairs={{0,256},{16,272},{32,288},{48,304},{64,320},{80,336},{96,352},{112... | collective-permute-start | bytes 1179656 | tf_op jit(solution)/shard_map/ppermute | solution.py:31
  34.3 2.4 %collective-permute-start.3 = (bf16[4,128,384]{2,1,0:T(8,128)(2,1)S(1)}, bf16[4,128,384]{2,1,0:T(8,128)(2,1)S(1)}, u32[]{:S(2)}, u32[]{:S(2)}) collective-permute-start(bf16[4,128,384]{2,1,0:T(8,128)(2,1)S(1)} %pad_maximum_fusion), channel_id=1, source_target_pairs={{0,128},{16,144},{32,160},{48,176},{64,192},{80,208},{96,224},{112... | collective-permute-start | bytes 1179656 | tf_op jit(solution)/shard_map/ppermute | solution.py:31
  36.8 4.4 %collective-permute-done.6 = bf16[256,768]{1,0:T(8,128)(2,1)S(1)} collective-permute-done((bf16[256,768]{1,0:T(8,128)(2,1)}, bf16[256,768]{1,0:T(8,128)(2,1)S(1)}, u32[]{:S(2)}, u32[]{:S(2)}) %collective-permute-start.6) | collective-permute-done | bytes 393248 | tf_op jit(solution)/shard_map/ppermute | solution.py:27
  41.2 0.0 copy-done.2
  41.2 20.8 %collective-permute-done.7 = bf16[256,768]{1,0:T(8,128)(2,1)S(1)} collective-permute-done((bf16[256,768]{1,0:T(8,128)(2,1)}, bf16[256,768]{1,0:T(8,128)(2,1)S(1)}, u32[]{:S(2)}, u32[]{:S(2)}) %collective-permute-start.7) | collective-permute-done | bytes 393248 | tf_op jit(solution)/shard_map/ppermute | solution.py:27
  62.0 2.7 %collective-permute-start.10 = (bf16[768,768]{1,0:T(8,128)(2,1)S(1)}, bf16[768,768]{1,0:T(8,128)(2,1)S(1)}, u32[]{:S(2)}, u32[]{:S(2)}) collective-permute-start(bf16[768,768]{1,0:T(8,128)(2,1)S(1)} %constant_dynamic-update-slice_fusion.7.near), channel_id=1, source_target_pairs={{0,3},{1,0},{2,1},{3,2},{4,7},{5,4},{6,5},{7,6},{8,11},{9,8},{10,9... | collective-permute-start | bytes 3538952 | tf_op jit(solution)/shard_map/ppermute | solution.py:27
  64.8 4.3 %collective-permute-start.9 = (bf16[768,768]{1,0:T(8,128)(2,1)S(1)}, bf16[768,768]{1,0:T(8,128)(2,1)S(1)}, u32[]{:S(2)}, u32[]{:S(2)}) collective-permute-start(bf16[768,768]{1,0:T(8,128)(2,1)S(1)} %constant_dynamic-update-slice_fusion.7.near), channel_id=1, source_target_pairs={{0,1},{1,2},{2,3},{3,0},{4,5},{5,6},{6,7},{7,4},{8,9},{9,10},{10,1... | collective-permute-start | bytes 3538952 | tf_op jit(solution)/shard_map/ppermute | solution.py:27
  69.1 0.0 collective-permute-done.3
  69.1 0.1 constant_dynamic-update-slice_fusion.2
  69.2 0.0 collective-permute-done.4
  69.2 0.1 constant_dynamic-update-slice_fusion.1
  69.3 0.0 collective-permute-done.5
  69.3 0.1 constant_dynamic-update-slice_fusion.own_ref
  69.4 1.9 %collective-permute-start.8 = (bf16[16,128,384]{2,1,0:T(8,128)(2,1)S(1)}, bf16[16,128,384]{2,1,0:T(8,128)(2,1)S(1)}, u32[]{:S(2)}, u32[]{:S(2)}) collective-permute-start(bf16[16,128,384]{2,1,0:T(8,128)(2,1)S(1)} %constant_dynamic-update-slice_fusion.own_ref), channel_id=1, source_target_pairs={{0,16},{16,0},{32,48},{48,32},{64,80},{80,64},{96,112},{112,96},{1... | collective-permute-start | bytes 4718600 | tf_op jit(solution)/shard_map/ppermute | solution.py:31
  71.3 7.2 %collective-permute-start.11 = (bf16[128,768]{1,0:T(8,128)(2,1)S(1)}, bf16[128,768]{1,0:T(8,128)(2,1)S(1)}, u32[]{:S(2)}, u32[]{:S(2)}) collective-permute-start(bf16[128,768]{1,0:T(8,128)(2,1)S(1)} %slice.8), channel_id=1, source_target_pairs={{0,4},{1,5},{2,6},{3,7},{4,8},{5,9},{6,10},{7,11},{8,12},{9,13},{1... | collective-permute-start | bytes 589832 | tf_op jit(solution)/shard_map/ppermute | solution.py:27
  78.5 0.0 copy-start
  78.6 0.0 copy-start.1
  78.6 2.5 %collective-permute-start.12 = (bf16[128,768]{1,0:T(8,128)(2,1)S(1)}, bf16[128,768]{1,0:T(8,128)(2,1)S(1)}, u32[]{:S(2)}, u32[]{:S(2)}) collective-permute-start(bf16[128,768]{1,0:T(8,128)(2,1)S(1)} %slice.9), channel_id=1, source_target_pairs={{0,12},{1,13},{2,14},{3,15},{4,0},{5,1},{6,2},{7,3},{8,4},{9,5},{1... | collective-permute-start | bytes 589832 | tf_op jit(solution)/shard_map/ppermute | solution.py:27
  81.1 10.6 %collective-permute-done.11.top_ref.top = bf16[128,768]{1,0:T(8,128)(2,1)S(1)} collective-permute-done((bf16[128,768]{1,0:T(8,128)(2,1)S(1)}, bf16[128,768]{1,0:T(8,128)(2,1)S(1)}, u32[]{:S(2)}, u32[]{:S(2)}) %collective-permute-start.11) | collective-permute-done | bytes 196640 | tf_op jit(solution)/shard_map/ppermute | solution.py:27
  91.7 2.8 %collective-permute-done.12.bottom_ref.bottom = bf16[128,768]{1,0:T(8,128)(2,1)S(1)} collective-permute-done((bf16[128,768]{1,0:T(8,128)(2,1)S(1)}, bf16[128,768]{1,0:T(8,128)(2,1)S(1)}, u32[]{:S(2)}, u32[]{:S(2)}) %collective-permute-start.12) | collective-permute-done | bytes 196640 | tf_op jit(solution)/shard_map/ppermute | solution.py:27
  94.5 0.0 collective-permute-done.10.high.high_ref
  94.5 0.0 collective-permute-done.9.low.low_ref
  94.5 0.1 shard_map.48
  94.6 4.8 %collective-permute-start.13 = (bf16[640,768]{1,0:T(8,128)(2,1)S(1)}, bf16[640,768]{1,0:T(8,128)(2,1)S(1)}, u32[]{:S(2)}, u32[]{:S(2)}) collective-permute-start(bf16[640,768]{1,0:T(8,128)(2,1)S(1)} %get-tuple-element.16), channel_id=1, source_target_pairs={{0,1},{1,2},{2,3},{3,0},{4,5},{5,6},{6,7},{7,4},{8,9},{9,10},{10,1... | collective-permute-start | bytes 2949128 | tf_op jit(solution)/shard_map/ppermute | solution.py:27
  99.4 1.9 %collective-permute-start.14 = (bf16[640,768]{1,0:T(8,128)(2,1)S(1)}, bf16[640,768]{1,0:T(8,128)(2,1)S(1)}, u32[]{:S(2)}, u32[]{:S(2)}) collective-permute-start(bf16[640,768]{1,0:T(8,128)(2,1)S(1)} %get-tuple-element.17), channel_id=1, source_target_pairs={{0,3},{1,0},{2,1},{3,2},{4,7},{5,4},{6,5},{7,6},{8,11},{9,8},{10,9... | collective-permute-start | bytes 2949128 | tf_op jit(solution)/shard_map/ppermute | solution.py:27
  101.4 0.0 copy-done
  101.4 1.2 shard_map.46.weights_ref
  102.6 0.0 collective-permute-done.8.core_ref
  102.6 7.7 %shard_map.47 = (bf16[32,128,384]{2,1,0:T(8,128)(2,1)S(1)}, f32[3,128,128]{2,1,0:T(8,128)S(1)}, f32[768,512]{1,0:T(8,128)S(1)}) custom-call(s32[32]{0:T(128)S(1)} %copy-done.1, bf16[16,128,384]{2,1,0:T(8,128)(2,1)S(1)} %constant_dynamic-update-slice_fusion.own_ref, bf16[16,128,384]{2,1,0:T(8,128)(2,1)S(1)} %collective-permute-done.8.core_ref, ...), custom_call_target="tpu_custom_call" | custom-call | flops 4600000000 | tf_op jit(solution)/shard_map/pallas_call | solution.py:282
  110.3 10.0 %collective-permute-done.13.low_ref.far_low = bf16[640,768]{1,0:T(8,128)(2,1)S(1)} collective-permute-done((bf16[640,768]{1,0:T(8,128)(2,1)S(1)}, bf16[640,768]{1,0:T(8,128)(2,1)S(1)}, u32[]{:S(2)}, u32[]{:S(2)}) %collective-permute-start.13) | collective-permute-done | bytes 983072 | tf_op jit(solution)/shard_map/ppermute | solution.py:27
  120.2 4.0 %collective-permute-done.14.high_ref.far_high = bf16[640,768]{1,0:T(8,128)(2,1)S(1)} collective-permute-done((bf16[640,768]{1,0:T(8,128)(2,1)S(1)}, bf16[640,768]{1,0:T(8,128)(2,1)S(1)}, u32[]{:S(2)}, u32[]{:S(2)}) %collective-permute-start.14) | collective-permute-done | bytes 983072 | tf_op jit(solution)/shard_map/ppermute | solution.py:27
  124.3 1.9 %collective-permute-start.15 = (bf16[128,768]{1,0:T(8,128)(2,1)S(1)}, bf16[128,768]{1,0:T(8,128)(2,1)S(1)}, u32[]{:S(2)}, u32[]{:S(2)}) collective-permute-start(bf16[128,768]{1,0:T(8,128)(2,1)S(1)} %get-tuple-element.18), channel_id=1, source_target_pairs={{0,1},{1,2},{2,3},{3,0},{4,5},{5,6},{6,7},{7,4},{8,9},{9,10},{10,1... | collective-permute-start | bytes 589832 | tf_op jit(solution)/shard_map/ppermute | solution.py:27
  126.2 4.1 %collective-permute-start.16 = (bf16[128,768]{1,0:T(8,128)(2,1)S(1)}, bf16[128,768]{1,0:T(8,128)(2,1)S(1)}, u32[]{:S(2)}, u32[]{:S(2)}) collective-permute-start(bf16[128,768]{1,0:T(8,128)(2,1)S(1)} %get-tuple-element.19), channel_id=1, source_target_pairs={{0,3},{1,0},{2,1},{3,2},{4,7},{5,4},{6,5},{7,6},{8,11},{9,8},{10,9... | collective-permute-start | bytes 589832 | tf_op jit(solution)/shard_map/ppermute | solution.py:27
  130.3 2.2 %shard_map.50.before = f32[768,512]{1,0:T(8,128)S(1)} custom-call(bf16[32,128,384]{2,1,0:T(8,128)(2,1)S(1)} %get-tuple-element.14.acts_ref, bf16[32,128,128]{2,1,0:T(8,128)(2,1)S(1)} %shard_map.46.weights_ref, bf16[640,768]{1,0:T(8,128)(2,1)S(1)} %collective-permute-done.13.low_ref.far_low, bf16[640,768]{1,0:T(8,128)(2,1)S(1)} %collective-permute-done.14.high_ref.far_high, ...), custom_call_target="tpu_custom_call" | custom-call | flops 2300000000 | tf_op jit(solution)/shard_map/pallas_call | solution.py:282
  132.5 0.0 collective-permute-done.15.far_low
  132.5 2.5 %collective-permute-done.16.far_high = bf16[128,768]{1,0:T(8,128)(2,1)S(1)} collective-permute-done((bf16[128,768]{1,0:T(8,128)(2,1)S(1)}, bf16[128,768]{1,0:T(8,128)(2,1)S(1)}, u32[]{:S(2)}, u32[]{:S(2)}) %collective-permute-start.16) | collective-permute-done | bytes 196640 | tf_op jit(solution)/shard_map/ppermute | solution.py:27
  135.0 5.7 %shard_map.51 = bf16[384,768]{1,0:T(8,128)(2,1)} custom-call(s32[32]{0:T(128)S(1)} %copy-done.1, bf16[32,128,384]{2,1,0:T(8,128)(2,1)S(1)} %get-tuple-element.14.acts_ref, bf16[32,128,128]{2,1,0:T(8,128)(2,1)S(1)} %shard_map.46.weights_ref, f32[3,128,128]{2,1,0:T(8,128)S(1)} %get-tuple-element.15.inv_ref, ...), custom_call_target="tpu_custom_call" | custom-call | flops 11500000256 | tf_op jit(solution)/shard_map/pallas_call | solution.py:282
  (11 shorter events, 0.2 us)
Async XLA Ops:
  0.0 41.2 %copy-start.2 = (bf16[256,768]{1,0:T(8,128)(2,1)S(1)}, bf16[256,768]{1,0:T(8,128)(2,1)}, u32[]{:S(2)}) copy-start(bf16[256,768]{1,0:T(8,128)(2,1)} %param.5) | copy-start | bytes 1179652
  0.0 25.8 %collective-permute-start.2 = (bf16[1,128,384]{2,1,0:T(8,128)(2,1)}, bf16[1,128,384]{2,1,0:T(8,128)(2,1)S(1)}, u32[]{:S(2)}, u32[]{:S(2)}) collective-permute-start(bf16[1,128,384]{2,1,0:T(8,128)(2,1)} %bitcast.4), channel_id=1, source_target_pairs={{0,96},{16,112},{32,64},{48,80},{64,32},{80,48},{96,0},{112,16},{1... | collective-permute-start | bytes 294920 | tf_op jit(solution)/shard_map/ppermute | solution.py:31
  6.7 19.2 %collective-permute-start.1 = (bf16[1,128,384]{2,1,0:T(8,128)(2,1)}, bf16[1,128,384]{2,1,0:T(8,128)(2,1)S(1)}, u32[]{:S(2)}, u32[]{:S(2)}) collective-permute-start(bf16[1,128,384]{2,1,0:T(8,128)(2,1)} %bitcast.5), channel_id=1, source_target_pairs={{0,64},{16,80},{32,96},{48,112},{64,0},{80,16},{96,32},{112,48},{1... | collective-permute-start | bytes 294920 | tf_op jit(solution)/shard_map/ppermute | solution.py:31
  8.6 17.3 %collective-permute-start = (bf16[1,128,384]{2,1,0:T(8,128)(2,1)}, bf16[1,128,384]{2,1,0:T(8,128)(2,1)S(1)}, u32[]{:S(2)}, u32[]{:S(2)}) collective-permute-start(bf16[1,128,384]{2,1,0:T(8,128)(2,1)} %bitcast.6), channel_id=1, source_target_pairs={{0,32},{16,48},{32,0},{48,16},{64,96},{80,112},{96,64},{112,80},{1... | collective-permute-start | bytes 294920 | tf_op jit(solution)/shard_map/ppermute | solution.py:31
  11.1 30.1 %collective-permute-start.6 = (bf16[256,768]{1,0:T(8,128)(2,1)}, bf16[256,768]{1,0:T(8,128)(2,1)S(1)}, u32[]{:S(2)}, u32[]{:S(2)}) collective-permute-start(bf16[256,768]{1,0:T(8,128)(2,1)} %param.5), channel_id=1, source_target_pairs={{0,4},{1,5},{2,6},{3,7},{4,8},{5,9},{6,10},{7,11},{8,12},{9,13},{1... | collective-permute-start | bytes 1179656 | tf_op jit(solution)/shard_map/ppermute | solution.py:27
  20.2 41.8 %collective-permute-start.7 = (bf16[256,768]{1,0:T(8,128)(2,1)}, bf16[256,768]{1,0:T(8,128)(2,1)S(1)}, u32[]{:S(2)}, u32[]{:S(2)}) collective-permute-start(bf16[256,768]{1,0:T(8,128)(2,1)} %param.5), channel_id=1, source_target_pairs={{0,12},{1,13},{2,14},{3,15},{4,0},{5,1},{6,2},{7,3},{8,4},{9,5},{1... | collective-permute-start | bytes 1179656 | tf_op jit(solution)/shard_map/ppermute | solution.py:27
  26.8 42.4 %collective-permute-start.5 = (bf16[4,128,384]{2,1,0:T(8,128)(2,1)S(1)}, bf16[4,128,384]{2,1,0:T(8,128)(2,1)S(1)}, u32[]{:S(2)}, u32[]{:S(2)}) collective-permute-start(bf16[4,128,384]{2,1,0:T(8,128)(2,1)S(1)} %pad_maximum_fusion), channel_id=1, source_target_pairs={{0,384},{16,400},{32,416},{48,432},{64,448},{80,464},{96,480},{112... | collective-permute-start | bytes 1179656 | tf_op jit(solution)/shard_map/ppermute | solution.py:31
  31.8 37.4 %collective-permute-start.4 = (bf16[4,128,384]{2,1,0:T(8,128)(2,1)S(1)}, bf16[4,128,384]{2,1,0:T(8,128)(2,1)S(1)}, u32[]{:S(2)}, u32[]{:S(2)}) collective-permute-start(bf16[4,128,384]{2,1,0:T(8,128)(2,1)S(1)} %pad_maximum_fusion), channel_id=1, source_target_pairs={{0,256},{16,272},{32,288},{48,304},{64,320},{80,336},{96,352},{112... | collective-permute-start | bytes 1179656 | tf_op jit(solution)/shard_map/ppermute | solution.py:31
  34.3 34.8 %collective-permute-start.3 = (bf16[4,128,384]{2,1,0:T(8,128)(2,1)S(1)}, bf16[4,128,384]{2,1,0:T(8,128)(2,1)S(1)}, u32[]{:S(2)}, u32[]{:S(2)}) collective-permute-start(bf16[4,128,384]{2,1,0:T(8,128)(2,1)S(1)} %pad_maximum_fusion), channel_id=1, source_target_pairs={{0,128},{16,144},{32,160},{48,176},{64,192},{80,208},{96,224},{112... | collective-permute-start | bytes 1179656 | tf_op jit(solution)/shard_map/ppermute | solution.py:31
  62.0 32.5 %collective-permute-start.10 = (bf16[768,768]{1,0:T(8,128)(2,1)S(1)}, bf16[768,768]{1,0:T(8,128)(2,1)S(1)}, u32[]{:S(2)}, u32[]{:S(2)}) collective-permute-start(bf16[768,768]{1,0:T(8,128)(2,1)S(1)} %constant_dynamic-update-slice_fusion.7.near), channel_id=1, source_target_pairs={{0,3},{1,0},{2,1},{3,2},{4,7},{5,4},{6,5},{7,6},{8,11},{9,8},{10,9... | collective-permute-start | bytes 3538952 | tf_op jit(solution)/shard_map/ppermute | solution.py:27
  64.8 29.7 %collective-permute-start.9 = (bf16[768,768]{1,0:T(8,128)(2,1)S(1)}, bf16[768,768]{1,0:T(8,128)(2,1)S(1)}, u32[]{:S(2)}, u32[]{:S(2)}) collective-permute-start(bf16[768,768]{1,0:T(8,128)(2,1)S(1)} %constant_dynamic-update-slice_fusion.7.near), channel_id=1, source_target_pairs={{0,1},{1,2},{2,3},{3,0},{4,5},{5,6},{6,7},{7,4},{8,9},{9,10},{10,1... | collective-permute-start | bytes 3538952 | tf_op jit(solution)/shard_map/ppermute | solution.py:27
  69.4 33.2 %collective-permute-start.8 = (bf16[16,128,384]{2,1,0:T(8,128)(2,1)S(1)}, bf16[16,128,384]{2,1,0:T(8,128)(2,1)S(1)}, u32[]{:S(2)}, u32[]{:S(2)}) collective-permute-start(bf16[16,128,384]{2,1,0:T(8,128)(2,1)S(1)} %constant_dynamic-update-slice_fusion.own_ref), channel_id=1, source_target_pairs={{0,16},{16,0},{32,48},{48,32},{64,80},{80,64},{96,112},{112,96},{1... | collective-permute-start | bytes 4718600 | tf_op jit(solution)/shard_map/ppermute | solution.py:31
  71.3 20.4 %collective-permute-start.11 = (bf16[128,768]{1,0:T(8,128)(2,1)S(1)}, bf16[128,768]{1,0:T(8,128)(2,1)S(1)}, u32[]{:S(2)}, u32[]{:S(2)}) collective-permute-start(bf16[128,768]{1,0:T(8,128)(2,1)S(1)} %slice.8), channel_id=1, source_target_pairs={{0,4},{1,5},{2,6},{3,7},{4,8},{5,9},{6,10},{7,11},{8,12},{9,13},{1... | collective-permute-start | bytes 589832 | tf_op jit(solution)/shard_map/ppermute | solution.py:27
  78.5 22.8 %copy-start = (s32[4096]{0:T(1024)S(1)}, s32[4096]{0:T(1024)}, u32[]{:S(2)}) copy-start(s32[4096]{0:T(1024)} %param.6) | copy-start | bytes 49156
  78.6 22.8 %copy-start.1 = (s32[32]{0:T(128)S(1)}, s32[32]{0:T(128)}, u32[]{:S(2)}) copy-start(s32[32]{0:T(128)} %tokens_ref.5) | copy-start | bytes 388
  78.6 15.9 %collective-permute-start.12 = (bf16[128,768]{1,0:T(8,128)(2,1)S(1)}, bf16[128,768]{1,0:T(8,128)(2,1)S(1)}, u32[]{:S(2)}, u32[]{:S(2)}) collective-permute-start(bf16[128,768]{1,0:T(8,128)(2,1)S(1)} %slice.9), channel_id=1, source_target_pairs={{0,12},{1,13},{2,14},{3,15},{4,0},{5,1},{6,2},{7,3},{8,4},{9,5},{1... | collective-permute-start | bytes 589832 | tf_op jit(solution)/shard_map/ppermute | solution.py:27
  94.6 25.6 %collective-permute-start.13 = (bf16[640,768]{1,0:T(8,128)(2,1)S(1)}, bf16[640,768]{1,0:T(8,128)(2,1)S(1)}, u32[]{:S(2)}, u32[]{:S(2)}) collective-permute-start(bf16[640,768]{1,0:T(8,128)(2,1)S(1)} %get-tuple-element.16), channel_id=1, source_target_pairs={{0,1},{1,2},{2,3},{3,0},{4,5},{5,6},{6,7},{7,4},{8,9},{9,10},{10,1... | collective-permute-start | bytes 2949128 | tf_op jit(solution)/shard_map/ppermute | solution.py:27
  99.4 24.8 %collective-permute-start.14 = (bf16[640,768]{1,0:T(8,128)(2,1)S(1)}, bf16[640,768]{1,0:T(8,128)(2,1)S(1)}, u32[]{:S(2)}, u32[]{:S(2)}) collective-permute-start(bf16[640,768]{1,0:T(8,128)(2,1)S(1)} %get-tuple-element.17), channel_id=1, source_target_pairs={{0,3},{1,0},{2,1},{3,2},{4,7},{5,4},{6,5},{7,6},{8,11},{9,8},{10,9... | collective-permute-start | bytes 2949128 | tf_op jit(solution)/shard_map/ppermute | solution.py:27
  124.3 8.2 %collective-permute-start.15 = (bf16[128,768]{1,0:T(8,128)(2,1)S(1)}, bf16[128,768]{1,0:T(8,128)(2,1)S(1)}, u32[]{:S(2)}, u32[]{:S(2)}) collective-permute-start(bf16[128,768]{1,0:T(8,128)(2,1)S(1)} %get-tuple-element.18), channel_id=1, source_target_pairs={{0,1},{1,2},{2,3},{3,0},{4,5},{5,6},{6,7},{7,4},{8,9},{9,10},{10,1... | collective-permute-start | bytes 589832 | tf_op jit(solution)/shard_map/ppermute | solution.py:27
  126.2 8.8 %collective-permute-start.16 = (bf16[128,768]{1,0:T(8,128)(2,1)S(1)}, bf16[128,768]{1,0:T(8,128)(2,1)S(1)}, u32[]{:S(2)}, u32[]{:S(2)}) collective-permute-start(bf16[128,768]{1,0:T(8,128)(2,1)S(1)} %get-tuple-element.19), channel_id=1, source_target_pairs={{0,3},{1,0},{2,1},{3,2},{4,7},{5,4},{6,5},{7,6},{8,11},{9,8},{10,9... | collective-permute-start | bytes 589832 | tf_op jit(solution)/shard_map/ppermute | solution.py:27

commit v6 on v5

--- a/solution.py
+++ b/solution.py
@@ -8,7 +8,7 @@
 BLK = 128
 TOK_DEV = 128
 DAMPING = 0.001
-VMEM_LIMIT = 40 * 1024 * 1024
+VMEM_LIMIT = 28 * 1024 * 1024
 
 
 def shift_x(step):

time: 142 us -> 142 us (level)
  no operation moved by 1% of the time
where the time goes in v6:
time: 142 us; the launch traced here: 141 us
  starting transfers between devices  66.2 us (47%)
  waiting for transfers between devices  55 us (39%)
  Pallas kernels  16.8 us (12%)
    ppermute x10, waiting for transfers between devices, hop(): return lax.ppermute(value, 'inv', pairs)  55 us
    ppermute x10, starting transfers between devices, hop(): return lax.ppermute(value, 'inv', pairs)  43.4 us
    ppermute x7, starting transfers between devices, swap(): return lax.ppermute(value, 'dp', flip_dp(mask))  22.8 us
    pallas_call x6, Pallas kernels, call(): pl.pallas_call(kernel, out_shape=shapes, in_specs=[pl.BlockSpec(memory_sp...  16.8 us
  transfers between devices with their start and end apart: 17, of which 7 were waited for; matrix products, arithmetic and copies ran while one was open for 2% of the time, Pallas kernels for 8%

profile of v6, /device:TPU:6, one launch (start us, length us, event | category | flops | bytes accessed | tf_op | source)
XLA Modules:
  0.0 140.6 jit_solution(9113764082126207786)
XLA Ops:
  0.0 6.7 %collective-permute-start.2 = (bf16[1,128,384]{2,1,0:T(8,128)(2,1)}, bf16[1,128,384]{2,1,0:T(8,128)(2,1)S(1)}, u32[]{:S(2)}, u32[]{:S(2)}) collective-permute-start(bf16[1,128,384]{2,1,0:T(8,128)(2,1)} %bitcast.4), channel_id=1, source_target_pairs={{0,96},{16,112},{32,64},{48,80},{64,32},{80,48},{96,0},{112,16},{1... | collective-permute-start | bytes 294920 | tf_op jit(solution)/shard_map/ppermute | solution.py:31
  6.7 1.9 %collective-permute-start.1 = (bf16[1,128,384]{2,1,0:T(8,128)(2,1)}, bf16[1,128,384]{2,1,0:T(8,128)(2,1)S(1)}, u32[]{:S(2)}, u32[]{:S(2)}) collective-permute-start(bf16[1,128,384]{2,1,0:T(8,128)(2,1)} %bitcast.5), channel_id=1, source_target_pairs={{0,64},{16,80},{32,96},{48,112},{64,0},{80,16},{96,32},{112,48},{1... | collective-permute-start | bytes 294920 | tf_op jit(solution)/shard_map/ppermute | solution.py:31
  8.6 2.5 %collective-permute-start = (bf16[1,128,384]{2,1,0:T(8,128)(2,1)}, bf16[1,128,384]{2,1,0:T(8,128)(2,1)S(1)}, u32[]{:S(2)}, u32[]{:S(2)}) collective-permute-start(bf16[1,128,384]{2,1,0:T(8,128)(2,1)} %bitcast.6), channel_id=1, source_target_pairs={{0,32},{16,48},{32,0},{48,16},{64,96},{80,112},{96,64},{112,80},{1... | collective-permute-start | bytes 294920 | tf_op jit(solution)/shard_map/ppermute | solution.py:31
  11.1 9.1 %collective-permute-start.6 = (bf16[256,768]{1,0:T(8,128)(2,1)}, bf16[256,768]{1,0:T(8,128)(2,1)S(1)}, u32[]{:S(2)}, u32[]{:S(2)}) collective-permute-start(bf16[256,768]{1,0:T(8,128)(2,1)} %param.5), channel_id=1, source_target_pairs={{0,4},{1,5},{2,6},{3,7},{4,8},{5,9},{6,10},{7,11},{8,12},{9,13},{1... | collective-permute-start | bytes 1179656 | tf_op jit(solution)/shard_map/ppermute | solution.py:27
  20.2 4.7 %collective-permute-start.7 = (bf16[256,768]{1,0:T(8,128)(2,1)}, bf16[256,768]{1,0:T(8,128)(2,1)S(1)}, u32[]{:S(2)}, u32[]{:S(2)}) collective-permute-start(bf16[256,768]{1,0:T(8,128)(2,1)} %param.5), channel_id=1, source_target_pairs={{0,12},{1,13},{2,14},{3,15},{4,0},{5,1},{6,2},{7,3},{8,4},{9,5},{1... | collective-permute-start | bytes 1179656 | tf_op jit(solution)/shard_map/ppermute | solution.py:27
  24.9 0.9 constant_dynamic-update-slice_fusion.6
  25.8 0.0 collective-permute-done.2
  25.9 0.0 collective-permute-done.1
  25.9 0.0 collective-permute-done
  25.9 1.0 pad_maximum_fusion
  26.8 4.9 %collective-permute-start.5 = (bf16[4,128,384]{2,1,0:T(8,128)(2,1)S(1)}, bf16[4,128,384]{2,1,0:T(8,128)(2,1)S(1)}, u32[]{:S(2)}, u32[]{:S(2)}) collective-permute-start(bf16[4,128,384]{2,1,0:T(8,128)(2,1)S(1)} %pad_maximum_fusion), channel_id=1, source_target_pairs={{0,384},{16,400},{32,416},{48,432},{64,448},{80,464},{96,480},{112... | collective-permute-start | bytes 1179656 | tf_op jit(solution)/shard_map/ppermute | solution.py:31
  31.8 2.5 %collective-permute-start.4 = (bf16[4,128,384]{2,1,0:T(8,128)(2,1)S(1)}, bf16[4,128,384]{2,1,0:T(8,128)(2,1)S(1)}, u32[]{:S(2)}, u32[]{:S(2)}) collective-permute-start(bf16[4,128,384]{2,1,0:T(8,128)(2,1)S(1)} %pad_maximum_fusion), channel_id=1, source_target_pairs={{0,256},{16,272},{32,288},{48,304},{64,320},{80,336},{96,352},{112... | collective-permute-start | bytes 1179656 | tf_op jit(solution)/shard_map/ppermute | solution.py:31
  34.3 2.4 %collective-permute-start.3 = (bf16[4,128,384]{2,1,0:T(8,128)(2,1)S(1)}, bf16[4,128,384]{2,1,0:T(8,128)(2,1)S(1)}, u32[]{:S(2)}, u32[]{:S(2)}) collective-permute-start(bf16[4,128,384]{2,1,0:T(8,128)(2,1)S(1)} %pad_maximum_fusion), channel_id=1, source_target_pairs={{0,128},{16,144},{32,160},{48,176},{64,192},{80,208},{96,224},{112... | collective-permute-start | bytes 1179656 | tf_op jit(solution)/shard_map/ppermute | solution.py:31
  36.8 4.4 %collective-permute-done.6 = bf16[256,768]{1,0:T(8,128)(2,1)S(1)} collective-permute-done((bf16[256,768]{1,0:T(8,128)(2,1)}, bf16[256,768]{1,0:T(8,128)(2,1)S(1)}, u32[]{:S(2)}, u32[]{:S(2)}) %collective-permute-start.6) | collective-permute-done | bytes 393248 | tf_op jit(solution)/shard_map/ppermute | solution.py:27
  41.2 0.0 copy-done.2
  41.2 20.8 %collective-permute-done.7 = bf16[256,768]{1,0:T(8,128)(2,1)S(1)} collective-permute-done((bf16[256,768]{1,0:T(8,128)(2,1)}, bf16[256,768]{1,0:T(8,128)(2,1)S(1)}, u32[]{:S(2)}, u32[]{:S(2)}) %collective-permute-start.7) | collective-permute-done | bytes 393248 | tf_op jit(solution)/shard_map/ppermute | solution.py:27
  62.0 2.7 %collective-permute-start.10 = (bf16[768,768]{1,0:T(8,128)(2,1)S(1)}, bf16[768,768]{1,0:T(8,128)(2,1)S(1)}, u32[]{:S(2)}, u32[]{:S(2)}) collective-permute-start(bf16[768,768]{1,0:T(8,128)(2,1)S(1)} %constant_dynamic-update-slice_fusion.7.near), channel_id=1, source_target_pairs={{0,3},{1,0},{2,1},{3,2},{4,7},{5,4},{6,5},{7,6},{8,11},{9,8},{10,9... | collective-permute-start | bytes 3538952 | tf_op jit(solution)/shard_map/ppermute | solution.py:27
  64.8 4.3 %collective-permute-start.9 = (bf16[768,768]{1,0:T(8,128)(2,1)S(1)}, bf16[768,768]{1,0:T(8,128)(2,1)S(1)}, u32[]{:S(2)}, u32[]{:S(2)}) collective-permute-start(bf16[768,768]{1,0:T(8,128)(2,1)S(1)} %constant_dynamic-update-slice_fusion.7.near), channel_id=1, source_target_pairs={{0,1},{1,2},{2,3},{3,0},{4,5},{5,6},{6,7},{7,4},{8,9},{9,10},{10,1... | collective-permute-start | bytes 3538952 | tf_op jit(solution)/shard_map/ppermute | solution.py:27
  69.1 0.0 collective-permute-done.3
  69.1 0.1 constant_dynamic-update-slice_fusion.2
  69.2 0.0 collective-permute-done.4
  69.2 0.1 constant_dynamic-update-slice_fusion.1
  69.3 0.0 collective-permute-done.5
  69.3 0.1 constant_dynamic-update-slice_fusion.own_ref
  69.4 1.9 %collective-permute-start.8 = (bf16[16,128,384]{2,1,0:T(8,128)(2,1)S(1)}, bf16[16,128,384]{2,1,0:T(8,128)(2,1)S(1)}, u32[]{:S(2)}, u32[]{:S(2)}) collective-permute-start(bf16[16,128,384]{2,1,0:T(8,128)(2,1)S(1)} %constant_dynamic-update-slice_fusion.own_ref), channel_id=1, source_target_pairs={{0,16},{16,0},{32,48},{48,32},{64,80},{80,64},{96,112},{112,96},{1... | collective-permute-start | bytes 4718600 | tf_op jit(solution)/shard_map/ppermute | solution.py:31
  71.3 7.2 %collective-permute-start.11 = (bf16[128,768]{1,0:T(8,128)(2,1)S(1)}, bf16[128,768]{1,0:T(8,128)(2,1)S(1)}, u32[]{:S(2)}, u32[]{:S(2)}) collective-permute-start(bf16[128,768]{1,0:T(8,128)(2,1)S(1)} %slice.8), channel_id=1, source_target_pairs={{0,4},{1,5},{2,6},{3,7},{4,8},{5,9},{6,10},{7,11},{8,12},{9,13},{1... | collective-permute-start | bytes 589832 | tf_op jit(solution)/shard_map/ppermute | solution.py:27
  78.5 0.0 copy-start
  78.6 0.0 copy-start.1
  78.6 2.5 %collective-permute-start.12 = (bf16[128,768]{1,0:T(8,128)(2,1)S(1)}, bf16[128,768]{1,0:T(8,128)(2,1)S(1)}, u32[]{:S(2)}, u32[]{:S(2)}) collective-permute-start(bf16[128,768]{1,0:T(8,128)(2,1)S(1)} %slice.9), channel_id=1, source_target_pairs={{0,12},{1,13},{2,14},{3,15},{4,0},{5,1},{6,2},{7,3},{8,4},{9,5},{1... | collective-permute-start | bytes 589832 | tf_op jit(solution)/shard_map/ppermute | solution.py:27
  81.1 10.6 %collective-permute-done.11.top_ref.top = bf16[128,768]{1,0:T(8,128)(2,1)S(1)} collective-permute-done((bf16[128,768]{1,0:T(8,128)(2,1)S(1)}, bf16[128,768]{1,0:T(8,128)(2,1)S(1)}, u32[]{:S(2)}, u32[]{:S(2)}) %collective-permute-start.11) | collective-permute-done | bytes 196640 | tf_op jit(solution)/shard_map/ppermute | solution.py:27
  91.7 2.8 %collective-permute-done.12.bottom_ref.bottom = bf16[128,768]{1,0:T(8,128)(2,1)S(1)} collective-permute-done((bf16[128,768]{1,0:T(8,128)(2,1)S(1)}, bf16[128,768]{1,0:T(8,128)(2,1)S(1)}, u32[]{:S(2)}, u32[]{:S(2)}) %collective-permute-start.12) | collective-permute-done | bytes 196640 | tf_op jit(solution)/shard_map/ppermute | solution.py:27
  94.5 0.0 collective-permute-done.10.high.high_ref
  94.5 0.0 collective-permute-done.9.low.low_ref
  94.5 0.1 shard_map.48
  94.6 4.8 %collective-permute-start.13 = (bf16[640,768]{1,0:T(8,128)(2,1)S(1)}, bf16[640,768]{1,0:T(8,128)(2,1)S(1)}, u32[]{:S(2)}, u32[]{:S(2)}) collective-permute-start(bf16[640,768]{1,0:T(8,128)(2,1)S(1)} %get-tuple-element.16), channel_id=1, source_target_pairs={{0,1},{1,2},{2,3},{3,0},{4,5},{5,6},{6,7},{7,4},{8,9},{9,10},{10,1... | collective-permute-start | bytes 2949128 | tf_op jit(solution)/shard_map/ppermute | solution.py:27
  99.4 1.9 %collective-permute-start.14 = (bf16[640,768]{1,0:T(8,128)(2,1)S(1)}, bf16[640,768]{1,0:T(8,128)(2,1)S(1)}, u32[]{:S(2)}, u32[]{:S(2)}) collective-permute-start(bf16[640,768]{1,0:T(8,128)(2,1)S(1)} %get-tuple-element.17), channel_id=1, source_target_pairs={{0,3},{1,0},{2,1},{3,2},{4,7},{5,4},{6,5},{7,6},{8,11},{9,8},{10,9... | collective-permute-start | bytes 2949128 | tf_op jit(solution)/shard_map/ppermute | solution.py:27
  101.4 0.0 copy-done
  101.4 1.2 shard_map.46.weights_ref
  102.6 0.0 collective-permute-done.8.core_ref
  102.6 7.7 %shard_map.47 = (bf16[32,128,384]{2,1,0:T(8,128)(2,1)S(1)}, f32[3,128,128]{2,1,0:T(8,128)S(1)}, f32[768,512]{1,0:T(8,128)S(1)}) custom-call(s32[32]{0:T(128)S(1)} %copy-done.1, bf16[16,128,384]{2,1,0:T(8,128)(2,1)S(1)} %constant_dynamic-update-slice_fusion.own_ref, bf16[16,128,384]{2,1,0:T(8,128)(2,1)S(1)} %collective-permute-done.8.core_ref, ...), custom_call_target="tpu_custom_call" | custom-call | flops 4600000000 | tf_op jit(solution)/shard_map/pallas_call | solution.py:282
  110.3 10.0 %collective-permute-done.13.low_ref.far_low = bf16[640,768]{1,0:T(8,128)(2,1)S(1)} collective-permute-done((bf16[640,768]{1,0:T(8,128)(2,1)S(1)}, bf16[640,768]{1,0:T(8,128)(2,1)S(1)}, u32[]{:S(2)}, u32[]{:S(2)}) %collective-permute-start.13) | collective-permute-done | bytes 983072 | tf_op jit(solution)/shard_map/ppermute | solution.py:27
  120.2 4.0 %collective-permute-done.14.high_ref.far_high = bf16[640,768]{1,0:T(8,128)(2,1)S(1)} collective-permute-done((bf16[640,768]{1,0:T(8,128)(2,1)S(1)}, bf16[640,768]{1,0:T(8,128)(2,1)S(1)}, u32[]{:S(2)}, u32[]{:S(2)}) %collective-permute-start.14) | collective-permute-done | bytes 983072 | tf_op jit(solution)/shard_map/ppermute | solution.py:27
  124.3 1.9 %collective-permute-start.15 = (bf16[128,768]{1,0:T(8,128)(2,1)S(1)}, bf16[128,768]{1,0:T(8,128)(2,1)S(1)}, u32[]{:S(2)}, u32[]{:S(2)}) collective-permute-start(bf16[128,768]{1,0:T(8,128)(2,1)S(1)} %get-tuple-element.18), channel_id=1, source_target_pairs={{0,1},{1,2},{2,3},{3,0},{4,5},{5,6},{6,7},{7,4},{8,9},{9,10},{10,1... | collective-permute-start | bytes 589832 | tf_op jit(solution)/shard_map/ppermute | solution.py:27
  126.2 4.1 %collective-permute-start.16 = (bf16[128,768]{1,0:T(8,128)(2,1)S(1)}, bf16[128,768]{1,0:T(8,128)(2,1)S(1)}, u32[]{:S(2)}, u32[]{:S(2)}) collective-permute-start(bf16[128,768]{1,0:T(8,128)(2,1)S(1)} %get-tuple-element.19), channel_id=1, source_target_pairs={{0,3},{1,0},{2,1},{3,2},{4,7},{5,4},{6,5},{7,6},{8,11},{9,8},{10,9... | collective-permute-start | bytes 589832 | tf_op jit(solution)/shard_map/ppermute | solution.py:27
  130.3 2.2 %shard_map.50.before = f32[768,512]{1,0:T(8,128)S(1)} custom-call(bf16[32,128,384]{2,1,0:T(8,128)(2,1)S(1)} %get-tuple-element.14.acts_ref, bf16[32,128,128]{2,1,0:T(8,128)(2,1)S(1)} %shard_map.46.weights_ref, bf16[640,768]{1,0:T(8,128)(2,1)S(1)} %collective-permute-done.13.low_ref.far_low, bf16[640,768]{1,0:T(8,128)(2,1)S(1)} %collective-permute-done.14.high_ref.far_high, ...), custom_call_target="tpu_custom_call" | custom-call | flops 2300000000 | tf_op jit(solution)/shard_map/pallas_call | solution.py:282
  132.5 0.0 collective-permute-done.15.far_low
  132.5 2.5 %collective-permute-done.16.far_high = bf16[128,768]{1,0:T(8,128)(2,1)S(1)} collective-permute-done((bf16[128,768]{1,0:T(8,128)(2,1)S(1)}, bf16[128,768]{1,0:T(8,128)(2,1)S(1)}, u32[]{:S(2)}, u32[]{:S(2)}) %collective-permute-start.16) | collective-permute-done | bytes 196640 | tf_op jit(solution)/shard_map/ppermute | solution.py:27
  135.0 5.7 %shard_map.51 = bf16[384,768]{1,0:T(8,128)(2,1)} custom-call(s32[32]{0:T(128)S(1)} %copy-done.1, bf16[32,128,384]{2,1,0:T(8,128)(2,1)S(1)} %get-tuple-element.14.acts_ref, bf16[32,128,128]{2,1,0:T(8,128)(2,1)S(1)} %shard_map.46.weights_ref, f32[3,128,128]{2,1,0:T(8,128)S(1)} %get-tuple-element.15.inv_ref, ...), custom_call_target="tpu_custom_call" | custom-call | flops 11500000256 | tf_op jit(solution)/shard_map/pallas_call | solution.py:282
  (11 shorter events, 0.2 us)
Async XLA Ops:
  0.0 41.2 %copy-start.2 = (bf16[256,768]{1,0:T(8,128)(2,1)S(1)}, bf16[256,768]{1,0:T(8,128)(2,1)}, u32[]{:S(2)}) copy-start(bf16[256,768]{1,0:T(8,128)(2,1)} %param.5) | copy-start | bytes 1179652
  0.0 25.8 %collective-permute-start.2 = (bf16[1,128,384]{2,1,0:T(8,128)(2,1)}, bf16[1,128,384]{2,1,0:T(8,128)(2,1)S(1)}, u32[]{:S(2)}, u32[]{:S(2)}) collective-permute-start(bf16[1,128,384]{2,1,0:T(8,128)(2,1)} %bitcast.4), channel_id=1, source_target_pairs={{0,96},{16,112},{32,64},{48,80},{64,32},{80,48},{96,0},{112,16},{1... | collective-permute-start | bytes 294920 | tf_op jit(solution)/shard_map/ppermute | solution.py:31
  6.7 19.2 %collective-permute-start.1 = (bf16[1,128,384]{2,1,0:T(8,128)(2,1)}, bf16[1,128,384]{2,1,0:T(8,128)(2,1)S(1)}, u32[]{:S(2)}, u32[]{:S(2)}) collective-permute-start(bf16[1,128,384]{2,1,0:T(8,128)(2,1)} %bitcast.5), channel_id=1, source_target_pairs={{0,64},{16,80},{32,96},{48,112},{64,0},{80,16},{96,32},{112,48},{1... | collective-permute-start | bytes 294920 | tf_op jit(solution)/shard_map/ppermute | solution.py:31
  8.6 17.3 %collective-permute-start = (bf16[1,128,384]{2,1,0:T(8,128)(2,1)}, bf16[1,128,384]{2,1,0:T(8,128)(2,1)S(1)}, u32[]{:S(2)}, u32[]{:S(2)}) collective-permute-start(bf16[1,128,384]{2,1,0:T(8,128)(2,1)} %bitcast.6), channel_id=1, source_target_pairs={{0,32},{16,48},{32,0},{48,16},{64,96},{80,112},{96,64},{112,80},{1... | collective-permute-start | bytes 294920 | tf_op jit(solution)/shard_map/ppermute | solution.py:31
  11.1 30.1 %collective-permute-start.6 = (bf16[256,768]{1,0:T(8,128)(2,1)}, bf16[256,768]{1,0:T(8,128)(2,1)S(1)}, u32[]{:S(2)}, u32[]{:S(2)}) collective-permute-start(bf16[256,768]{1,0:T(8,128)(2,1)} %param.5), channel_id=1, source_target_pairs={{0,4},{1,5},{2,6},{3,7},{4,8},{5,9},{6,10},{7,11},{8,12},{9,13},{1... | collective-permute-start | bytes 1179656 | tf_op jit(solution)/shard_map/ppermute | solution.py:27
  20.2 41.8 %collective-permute-start.7 = (bf16[256,768]{1,0:T(8,128)(2,1)}, bf16[256,768]{1,0:T(8,128)(2,1)S(1)}, u32[]{:S(2)}, u32[]{:S(2)}) collective-permute-start(bf16[256,768]{1,0:T(8,128)(2,1)} %param.5), channel_id=1, source_target_pairs={{0,12},{1,13},{2,14},{3,15},{4,0},{5,1},{6,2},{7,3},{8,4},{9,5},{1... | collective-permute-start | bytes 1179656 | tf_op jit(solution)/shard_map/ppermute | solution.py:27
  26.8 42.4 %collective-permute-start.5 = (bf16[4,128,384]{2,1,0:T(8,128)(2,1)S(1)}, bf16[4,128,384]{2,1,0:T(8,128)(2,1)S(1)}, u32[]{:S(2)}, u32[]{:S(2)}) collective-permute-start(bf16[4,128,384]{2,1,0:T(8,128)(2,1)S(1)} %pad_maximum_fusion), channel_id=1, source_target_pairs={{0,384},{16,400},{32,416},{48,432},{64,448},{80,464},{96,480},{112... | collective-permute-start | bytes 1179656 | tf_op jit(solution)/shard_map/ppermute | solution.py:31
  31.8 37.4 %collective-permute-start.4 = (bf16[4,128,384]{2,1,0:T(8,128)(2,1)S(1)}, bf16[4,128,384]{2,1,0:T(8,128)(2,1)S(1)}, u32[]{:S(2)}, u32[]{:S(2)}) collective-permute-start(bf16[4,128,384]{2,1,0:T(8,128)(2,1)S(1)} %pad_maximum_fusion), channel_id=1, source_target_pairs={{0,256},{16,272},{32,288},{48,304},{64,320},{80,336},{96,352},{112... | collective-permute-start | bytes 1179656 | tf_op jit(solution)/shard_map/ppermute | solution.py:31
  34.3 34.8 %collective-permute-start.3 = (bf16[4,128,384]{2,1,0:T(8,128)(2,1)S(1)}, bf16[4,128,384]{2,1,0:T(8,128)(2,1)S(1)}, u32[]{:S(2)}, u32[]{:S(2)}) collective-permute-start(bf16[4,128,384]{2,1,0:T(8,128)(2,1)S(1)} %pad_maximum_fusion), channel_id=1, source_target_pairs={{0,128},{16,144},{32,160},{48,176},{64,192},{80,208},{96,224},{112... | collective-permute-start | bytes 1179656 | tf_op jit(solution)/shard_map/ppermute | solution.py:31
  62.0 32.5 %collective-permute-start.10 = (bf16[768,768]{1,0:T(8,128)(2,1)S(1)}, bf16[768,768]{1,0:T(8,128)(2,1)S(1)}, u32[]{:S(2)}, u32[]{:S(2)}) collective-permute-start(bf16[768,768]{1,0:T(8,128)(2,1)S(1)} %constant_dynamic-update-slice_fusion.7.near), channel_id=1, source_target_pairs={{0,3},{1,0},{2,1},{3,2},{4,7},{5,4},{6,5},{7,6},{8,11},{9,8},{10,9... | collective-permute-start | bytes 3538952 | tf_op jit(solution)/shard_map/ppermute | solution.py:27
  64.8 29.7 %collective-permute-start.9 = (bf16[768,768]{1,0:T(8,128)(2,1)S(1)}, bf16[768,768]{1,0:T(8,128)(2,1)S(1)}, u32[]{:S(2)}, u32[]{:S(2)}) collective-permute-start(bf16[768,768]{1,0:T(8,128)(2,1)S(1)} %constant_dynamic-update-slice_fusion.7.near), channel_id=1, source_target_pairs={{0,1},{1,2},{2,3},{3,0},{4,5},{5,6},{6,7},{7,4},{8,9},{9,10},{10,1... | collective-permute-start | bytes 3538952 | tf_op jit(solution)/shard_map/ppermute | solution.py:27
  69.4 33.2 %collective-permute-start.8 = (bf16[16,128,384]{2,1,0:T(8,128)(2,1)S(1)}, bf16[16,128,384]{2,1,0:T(8,128)(2,1)S(1)}, u32[]{:S(2)}, u32[]{:S(2)}) collective-permute-start(bf16[16,128,384]{2,1,0:T(8,128)(2,1)S(1)} %constant_dynamic-update-slice_fusion.own_ref), channel_id=1, source_target_pairs={{0,16},{16,0},{32,48},{48,32},{64,80},{80,64},{96,112},{112,96},{1... | collective-permute-start | bytes 4718600 | tf_op jit(solution)/shard_map/ppermute | solution.py:31
  71.3 20.4 %collective-permute-start.11 = (bf16[128,768]{1,0:T(8,128)(2,1)S(1)}, bf16[128,768]{1,0:T(8,128)(2,1)S(1)}, u32[]{:S(2)}, u32[]{:S(2)}) collective-permute-start(bf16[128,768]{1,0:T(8,128)(2,1)S(1)} %slice.8), channel_id=1, source_target_pairs={{0,4},{1,5},{2,6},{3,7},{4,8},{5,9},{6,10},{7,11},{8,12},{9,13},{1... | collective-permute-start | bytes 589832 | tf_op jit(solution)/shard_map/ppermute | solution.py:27
  78.5 22.8 %copy-start = (s32[4096]{0:T(1024)S(1)}, s32[4096]{0:T(1024)}, u32[]{:S(2)}) copy-start(s32[4096]{0:T(1024)} %param.6) | copy-start | bytes 49156
  78.6 22.8 %copy-start.1 = (s32[32]{0:T(128)S(1)}, s32[32]{0:T(128)}, u32[]{:S(2)}) copy-start(s32[32]{0:T(128)} %tokens_ref.5) | copy-start | bytes 388
  78.6 15.9 %collective-permute-start.12 = (bf16[128,768]{1,0:T(8,128)(2,1)S(1)}, bf16[128,768]{1,0:T(8,128)(2,1)S(1)}, u32[]{:S(2)}, u32[]{:S(2)}) collective-permute-start(bf16[128,768]{1,0:T(8,128)(2,1)S(1)} %slice.9), channel_id=1, source_target_pairs={{0,12},{1,13},{2,14},{3,15},{4,0},{5,1},{6,2},{7,3},{8,4},{9,5},{1... | collective-permute-start | bytes 589832 | tf_op jit(solution)/shard_map/ppermute | solution.py:27
  94.6 25.6 %collective-permute-start.13 = (bf16[640,768]{1,0:T(8,128)(2,1)S(1)}, bf16[640,768]{1,0:T(8,128)(2,1)S(1)}, u32[]{:S(2)}, u32[]{:S(2)}) collective-permute-start(bf16[640,768]{1,0:T(8,128)(2,1)S(1)} %get-tuple-element.16), channel_id=1, source_target_pairs={{0,1},{1,2},{2,3},{3,0},{4,5},{5,6},{6,7},{7,4},{8,9},{9,10},{10,1... | collective-permute-start | bytes 2949128 | tf_op jit(solution)/shard_map/ppermute | solution.py:27
  99.4 24.8 %collective-permute-start.14 = (bf16[640,768]{1,0:T(8,128)(2,1)S(1)}, bf16[640,768]{1,0:T(8,128)(2,1)S(1)}, u32[]{:S(2)}, u32[]{:S(2)}) collective-permute-start(bf16[640,768]{1,0:T(8,128)(2,1)S(1)} %get-tuple-element.17), channel_id=1, source_target_pairs={{0,3},{1,0},{2,1},{3,2},{4,7},{5,4},{6,5},{7,6},{8,11},{9,8},{10,9... | collective-permute-start | bytes 2949128 | tf_op jit(solution)/shard_map/ppermute | solution.py:27
  124.3 8.2 %collective-permute-start.15 = (bf16[128,768]{1,0:T(8,128)(2,1)S(1)}, bf16[128,768]{1,0:T(8,128)(2,1)S(1)}, u32[]{:S(2)}, u32[]{:S(2)}) collective-permute-start(bf16[128,768]{1,0:T(8,128)(2,1)S(1)} %get-tuple-element.18), channel_id=1, source_target_pairs={{0,1},{1,2},{2,3},{3,0},{4,5},{5,6},{6,7},{7,4},{8,9},{9,10},{10,1... | collective-permute-start | bytes 589832 | tf_op jit(solution)/shard_map/ppermute | solution.py:27
  126.2 8.8 %collective-permute-start.16 = (bf16[128,768]{1,0:T(8,128)(2,1)S(1)}, bf16[128,768]{1,0:T(8,128)(2,1)S(1)}, u32[]{:S(2)}, u32[]{:S(2)}) collective-permute-start(bf16[128,768]{1,0:T(8,128)(2,1)S(1)} %get-tuple-element.19), channel_id=1, source_target_pairs={{0,3},{1,0},{2,1},{3,2},{4,7},{5,4},{6,5},{7,6},{8,11},{9,8},{10,9... | collective-permute-start | bytes 589832 | tf_op jit(solution)/shard_map/ppermute | solution.py:27
